TPU v7x, 256 devices: a whole 4x4x8 slice. The times are simulated.
256 devices in a mesh: dp: 16 (over z, y_hi), tensor: 16 (over x, y_lo, core).
Axes of the slice: x: 4, y: 4 (y_hi: 2, y_lo: 2; y = y_hi * 2 + y_lo), z: 8, core: 2. Of those that a mesh axis runs over, the one named last changes fastest.
Arguments:
- inputs: bfloat16 [2048, 16384], P('tensor', 'dp'), may hold values from -6 to 6
- out_grad: bfloat16 [2048, 16384], P('tensor', 'dp'), may hold values from -6 to 6
- attn_out: bfloat16 [2048, 12288], P('dp', 'tensor'), may hold values from -6 to 6
- qkv_grad: bfloat16 [2048, 14336], P('dp', 'tensor'), may hold values from -6 to 6
- w_qkv: bfloat16 [16384, 14336], P('dp', 'tensor'), may hold values from -0.046875 to 0.046875
- w_out: bfloat16 [12288, 16384], P('tensor', 'dp'), may hold values from -0.0546875 to 0.0546875
- doc_ids: int32 [2048], P('dp'), may hold values from 0 to 15, as said below
Outputs:
- input_grad: bfloat16 [2048, 16384], P('tensor', 'dp')
- attn_grad: bfloat16 [2048, 12288], P('dp', 'tensor')
- wqkv_grad: float32 [16384, 14336], P('dp', 'tensor')
- wout_grad: float32 [12288, 16384], P('tensor', 'dp')
Inputs may be any that keep to these rules, and one draw needn't show every extreme that they name: `doc_ids`: ids never fall along the tokens; every id occurs; each document holds 1 to 960 tokens; document 0 holds fewer than 128 tokens and the last document holds exactly 960.
All inputs are finite; a program needn't handle non-finite values.
Results may differ from a plain program's by a relative error of at most 0.019.
Values may be sent and summed in bfloat16 or wider, within the bound.
No kernel may reach another device: no remote copies, remote signals or barrier semaphores. Data moves between devices by JAX's collectives and lax.ppermute only.
A program may use at most 128 MiB of HBM per device.

v0:
```python
import math

import jax
import jax.numpy as jnp
from jax import lax
from jax.experimental import pallas as pl
from jax.experimental.pallas import tpu as pltpu
from jax.sharding import PartitionSpec as P

HD = 128
HQ = 96
HK = 8
ROPE_BASE = 500000.0
NZ = 8
NX = 4
TB = 128
BEHIND = 4


def over_z(value, steps):
    pairs = [(z * 2 + h, (z + steps) % NZ * 2 + h) for z in range(NZ) for h in range(2)]
    return lax.ppermute(value, "dp", pairs)


def over_yh(value):
    return lax.ppermute(value, "dp", [(d, d ^ 1) for d in range(16)])


def over_x(value, steps):
    pairs = [(x * 4 + k, (x + steps) % NX * 4 + k) for x in range(NX) for k in range(4)]
    return lax.ppermute(value, "tensor", pairs)


def over_yl(value):
    return lax.ppermute(value, "tensor", [(t, t ^ 2) for t in range(16)])


def over_core(value):
    return lax.ppermute(value, "tensor", [(t, t ^ 1) for t in range(16)])


def tie(*values):
    return lax.optimization_barrier(values)


def rotary_tables(ids, window, z):
    smaller = jnp.sum((window[None, :] < ids[:, None]).astype(jnp.int32), axis=1)
    start = jnp.maximum((z - BEHIND) * 2 * TB, 0) + smaller
    positions = z * 2 * TB + jnp.arange(2 * TB, dtype=jnp.int32) - start
    lane = jnp.arange(HD, dtype=jnp.int32)
    frequency = jnp.power(jnp.float32(ROPE_BASE), -(2.0 * (lane // 2).astype(jnp.float32)) / HD)
    angles = positions.astype(jnp.float32)[:, None] * frequency[None, :]
    sign = jnp.where(lane % 2 == 0, 1.0, -1.0)
    return jnp.cos(angles), jnp.sin(angles) * sign[None, :]


def unrotate_kernel(where_ref, own_ref, other_ref, cos_ref, sin_ref, up_attn_ref, down_attn_ref, up_ref, down_ref):
    even = lax.broadcasted_iota(jnp.int32, (TB, HD), 1) % 2 == 0
    swapped = where_ref[0] == 1
    cols = own_ref.shape[1]
    for h in range(cols // HD):
        part = slice(h * HD, (h + 1) * HD)
        rotated = where_ref[1] + h < HQ + HK
        own, other = own_ref[:, part], other_ref[:, part]
        for half in range(2):
            rows = slice(half * TB, (half + 1) * TB)
            values = jnp.where(swapped, *((other, own) if half == 0 else (own, other))).astype(jnp.float32)
            partner = jnp.where(even, pltpu.roll(values, HD - 1, 1), pltpu.roll(values, 1, 1))
            cosine = jnp.where(rotated, cos_ref[rows, :], 1.0)
            sine = jnp.where(rotated, sin_ref[rows, :], 0.0)
            result = (values * cosine + partner * sine).astype(jnp.bfloat16)
            at = slice(half * cols + h * HD, half * cols + (h + 1) * HD)
            up_ref[:, at] = result
            down_ref[:, at] = result
    up_ref[:, 2 * cols :] = up_attn_ref[...]
    down_ref[:, 2 * cols :] = down_attn_ref[...]


def unrotate(own, other, tables, up_attn, down_attn, yh, t):
    cols = own.shape[1]
    vmem = pl.BlockSpec(memory_space=pltpu.VMEM)
    shape = jax.ShapeDtypeStruct((TB, 2 * cols + up_attn.shape[1]), jnp.bfloat16)
    return pl.pallas_call(
        unrotate_kernel,
        out_shape=(shape, shape),
        in_specs=[pl.BlockSpec(memory_space=pltpu.SMEM)] + [vmem] * 6,
        out_specs=(vmem, vmem),
        cost_estimate=pl.CostEstimate(flops=20 * TB * cols, bytes_accessed=16 * TB * cols, transcendentals=0),
    )(jnp.stack([yh, t * (cols // HD)]).astype(jnp.int32), own, other, *tables, up_attn, down_attn)


def place_first(block, count):
    def body(block_ref, out_ref):
        out_ref[0] = block_ref[...]

    n = block.shape[1]
    return pl.pallas_call(
        body,
        out_shape=jax.ShapeDtypeStruct((count, TB, n), jnp.bfloat16),
        grid=(1,),
        in_specs=[pl.BlockSpec((TB, n), lambda i: (0, 0))],
        out_specs=pl.BlockSpec((1, TB, n), lambda i: (0, 0, 0)),
    )(block)


def absorb(blocks, q_places, a_places, z, core, weights, wholes):
    count, with_attn = len(blocks), bool(a_places)
    width, cols = weights.shape
    attn_cols = blocks[0].shape[1] - 2 * cols
    at = lambda p: (z + p + NZ) % NZ
    where = jnp.stack([*map(at, q_places), core]).astype(jnp.int32)
    q_spec = pl.BlockSpec((2, 1, TB, cols), lambda i, s: (0, s[i], 0, 0))
    share = pl.BlockSpec((1, TB, width), lambda i, s: (s[i], 0, 0))
    out_specs = [q_spec, share, share]
    out_shape = [jax.ShapeDtypeStruct((2, NZ, TB, cols), jnp.bfloat16)]
    out_shape += [jax.ShapeDtypeStruct((NZ, TB, width), jnp.bfloat16)] * 2
    if with_attn:
        first, total = a_places
        out_specs.append(pl.BlockSpec((1, TB, attn_cols), lambda i, s: (jnp.minimum(first + i, total - 1), 0, 0)))
        out_shape.append(jax.ShapeDtypeStruct((total, TB, attn_cols), jnp.bfloat16))
    operands = [*blocks, weights]
    in_specs = [pl.BlockSpec(v.shape, lambda i, s: (0, 0)) for v in operands]
    aliases = {}
    for k, whole in enumerate(wholes):
        if whole is not None:
            aliases[1 + len(operands)] = k
            operands.append(whole)
            in_specs.append(pl.BlockSpec(memory_space=pltpu.HBM))
    n_out = len(out_specs)

    def body(where_ref, *refs):
        weights_ref = refs[count]
        outs = refs[-n_out:]
        first = where_ref[count] == 0
        for k in range(count):

            @pl.when(pl.program_id(0) == k)
            def _():
                halves = [refs[k][:, :cols], refs[k][:, cols : 2 * cols]]
                outs[0][0, 0], outs[0][1, 0] = halves
                if with_attn:
                    outs[3][0] = refs[k][:, 2 * cols :]
                product = lax.dot_general(
                    jnp.concatenate(halves),
                    weights_ref[...],
                    (((1,), (1,)), ((), ())),
                    preferred_element_type=jnp.float32,
                ).astype(jnp.bfloat16)
                outs[1][0] = jnp.where(first, product[:TB], product[TB:])
                outs[2][0] = jnp.where(first, product[TB:], product[:TB])

    return pl.pallas_call(
        body,
        out_shape=tuple(out_shape),
        grid_spec=pltpu.PrefetchScalarGridSpec(
            num_scalar_prefetch=1, grid=(count,), in_specs=in_specs, out_specs=tuple(out_specs)
        ),
        input_output_aliases=aliases,
        compiler_params=pltpu.CompilerParams(vmem_limit_bytes=60 * 2**20),
        cost_estimate=pl.CostEstimate(
            flops=4 * count * TB * cols * width,
            bytes_accessed=2 * width * cols + 4 * count * TB * (2 * cols + attn_cols + width),
            transcendentals=0,
        ),
    )(where, *operands)


def contract_rows(left, right, factor, tile):
    m, n = left.shape[1], right.shape[2]

    def body(left_ref, right_ref, out_ref):
        total = jnp.zeros(out_ref.shape, jnp.float32)
        for h in range(2):
            tokens = left_ref[:, h].reshape(NZ * TB, tile)
            total += lax.dot_general(
                tokens, right_ref[h], (((0,), (0,)), ((), ())), preferred_element_type=jnp.float32
            )
        out_ref[...] = total * factor

    return pl.pallas_call(
        body,
        out_shape=jax.ShapeDtypeStruct((m, n), jnp.float32),
        grid=(m // tile,),
        in_specs=[
            pl.BlockSpec((NZ, 2, TB, tile), lambda i: (0, 0, 0, i)),
            pl.BlockSpec(right.shape, lambda i: (0, 0, 0)),
        ],
        out_specs=pl.BlockSpec((tile, n), lambda i: (i, 0)),
        compiler_params=pltpu.CompilerParams(vmem_limit_bytes=60 * 2**20),
        cost_estimate=pl.CostEstimate(
            flops=4 * NZ * TB * m * n, bytes_accessed=4 * NZ * TB * (m + n) + 4 * m * n, transcendentals=0
        ),
    )(left.reshape(NZ, 2, TB, m), right)


def ring_rows(chunks, both, order, yh, factor, tile):
    m, n = chunks[0][0].shape[2], both.shape[1]
    operands = [v for chunk in chunks for v in chunk]

    def body(where_ref, *refs):
        both_ref, out_ref = refs[-2:]
        total = jnp.zeros(out_ref.shape, jnp.float32)
        for side in range(2):
            h = where_ref[NZ] if side == 0 else 1 - where_ref[NZ]
            first = 0
            for c in range(len(chunks)):
                part = refs[2 * c + side]
                k = part.shape[0]
                tokens = jnp.concatenate([both_ref[where_ref[first + j], h] for j in range(k)])
                left = part[...].reshape(k * TB, tile)
                total += lax.dot_general(left, tokens, (((0,), (0,)), ((), ())), preferred_element_type=jnp.float32)
                first += k
        out_ref[...] = total * factor

    return pl.pallas_call(
        body,
        out_shape=jax.ShapeDtypeStruct((m, n), jnp.float32),
        grid_spec=pltpu.PrefetchScalarGridSpec(
            num_scalar_prefetch=1,
            grid=(m // tile,),
            in_specs=[pl.BlockSpec((v.shape[0], TB, tile), lambda i, s: (0, 0, i)) for v in operands]
            + [pl.BlockSpec((NZ, 2, TB, n), lambda i, s: (0, 0, 0, 0))],
            out_specs=pl.BlockSpec((tile, n), lambda i, s: (i, 0)),
        ),
        compiler_params=pltpu.CompilerParams(vmem_limit_bytes=60 * 2**20),
        cost_estimate=pl.CostEstimate(
            flops=4 * NZ * TB * m * n, bytes_accessed=4 * NZ * TB * (m + n) + 4 * m * n, transcendentals=0
        ),
    )(jnp.stack([*order, yh]).astype(jnp.int32), *operands, both.reshape(NZ, 2, TB, n))


def contract_cols(left, right):
    return lax.dot_general(
        left, right, (((1,), (1,)), ((), ())), preferred_element_type=jnp.float32
    )


class Fold:
    def __init__(self, partial, z):
        self.partial, self.z = partial, z
        self.rows = partial.shape[0] // NZ
        self.up = self.down = None
        self.k = 4

    def mine(self, at):
        return lax.dynamic_slice_in_dim(self.partial, at % NZ * self.rows, self.rows, 0).astype(jnp.float32)

    def add(self, part, got):
        return (part if got is None else part + got.astype(jnp.float32)).astype(jnp.bfloat16)

    def step(self):
        k = self.k
        self.k -= 1
        if k < 4:
            self.up = over_z(self.add(self.mine(self.z + k), self.up), 1)
        self.down = over_z(self.add(self.mine(self.z - k + NZ), self.down), -1)

    def sums(self):
        return self.mine(self.z) + self.up.astype(jnp.float32) + self.down.astype(jnp.float32)


def shards(inputs, out_grad, attn_out, qkv_grad, w_qkv, w_out, doc_ids):
    d, t = lax.axis_index("dp"), lax.axis_index("tensor")
    z, yh = d // 2, d % 2
    x, yl, core = t // 4, t // 2 % 2, t % 2
    factor = 1.0 / math.sqrt(NZ * 2 * TB)

    g_all = lax.all_gather(out_grad, "tensor", axis=0, tiled=True)
    x_all = lax.all_gather(inputs, "tensor", axis=0, tiled=True)

    ids = doc_ids[None, :]
    other_ids = over_yh(ids)
    q_other = over_yh(qkv_grad)
    pair_ids = jnp.where(yh == 1, jnp.concatenate([other_ids, ids]), jnp.concatenate([ids, other_ids]))
    near = [over_z(pair_ids, 1), over_z(pair_ids, 2)]
    attn, _ = tie(attn_out, pair_ids)
    up_attn, down_attn = over_z(attn, 1), over_z(attn, -1)
    far = over_z(jnp.concatenate(near), 2)
    window = jnp.concatenate([pair_ids, *near, far]).reshape(-1)
    tables = rotary_tables(pair_ids.reshape(-1), window, z)

    up0, down0 = unrotate(qkv_grad, q_other, tables, up_attn, down_attn, yh, t)
    up1, down1 = tie(over_z(up0, 1), over_z(down0, -1))

    attn1 = place_first(attn_out, 5)
    *shares, attn1 = absorb([up0, down0], [0, 0], (1, 5), z, core, w_qkv, [None, None, None, attn1])
    *shares, attn1 = absorb([up1, down1], [-1, 1], (3, 5), z, core, w_qkv, [*shares, attn1])
    up2, down2, attn1, *shares = tie(over_z(up1, 1), over_z(down1, -1), attn1, *shares)

    *shares, attn2 = absorb([up2, down2], [-2, 2], (0, 3), z, core, w_qkv, [*shares, None])
    attn_part = contract_cols(g_all, w_out).astype(jnp.bfloat16)
    up3, down3, attn_part, attn2, *shares = tie(over_z(up2, 1), over_z(down2, -1), attn_part, attn2, *shares)

    attn1_other = over_yh(attn1)
    fold = Fold(attn_part, z)
    fold.step()
    last = over_z(up3[:, : 2 * qkv_grad.shape[1]], 1)
    *shares, attn2 = absorb([up3, down3], [-3, 3], (2, 3), z, core, w_qkv, [*shares, attn2])
    last, fold.down, *shares = tie(last, fold.down, *shares)
    q_all, kept, given = absorb([last], [4], None, z, core, w_qkv, shares)

    q_all = q_all.reshape(2, NZ * TB, -1)
    sent = over_core(given)
    fold.step()
    chip = (kept.astype(jnp.float32) + sent.astype(jnp.float32)).astype(jnp.bfloat16).reshape(NZ * TB, -1)
    fold.up, fold.down, x_all, attn1_other, attn2, _ = tie(fold.up, fold.down, x_all, attn1_other, attn2, chip)
    attn2_other = over_yh(attn2)
    fold.step()
    toward = lambda at: lax.dynamic_slice_in_dim(chip, at % NX * 2 * TB, 2 * TB, 0)
    total = toward(x).astype(jnp.float32)
    for steps in (1, -1, 2):
        total = total + over_x(toward(x + steps + NX), steps).astype(jnp.float32)
    keep = lax.dynamic_slice_in_dim(total, yl * TB, TB, 0)
    give = lax.dynamic_slice_in_dim(total, (1 - yl) * TB, TB, 0).astype(jnp.bfloat16)
    summed = keep + over_yl(give).astype(jnp.float32)
    input_grad = (out_grad.astype(jnp.float32) + summed).astype(jnp.bfloat16)

    fold.step()
    sums = fold.sums()
    keep = lax.dynamic_slice_in_dim(sums, yh * TB, TB, 0)
    send = lax.dynamic_slice_in_dim(sums, (1 - yh) * TB, TB, 0).astype(jnp.bfloat16)
    attn_grad = (keep + over_yh(send).astype(jnp.float32)).astype(jnp.bfloat16)

    attn2_other, _, _ = tie(attn2_other, give, send)
    wqkv_grad = contract_rows(x_all, q_all, factor, 256)
    order = [(z + p + NZ) % NZ for p in (0, -1, 1, -2, 2, -3, 3, 4)]
    wout_grad = ring_rows([(attn1, attn1_other), (attn2, attn2_other)], g_all, order, yh, factor, 256)
    return (input_grad, attn_grad, wqkv_grad, wout_grad)


def solution(mesh):
    return jax.shard_map(
        shards,
        mesh=mesh,
        in_specs=(
            P("tensor", "dp"),
            P("tensor", "dp"),
            P("dp", "tensor"),
            P("dp", "tensor"),
            P("dp", "tensor"),
            P("tensor", "dp"),
            P("dp"),
        ),
        out_specs=(P("tensor", "dp"), P("dp", "tensor"), P("dp", "tensor"), P("tensor", "dp")),
        check_vma=False,
    )
```

profile of v0, /device:TPU:2, one launch (start us, length us, event | category | flops | bytes accessed | tf_op | source)
XLA Modules:
  0.0 192.9 jit_solution(3549315337016330558)
XLA Ops:
  8.7 3.3 %collective-permute-start.1 = (s32[1,128]{1,0:T(1,128)}, s32[1,128]{1,0:T(1,128)S(1)}, u32[]{:S(2)}, u32[]{:S(2)}) collective-permute-start(s32[1,128]{1,0:T(1,128)} %bitcast.25), channel_id=1, source_target_pairs={{0,16},{16,0},{32,48},{48,32},{64,80},{80,64},{96,112},{112,96},{1... | collective-permute-start | bytes 1544 | tf_op jit(solution)/shard_map/ppermute | solution.py:26
  16.6 3.3 %collective-permute-start.3 = (s32[2,128]{1,0:T(2,128)S(1)}, s32[2,128]{1,0:T(2,128)S(1)}, u32[]{:S(2)}, u32[]{:S(2)}) collective-permute-start(s32[2,128]{1,0:T(2,128)S(1)} %add_select_fusion), channel_id=1, source_target_pairs={{0,64},{16,80},{32,96},{48,112},{64,128},{80,144},{96,160},{112,17... | collective-permute-start | bytes 3080 | tf_op jit(solution)/shard_map/ppermute | solution.py:22
  19.9 3.1 %collective-permute-start.5 = (bf16[128,768]{1,0:T(8,128)(2,1)}, bf16[128,768]{1,0:T(8,128)(2,1)S(1)}, u32[]{:S(2)}, u32[]{:S(2)}) collective-permute-start(bf16[128,768]{1,0:T(8,128)(2,1)} %block_ref.1), channel_id=1, source_target_pairs={{0,32},{16,48},{32,64},{48,80},{64,96},{80,112},{96,128},{112,144}... | collective-permute-start | bytes 589832 | tf_op jit(solution)/shard_map/ppermute | solution.py:22
  26.3 3.0 %collective-permute-done.4 = s32[4,128]{1,0:T(4,128)S(1)} collective-permute-done((s32[4,128]{1,0:T(4,128)S(1)}, s32[4,128]{1,0:T(4,128)S(1)}, u32[]{:S(2)}, u32[]{:S(2)}) %collective-permute-start.4) | collective-permute-done | bytes 2080 | tf_op jit(solution)/shard_map/ppermute | solution.py:22
  31.7 2.8 %shard_map.102 = (bf16[128,2560]{1,0:T(8,128)(2,1)}, bf16[128,2560]{1,0:T(8,128)(2,1)}) custom-call(s32[2]{0:T(128)} %pad_add_fusion.2.where_ref, bf16[128,896]{1,0:T(8,128)(2,1)} %own_ref.1, bf16[128,896]{1,0:T(8,128)(2,1)} %copy-done.10, f32[256,128]{1,0:T(8,128)} %get-tuple-element.108.cos_ref, f32[256,128]{1,0:T(8,128)} %get-tuple-element.107.sin_ref, ...), custom_call_target="tpu_custom_call" | custom-call | flops 2293760 | bytes 1835008 | tf_op jit(solution)/shard_map/pallas_call | solution.py:83
  37.7 11.2 %collective-permute-done.7.refs_0_ = bf16[128,2560]{1,0:T(8,128)(2,1)S(1)} collective-permute-done((bf16[128,2560]{1,0:T(8,128)(2,1)}, bf16[128,2560]{1,0:T(8,128)(2,1)S(1)}, u32[]{:S(2)}, u32[]{:S(2)}) %collective-permute-start.7) | collective-permute-done | bytes 655392 | tf_op jit(solution)/shard_map/ppermute | solution.py:22
  55.6 5.3 %shard_map.104 = (bf16[2,8,128,896]{3,2,1,0:T(8,128)(2,1)}, bf16[8,128,1024]{2,1,0:T(8,128)(2,1)}, bf16[8,128,1024]{2,1,0:T(8,128)(2,1)}, bf16[5,128,768]{2,1,0:T(8,128)(2,1)}) custom-call(s32[3]{0:T(128)} %add_add_fusion.1.where_ref, bf16[128,2560]{1,0:T(8,128)(2,1)} %get-tuple-element.53.refs_0_, ...), custom_call_target="tpu_custom_call", output_to_operand_aliasing={{3}: (4, {})} | custom-call | flops 939524096 | bytes 5505024 | tf_op jit(solution)/shard_map/pallas_call | solution.py:152
  60.9 5.3 %shard_map.105 = (bf16[2,8,128,896]{3,2,1,0:T(8,128)(2,1)}, bf16[8,128,1024]{2,1,0:T(8,128)(2,1)}, bf16[8,128,1024]{2,1,0:T(8,128)(2,1)}, bf16[5,128,768]{2,1,0:T(8,128)(2,1)}) custom-call(s32[3]{0:T(128)} %get-tuple-element.111.where_ref, bf16[128,2560]{1,0:T(8,128)(2,1)} %copy-done.7, ...), custom_call_target="tpu_custom_call", output_to_operand_aliasing={{0}: (4, {}), {1}: (5, {}), {2}: (6, {}), {3}: (7, {})} | custom-call | flops 939524096 | bytes 5505024 | tf_op jit(solution)/shard_map/pallas_call | solution.py:152
  66.8 2.9 %collective-permute-start.12 = (bf16[128,2560]{1,0:T(8,128)(2,1)S(1)}, bf16[128,2560]{1,0:T(8,128)(2,1)}, u32[]{:S(2)}, u32[]{:S(2)}) collective-permute-start(bf16[128,2560]{1,0:T(8,128)(2,1)S(1)} %collective-permute-done.10.refs_1_), channel_id=1, source_target_pairs={{0,224},{16,240},{32,0},{48,16},{64,32},{80,48},{96,64},{112,80},{... | collective-permute-start | bytes 1966088 | tf_op jit(solution)/shard_map/ppermute | solution.py:22
  69.7 5.3 %shard_map.106 = (bf16[2,8,128,896]{3,2,1,0:T(8,128)(2,1)}, bf16[8,128,1024]{2,1,0:T(8,128)(2,1)}, bf16[8,128,1024]{2,1,0:T(8,128)(2,1)}, bf16[3,128,768]{2,1,0:T(8,128)(2,1)}) custom-call(s32[3]{0:T(128)} %get-tuple-element.112.where_ref, bf16[128,2560]{1,0:T(8,128)(2,1)} %copy-done.6, ...), custom_call_target="tpu_custom_call", output_to_operand_aliasing={{0}: (4, {}), {1}: (5, {}), {2}: (6, {})} | custom-call | flops 939524096 | bytes 5505024 | tf_op jit(solution)/shard_map/pallas_call | solution.py:152
  75.0 5.7 %convolution_convert_fusion = bf16[2048,768]{1,0:T(8,128)(2,1)S(1)} fusion(bf16[2048,1024]{1,0:T(8,128)(2,1)} %all-gather.3.cloned.1.call-done, bf16[768,1024]{1,0:T(8,128)(2,1)S(1)} %copy-done), kind=kOutput, calls=%fused_computation.1 | convolution fusion | flops 3222798336 | bytes 8912896 | tf_op jit(solution)/shard_map/dot_general | solution.py:233
  86.4 5.3 %shard_map.107 = (bf16[2,8,128,896]{3,2,1,0:T(8,128)(2,1)}, bf16[8,128,1024]{2,1,0:T(8,128)(2,1)}, bf16[8,128,1024]{2,1,0:T(8,128)(2,1)}, bf16[3,128,768]{2,1,0:T(8,128)(2,1)}) custom-call(s32[3]{0:T(128)} %add_add_fusion.3.where_ref, bf16[128,2560]{1,0:T(8,128)(2,1)} %copy-done.3, ...), custom_call_target="tpu_custom_call", output_to_operand_aliasing={{0}: (4, {}), {1}: (5, {}), {2}: (6, {}), {3}: (7, {})} | custom-call | flops 939524096 | bytes 5505024 | tf_op jit(solution)/shard_map/pallas_call | solution.py:152
  92.4 4.2 %shard_map.108 = (bf16[2,8,128,896]{3,2,1,0:T(8,128)(2,1)}, bf16[8,128,1024]{2,1,0:T(8,128)(2,1)}, bf16[8,128,1024]{2,1,0:T(8,128)(2,1)}) custom-call(s32[2]{0:T(128)} %pad_add_fusion.1.where_ref, bf16[128,1792]{1,0:T(8,128)(2,1)} %copy-done.9, bf16[1024,896]{1,0:T(8,128)(2,1)} %refs_1_.1, ...), custom_call_target="tpu_custom_call", output_to_operand_aliasing={{0}: (3, {}), {1}: (4, {}), {2}: (5, {})} | custom-call | flops 469762048 | bytes 3276800 | tf_op jit(solution)/shard_map/pallas_call | solution.py:152
  96.6 3.3 %collective-permute-start.22 = (bf16[5,128,768]{2,1,0:T(8,128)(2,1)S(1)}, bf16[5,128,768]{2,1,0:T(8,128)(2,1)}, u32[]{:S(2)}, u32[]{:S(2)}) collective-permute-start(bf16[5,128,768]{2,1,0:T(8,128)(2,1)S(1)} %copy-done.1), channel_id=1, source_target_pairs={{0,16},{16,0},{32,48},{48,32},{64,80},{80,64},{96,112},{112,96},{1... | collective-permute-start | bytes 2949128 | tf_op jit(solution)/shard_map/ppermute | solution.py:26
  104.6 4.6 %add_convert_fusion = bf16[8,128,1024]{2,1,0:T(8,128)(2,1)} fusion(bf16[8,128,1024]{2,1,0:T(8,128)(2,1)} %collective-permute-done.15, bf16[8,128,1024]{2,1,0:T(8,128)(2,1)} %get-tuple-element.88), kind=kLoop, calls=%fused_computation | loop fusion | flops 4194304 | bytes 6291456 | tf_op jit(solution)/shard_map/convert_element_type | solution.py:305
  109.2 13.2 %collective-permute-done.22.refs_1_ = bf16[5,128,768]{2,1,0:T(8,128)(2,1)} collective-permute-done((bf16[5,128,768]{2,1,0:T(8,128)(2,1)S(1)}, bf16[5,128,768]{2,1,0:T(8,128)(2,1)}, u32[]{:S(2)}, u32[]{:S(2)}) %collective-permute-start.22) | collective-permute-done | bytes 983072 | tf_op jit(solution)/shard_map/ppermute | solution.py:26
  126.4 2.3 %constant_dynamic-slice_fusion.3 = (bf16[256,1024]{1,0:T(8,128)(2,1)}, bf16[256,1024]{1,0:T(8,128)(2,1)S(1)}, bf16[256,1024]{1,0:T(8,128)(2,1)S(1)}) fusion(bf16[1024,1024]{1,0:T(8,128)(2,1)} %bitcast.23, s32[]{:T(128)S(6)} %select_n.230, s32[]{:T(128)S(6)} %select_n.234, s32[]{:T(128)S(6)} %select_n.232), kind=kLoop, calls=%fused_computation.21 | loop fusion | bytes 3145740 | tf_op jit(solution)/shard_map/dynamic_slice | solution.py:309
  133.5 3.2 %collective-permute-start.28 = (bf16[3,128,768]{2,1,0:T(8,128)(2,1)S(1)}, bf16[3,128,768]{2,1,0:T(8,128)(2,1)}, u32[]{:S(2)}, u32[]{:S(2)}) collective-permute-start(bf16[3,128,768]{2,1,0:T(8,128)(2,1)S(1)} %copy-done.8), channel_id=1, source_target_pairs={{0,16},{16,0},{32,48},{48,32},{64,80},{80,64},{96,112},{112,96},{1... | collective-permute-start | bytes 1769480 | tf_op jit(solution)/shard_map/ppermute | solution.py:26
  136.7 2.3 %add_convert_fusion.3 = (bf16[256,768]{1,0:T(8,128)(2,1)}, bf16[256,768]{1,0:T(8,128)(2,1)S(1)}) fusion(bf16[256,768]{1,0:T(8,128)(2,1)} %collective-permute-done.23, bf16[2048,768]{1,0:T(8,128)(2,1)} %copy-done.2, s32[]{:T(128)S(6)} %select_n.242, bf16[256,768]{1,0:T(8,128)(2,1)} %collective-permute-done.21, s32[]{:T(128)S(6)} %select_n.249), kind=kLoop, calls=%fused_computation.7 | loop fusion | flops 1572864 | bytes 2359304 | tf_op jit(solution)/shard_map/convert_element_type | solution.py:249
  140.6 3.3 %collective-permute-done.16 = bf16[256,1024]{1,0:T(8,128)(2,1)} collective-permute-done((bf16[256,1024]{1,0:T(8,128)(2,1)}, bf16[256,1024]{1,0:T(8,128)(2,1)}, u32[]{:S(2)}, u32[]{:S(2)}) %collective-permute-start.16) | collective-permute-done | bytes 524320 | tf_op jit(solution)/shard_map/ppermute | solution.py:31
  145.3 10.0 %collective-permute-done.18 = bf16[256,1024]{1,0:T(8,128)(2,1)} collective-permute-done((bf16[256,1024]{1,0:T(8,128)(2,1)S(1)}, bf16[256,1024]{1,0:T(8,128)(2,1)}, u32[]{:S(2)}, u32[]{:S(2)}) %collective-permute-start.18) | collective-permute-done | bytes 524320 | tf_op jit(solution)/shard_map/ppermute | solution.py:31
  162.4 8.9 %shard_map.109 = f32[1024,896]{1,0:T(8,128)} custom-call(bf16[8,2,128,1024]{3,2,1,0:T(8,128)(2,1)} %bitcast.29, bf16[2,1024,896]{2,1,0:T(8,128)(2,1)} %bitcast.22), custom_call_target="tpu_custom_call" | custom-call | flops 3758096384 | bytes 11534336 | tf_op jit(solution)/shard_map/pallas_call | solution.py:180
  173.4 3.0 %collective-permute-start.27 = (bf16[128,768]{1,0:T(8,128)(2,1)S(1)}, bf16[128,768]{1,0:T(8,128)(2,1)S(1)}, u32[]{:S(2)}, u32[]{:S(2)}) collective-permute-start(bf16[128,768]{1,0:T(8,128)(2,1)S(1)} %dynamic-slice_convert_fusion.1), channel_id=1, source_target_pairs={{0,16},{16,0},{32,48},{48,32},{64,80},{80,64},{96,112},{112,96},{1... | collective-permute-start | bytes 589832 | tf_op jit(solution)/shard_map/ppermute | solution.py:26
  176.4 9.0 %shard_map.110 = f32[768,1024]{1,0:T(8,128)} custom-call(s32[9]{0:T(128)} %stack.85.where_ref, bf16[5,128,768]{2,1,0:T(8,128)(2,1)} %get-tuple-element.91.refs_0_, bf16[5,128,768]{2,1,0:T(8,128)(2,1)} %collective-permute-done.22.refs_1_, bf16[3,128,768]{2,1,0:T(8,128)(2,1)} %get-tuple-element.98.refs_2_, ...), custom_call_target="tpu_custom_call" | custom-call | flops 3221225472 | bytes 10485760 | tf_op jit(solution)/shard_map/pallas_call | solution.py:215
  (104 shorter events, 55.0 us)
Async XLA Ops:
  7.2 67.9 %all-gather.3.cloned.1.call-start = ((), (), s32[]{:S(2)}) async-start(), calls=%async_computation | async-start | bytes 4456448 | tf_op jit(solution)/shard_map/all_gather | solution.py:268
  7.9 114.5 %all-gather.5.cloned.1.call-start = ((), (), s32[]{:S(2)}) async-start(), calls=%async_computation.1 | async-start | bytes 4456448 | tf_op jit(solution)/shard_map/all_gather | solution.py:269
  11.9 19.0 %collective-permute-start = (bf16[128,896]{1,0:T(8,128)(2,1)}, bf16[128,896]{1,0:T(8,128)(2,1)S(1)}, u32[]{:S(2)}, u32[]{:S(2)}) collective-permute-start(bf16[128,896]{1,0:T(8,128)(2,1)} %own_ref.1), channel_id=1, source_target_pairs={{0,16},{16,0},{32,48},{48,32},{64,80},{80,64},{96,112},{112,96},{1... | collective-permute-start | bytes 688136 | tf_op jit(solution)/shard_map/ppermute | solution.py:26
  19.9 11.0 %collective-permute-start.5 = (bf16[128,768]{1,0:T(8,128)(2,1)}, bf16[128,768]{1,0:T(8,128)(2,1)S(1)}, u32[]{:S(2)}, u32[]{:S(2)}) collective-permute-start(bf16[128,768]{1,0:T(8,128)(2,1)} %block_ref.1), channel_id=1, source_target_pairs={{0,32},{16,48},{32,64},{48,80},{64,96},{80,112},{96,128},{112,144}... | collective-permute-start | bytes 589832 | tf_op jit(solution)/shard_map/ppermute | solution.py:22
  34.5 14.5 %collective-permute-start.7 = (bf16[128,2560]{1,0:T(8,128)(2,1)}, bf16[128,2560]{1,0:T(8,128)(2,1)S(1)}, u32[]{:S(2)}, u32[]{:S(2)}) collective-permute-start(bf16[128,2560]{1,0:T(8,128)(2,1)} %get-tuple-element.53.refs_0_), channel_id=1, source_target_pairs={{0,32},{16,48},{32,64},{48,80},{64,96},{80,112},{96,128},{112,144}... | collective-permute-start | bytes 1966088 | tf_op jit(solution)/shard_map/ppermute | solution.py:22
  36.0 14.8 %collective-permute-start.8 = (bf16[128,2560]{1,0:T(8,128)(2,1)}, bf16[128,2560]{1,0:T(8,128)(2,1)}, u32[]{:S(2)}, u32[]{:S(2)}) collective-permute-start(bf16[128,2560]{1,0:T(8,128)(2,1)} %get-tuple-element.54.refs_1_), channel_id=1, source_target_pairs={{0,224},{16,240},{32,0},{48,16},{64,32},{80,48},{96,64},{112,80},{... | collective-permute-start | bytes 1966088 | tf_op jit(solution)/shard_map/ppermute | solution.py:22
  50.8 15.3 %collective-permute-start.10 = (bf16[128,2560]{1,0:T(8,128)(2,1)}, bf16[128,2560]{1,0:T(8,128)(2,1)S(1)}, u32[]{:S(2)}, u32[]{:S(2)}) collective-permute-start(bf16[128,2560]{1,0:T(8,128)(2,1)} %collective-permute-done.8.refs_1_), channel_id=1, source_target_pairs={{0,224},{16,240},{32,0},{48,16},{64,32},{80,48},{96,64},{112,80},{... | collective-permute-start | bytes 1966088 | tf_op jit(solution)/shard_map/ppermute | solution.py:22
  52.6 13.5 %collective-permute-start.9 = (bf16[128,2560]{1,0:T(8,128)(2,1)S(1)}, bf16[128,2560]{1,0:T(8,128)(2,1)S(1)}, u32[]{:S(2)}, u32[]{:S(2)}) collective-permute-start(bf16[128,2560]{1,0:T(8,128)(2,1)S(1)} %collective-permute-done.7.refs_0_), channel_id=1, source_target_pairs={{0,32},{16,48},{32,64},{48,80},{64,96},{80,112},{96,128},{112,144}... | collective-permute-start | bytes 1966088 | tf_op jit(solution)/shard_map/ppermute | solution.py:22
  66.2 14.6 %collective-permute-start.11 = (bf16[128,2560]{1,0:T(8,128)(2,1)S(1)}, bf16[128,2560]{1,0:T(8,128)(2,1)S(1)}, u32[]{:S(2)}, u32[]{:S(2)}) collective-permute-start(bf16[128,2560]{1,0:T(8,128)(2,1)S(1)} %collective-permute-done.9.refs_0_), channel_id=1, source_target_pairs={{0,32},{16,48},{32,64},{48,80},{64,96},{80,112},{96,128},{112,144}... | collective-permute-start | bytes 1966088 | tf_op jit(solution)/shard_map/ppermute | solution.py:22
  66.8 14.0 %collective-permute-start.12 = (bf16[128,2560]{1,0:T(8,128)(2,1)S(1)}, bf16[128,2560]{1,0:T(8,128)(2,1)}, u32[]{:S(2)}, u32[]{:S(2)}) collective-permute-start(bf16[128,2560]{1,0:T(8,128)(2,1)S(1)} %collective-permute-done.10.refs_1_), channel_id=1, source_target_pairs={{0,224},{16,240},{32,0},{48,16},{64,32},{80,48},{96,64},{112,80},{... | collective-permute-start | bytes 1966088 | tf_op jit(solution)/shard_map/ppermute | solution.py:22
  80.8 10.8 %collective-permute-start.13 = (bf16[128,1792]{1,0:T(8,128)(2,1)S(1)}, bf16[128,1792]{1,0:T(8,128)(2,1)S(1)}, u32[]{:S(2)}, u32[]{:S(2)}) collective-permute-start(bf16[128,1792]{1,0:T(8,128)(2,1)S(1)} %slice.3), channel_id=1, source_target_pairs={{0,32},{16,48},{32,64},{48,80},{64,96},{80,112},{96,128},{112,144}... | collective-permute-start | bytes 1376264 | tf_op jit(solution)/shard_map/ppermute | solution.py:22
  96.6 25.8 %collective-permute-start.22 = (bf16[5,128,768]{2,1,0:T(8,128)(2,1)S(1)}, bf16[5,128,768]{2,1,0:T(8,128)(2,1)}, u32[]{:S(2)}, u32[]{:S(2)}) collective-permute-start(bf16[5,128,768]{2,1,0:T(8,128)(2,1)S(1)} %copy-done.1), channel_id=1, source_target_pairs={{0,16},{16,0},{32,48},{48,32},{64,80},{80,64},{96,112},{112,96},{1... | collective-permute-start | bytes 2949128 | tf_op jit(solution)/shard_map/ppermute | solution.py:26
  99.9 22.5 %collective-permute-start.20 = (bf16[256,768]{1,0:T(8,128)(2,1)S(1)}, bf16[256,768]{1,0:T(8,128)(2,1)}, u32[]{:S(2)}, u32[]{:S(2)}) collective-permute-start(bf16[256,768]{1,0:T(8,128)(2,1)S(1)} %get-tuple-element.102), channel_id=1, source_target_pairs={{0,32},{16,48},{32,64},{48,80},{64,96},{80,112},{96,128},{112,144}... | collective-permute-start | bytes 1179656 | tf_op jit(solution)/shard_map/ppermute | solution.py:22
  103.1 19.3 %collective-permute-start.21 = (bf16[256,768]{1,0:T(8,128)(2,1)S(1)}, bf16[256,768]{1,0:T(8,128)(2,1)}, u32[]{:S(2)}, u32[]{:S(2)}) collective-permute-start(bf16[256,768]{1,0:T(8,128)(2,1)S(1)} %add_convert_fusion.5), channel_id=1, source_target_pairs={{0,224},{16,240},{32,0},{48,16},{64,32},{80,48},{96,64},{112,80},{... | collective-permute-start | bytes 1179656 | tf_op jit(solution)/shard_map/ppermute | solution.py:22
  124.4 12.3 %collective-permute-start.23 = (bf16[256,768]{1,0:T(8,128)(2,1)}, bf16[256,768]{1,0:T(8,128)(2,1)}, u32[]{:S(2)}, u32[]{:S(2)}) collective-permute-start(bf16[256,768]{1,0:T(8,128)(2,1)} %add_convert_fusion.4), channel_id=1, source_target_pairs={{0,32},{16,48},{32,64},{48,80},{64,96},{80,112},{96,128},{112,144}... | collective-permute-start | bytes 1179656 | tf_op jit(solution)/shard_map/ppermute | solution.py:22
  128.7 15.2 %collective-permute-start.16 = (bf16[256,1024]{1,0:T(8,128)(2,1)}, bf16[256,1024]{1,0:T(8,128)(2,1)}, u32[]{:S(2)}, u32[]{:S(2)}) collective-permute-start(bf16[256,1024]{1,0:T(8,128)(2,1)} %get-tuple-element.104), channel_id=1, source_target_pairs={{0,4},{1,5},{2,6},{3,7},{4,8},{5,9},{6,10},{7,11},{8,12},{9,13},{1... | collective-permute-start | bytes 1572872 | tf_op jit(solution)/shard_map/ppermute | solution.py:31
  130.1 15.2 %collective-permute-start.17 = (bf16[256,1024]{1,0:T(8,128)(2,1)S(1)}, bf16[256,1024]{1,0:T(8,128)(2,1)}, u32[]{:S(2)}, u32[]{:S(2)}) collective-permute-start(bf16[256,1024]{1,0:T(8,128)(2,1)S(1)} %get-tuple-element.106), channel_id=1, source_target_pairs={{0,12},{1,13},{2,14},{3,15},{4,0},{5,1},{6,2},{7,3},{8,4},{9,5},{1... | collective-permute-start | bytes 1572872 | tf_op jit(solution)/shard_map/ppermute | solution.py:31
  130.7 24.6 %collective-permute-start.18 = (bf16[256,1024]{1,0:T(8,128)(2,1)S(1)}, bf16[256,1024]{1,0:T(8,128)(2,1)}, u32[]{:S(2)}, u32[]{:S(2)}) collective-permute-start(bf16[256,1024]{1,0:T(8,128)(2,1)S(1)} %get-tuple-element.105), channel_id=1, source_target_pairs={{0,8},{1,9},{2,10},{3,11},{4,12},{5,13},{6,14},{7,15},{8,0},{9,1},... | collective-permute-start | bytes 1572872 | tf_op jit(solution)/shard_map/ppermute | solution.py:31
  133.5 42.9 %collective-permute-start.28 = (bf16[3,128,768]{2,1,0:T(8,128)(2,1)S(1)}, bf16[3,128,768]{2,1,0:T(8,128)(2,1)}, u32[]{:S(2)}, u32[]{:S(2)}) collective-permute-start(bf16[3,128,768]{2,1,0:T(8,128)(2,1)S(1)} %copy-done.8), channel_id=1, source_target_pairs={{0,16},{16,0},{32,48},{48,32},{64,80},{80,64},{96,112},{112,96},{1... | collective-permute-start | bytes 1769480 | tf_op jit(solution)/shard_map/ppermute | solution.py:26
  139.0 20.2 %collective-permute-start.25 = (bf16[256,768]{1,0:T(8,128)(2,1)S(1)}, bf16[256,768]{1,0:T(8,128)(2,1)S(1)}, u32[]{:S(2)}, u32[]{:S(2)}) collective-permute-start(bf16[256,768]{1,0:T(8,128)(2,1)S(1)} %get-tuple-element.101), channel_id=1, source_target_pairs={{0,224},{16,240},{32,0},{48,16},{64,32},{80,48},{96,64},{112,80},{... | collective-permute-start | bytes 1179656 | tf_op jit(solution)/shard_map/ppermute | solution.py:22
  143.9 28.2 %collective-permute-start.24 = (bf16[256,768]{1,0:T(8,128)(2,1)}, bf16[256,768]{1,0:T(8,128)(2,1)}, u32[]{:S(2)}, u32[]{:S(2)}) collective-permute-start(bf16[256,768]{1,0:T(8,128)(2,1)} %get-tuple-element.100), channel_id=1, source_target_pairs={{0,32},{16,48},{32,64},{48,80},{64,96},{80,112},{96,128},{112,144}... | collective-permute-start | bytes 1179656 | tf_op jit(solution)/shard_map/ppermute | solution.py:22
  157.9 13.4 %collective-permute-start.19 = (bf16[128,1024]{1,0:T(8,128)(2,1)}, bf16[128,1024]{1,0:T(8,128)(2,1)S(1)}, u32[]{:S(2)}, u32[]{:S(2)}) collective-permute-start(bf16[128,1024]{1,0:T(8,128)(2,1)} %dynamic-slice_convert_fusion), channel_id=1, source_target_pairs={{0,2},{1,3},{2,0},{3,1},{4,6},{5,7},{6,4},{7,5},{8,10},{9,11},{10,... | collective-permute-start | bytes 786440 | tf_op jit(solution)/shard_map/ppermute | solution.py:35
  161.1 11.0 %collective-permute-start.26 = (bf16[256,768]{1,0:T(8,128)(2,1)}, bf16[256,768]{1,0:T(8,128)(2,1)S(1)}, u32[]{:S(2)}, u32[]{:S(2)}) collective-permute-start(bf16[256,768]{1,0:T(8,128)(2,1)} %add_convert_fusion.1), channel_id=1, source_target_pairs={{0,224},{16,240},{32,0},{48,16},{64,32},{80,48},{96,64},{112,80},{... | collective-permute-start | bytes 1179656 | tf_op jit(solution)/shard_map/ppermute | solution.py:22
  173.4 12.0 %collective-permute-start.27 = (bf16[128,768]{1,0:T(8,128)(2,1)S(1)}, bf16[128,768]{1,0:T(8,128)(2,1)S(1)}, u32[]{:S(2)}, u32[]{:S(2)}) collective-permute-start(bf16[128,768]{1,0:T(8,128)(2,1)S(1)} %dynamic-slice_convert_fusion.1), channel_id=1, source_target_pairs={{0,16},{16,0},{32,48},{48,32},{64,80},{80,64},{96,112},{112,96},{1... | collective-permute-start | bytes 589832 | tf_op jit(solution)/shard_map/ppermute | solution.py:26
  (20 other events, 172.0 us)
Sparse Core Ops, SparseCore 0:
  9.9 42.6 all-gather.2
  54.4 39.9 all-gather.4
where the time goes:
time: 194 us; the launch traced here: 193 us
  starting transfers between devices  50.6 us (26%)
  Pallas kernels  47.6 us (25%)
  waiting for transfers between devices  45.5 us (23%)
  other arithmetic  22.7 us (12%)
  between operations  14.2 us (7%)
  local copies, waits for them, and re-layouts  6.61 us (3%)
  matrix products  5.71 us (3%)
    ppermute x19, starting transfers between devices, over_z(): return lax.ppermute(value, 'dp', pairs)  31.9 us
    pallas_call x5, Pallas kernels, absorb(): pl.pallas_call(body, out_shape=tuple(out_shape), grid_spec=pltpu.Prefetch...  25.3 us
    ppermute x19, waiting for transfers between devices, over_z(): return lax.ppermute(value, 'dp', pairs)  16.7 us
    ppermute x5, waiting for transfers between devices, over_yh(): return lax.ppermute(value, 'dp', [(d, d ^ 1) for d in range(16)])  14.2 us
    ppermute x3, waiting for transfers between devices, over_x(): return lax.ppermute(value, 'tensor', pairs)  13.3 us
    ppermute x5, starting transfers between devices, over_yh(): return lax.ppermute(value, 'dp', [(d, d ^ 1) for d in range(16)])  13.1 us
    pallas_call x1, Pallas kernels, ring_rows(): pl.pallas_call(body, out_shape=jax.ShapeDtypeStruct((m, n), jnp.float32),...  8.98 us
    pallas_call x1, Pallas kernels, contract_rows(): pl.pallas_call(body, out_shape=jax.ShapeDtypeStruct((m, n), jnp.float32),...  8.86 us
  transfers between devices with their start and end apart: 31, of which 8 were waited for; matrix products, arithmetic and copies ran while one was open for 16% of the time, Pallas kernels for 25%

commit v1 on v0

--- a/solution.py
+++ b/solution.py
@@ -105,7 +105,7 @@
 
 def absorb(blocks, q_places, a_places, z, core, weights, wholes):
     count, with_attn = len(blocks), bool(a_places)
-    width, cols = weights.shape
+    cols, width = weights.shape
     attn_cols = blocks[0].shape[1] - 2 * cols
     at = lambda p: (z + p + NZ) % NZ
     where = jnp.stack([*map(at, q_places), core]).astype(jnp.int32)
@@ -140,11 +140,8 @@
                 outs[0][0, 0], outs[0][1, 0] = halves
                 if with_attn:
                     outs[3][0] = refs[k][:, 2 * cols :]
-                product = lax.dot_general(
-                    jnp.concatenate(halves),
-                    weights_ref[...],
-                    (((1,), (1,)), ((), ())),
-                    preferred_element_type=jnp.float32,
+                product = jnp.dot(
+                    jnp.concatenate(halves), weights_ref[...], preferred_element_type=jnp.float32
                 ).astype(jnp.bfloat16)
                 outs[1][0] = jnp.where(first, product[:TB], product[TB:])
                 outs[2][0] = jnp.where(first, product[TB:], product[:TB])
@@ -163,6 +160,32 @@
             transcendentals=0,
         ),
     )(where, *operands)
+
+
+def chip_parts(kept, sent, targets):
+    n = kept.shape[2]
+    count = len(targets)
+    pair = pl.BlockSpec((2, TB, n), lambda i, s: (s[i], 0, 0))
+
+    def body(where_ref, kept_ref, sent_ref, *outs):
+        total = (kept_ref[...].astype(jnp.float32) + sent_ref[...].astype(jnp.float32)).astype(jnp.bfloat16)
+        for k in range(count):
+
+            @pl.when(pl.program_id(0) == k)
+            def _():
+                outs[k][...] = total.reshape(2 * TB, n)
+
+    return pl.pallas_call(
+        body,
+        out_shape=(jax.ShapeDtypeStruct((2 * TB, n), jnp.bfloat16),) * count,
+        grid_spec=pltpu.PrefetchScalarGridSpec(
+            num_scalar_prefetch=1,
+            grid=(count,),
+            in_specs=[pair, pair],
+            out_specs=(pl.BlockSpec((2 * TB, n), lambda i, s: (0, 0)),) * count,
+        ),
+        cost_estimate=pl.CostEstimate(flops=NZ * TB * n, bytes_accessed=6 * NZ * TB * n, transcendentals=0),
+    )(jnp.stack(targets).astype(jnp.int32), kept, sent)
 
 
 def contract_rows(left, right, factor, tile):
@@ -186,7 +209,7 @@
             pl.BlockSpec(right.shape, lambda i: (0, 0, 0)),
         ],
         out_specs=pl.BlockSpec((tile, n), lambda i: (i, 0)),
-        compiler_params=pltpu.CompilerParams(vmem_limit_bytes=60 * 2**20),
+        compiler_params=pltpu.CompilerParams(vmem_limit_bytes=40 * 2**20),
         cost_estimate=pl.CostEstimate(
             flops=4 * NZ * TB * m * n, bytes_accessed=4 * NZ * TB * (m + n) + 4 * m * n, transcendentals=0
         ),
@@ -222,7 +245,7 @@
             + [pl.BlockSpec((NZ, 2, TB, n), lambda i, s: (0, 0, 0, 0))],
             out_specs=pl.BlockSpec((tile, n), lambda i, s: (i, 0)),
         ),
-        compiler_params=pltpu.CompilerParams(vmem_limit_bytes=60 * 2**20),
+        compiler_params=pltpu.CompilerParams(vmem_limit_bytes=40 * 2**20),
         cost_estimate=pl.CostEstimate(
             flops=4 * NZ * TB * m * n, bytes_accessed=4 * NZ * TB * (m + n) + 4 * m * n, transcendentals=0
         ),
@@ -280,36 +303,38 @@
     tables = rotary_tables(pair_ids.reshape(-1), window, z)
 
     up0, down0 = unrotate(qkv_grad, q_other, tables, up_attn, down_attn, yh, t)
+    up0, down0, w_t = tie(up0, down0, w_qkv.T)
     up1, down1 = tie(over_z(up0, 1), over_z(down0, -1))
 
-    attn1 = place_first(attn_out, 5)
-    *shares, attn1 = absorb([up0, down0], [0, 0], (1, 5), z, core, w_qkv, [None, None, None, attn1])
-    *shares, attn1 = absorb([up1, down1], [-1, 1], (3, 5), z, core, w_qkv, [*shares, attn1])
-    up2, down2, attn1, *shares = tie(over_z(up1, 1), over_z(down1, -1), attn1, *shares)
-
-    *shares, attn2 = absorb([up2, down2], [-2, 2], (0, 3), z, core, w_qkv, [*shares, None])
+    attn1 = place_first(attn_out, 3)
+    *shares, attn1 = absorb([up0, down0], [0, 0], (1, 3), z, core, w_t, [None, None, None, attn1])
+    *shares, attn2 = absorb([up1, down1], [-1, 1], (0, 2), z, core, w_t, [*shares, None])
+    up2, down2, attn1, attn2, *shares = tie(over_z(up1, 1), over_z(down1, -1), attn1, attn2, *shares)
+
+    *shares, attn3 = absorb([up2, down2], [-2, 2], (0, 3), z, core, w_t, [*shares, None])
     attn_part = contract_cols(g_all, w_out).astype(jnp.bfloat16)
-    up3, down3, attn_part, attn2, *shares = tie(over_z(up2, 1), over_z(down2, -1), attn_part, attn2, *shares)
-
-    attn1_other = over_yh(attn1)
+    up3, down3, attn1_other, attn_part, attn2, attn3, *shares = tie(
+        over_z(up2, 1), over_z(down2, -1), over_yh(attn1), attn_part, attn2, attn3, *shares
+    )
+
     fold = Fold(attn_part, z)
     fold.step()
     last = over_z(up3[:, : 2 * qkv_grad.shape[1]], 1)
-    *shares, attn2 = absorb([up3, down3], [-3, 3], (2, 3), z, core, w_qkv, [*shares, attn2])
-    last, fold.down, *shares = tie(last, fold.down, *shares)
-    q_all, kept, given = absorb([last], [4], None, z, core, w_qkv, shares)
+    *shares, attn3 = absorb([up3, down3], [-3, 3], (2, 3), z, core, w_t, [*shares, attn3])
+    last, fold.down, attn2_other, *shares = tie(last, fold.down, over_yh(attn2), *shares)
+    q_all, kept, given = absorb([last], [4], None, z, core, w_t, shares)
 
     q_all = q_all.reshape(2, NZ * TB, -1)
     sent = over_core(given)
+    attn3_other = over_yh(attn3)
     fold.step()
-    chip = (kept.astype(jnp.float32) + sent.astype(jnp.float32)).astype(jnp.bfloat16).reshape(NZ * TB, -1)
-    fold.up, fold.down, x_all, attn1_other, attn2, _ = tie(fold.up, fold.down, x_all, attn1_other, attn2, chip)
-    attn2_other = over_yh(attn2)
+    steps = (1, -1, 2)
+    mine, *away = chip_parts(kept, sent, [(x + k + NX) % NX for k in (0, *steps)])
+    fold.up, fold.down, x_all, attn3_other, _ = tie(fold.up, fold.down, x_all, attn3_other, mine)
     fold.step()
-    toward = lambda at: lax.dynamic_slice_in_dim(chip, at % NX * 2 * TB, 2 * TB, 0)
-    total = toward(x).astype(jnp.float32)
-    for steps in (1, -1, 2):
-        total = total + over_x(toward(x + steps + NX), steps).astype(jnp.float32)
+    total = mine.astype(jnp.float32)
+    for k, part in zip(steps, away):
+        total = total + over_x(part, k).astype(jnp.float32)
     keep = lax.dynamic_slice_in_dim(total, yl * TB, TB, 0)
     give = lax.dynamic_slice_in_dim(total, (1 - yl) * TB, TB, 0).astype(jnp.bfloat16)
     summed = keep + over_yl(give).astype(jnp.float32)
@@ -321,10 +346,10 @@
     send = lax.dynamic_slice_in_dim(sums, (1 - yh) * TB, TB, 0).astype(jnp.bfloat16)
     attn_grad = (keep + over_yh(send).astype(jnp.float32)).astype(jnp.bfloat16)
 
-    attn2_other, _, _ = tie(attn2_other, give, send)
+    attn3_other, _, _ = tie(attn3_other, give, send)
     wqkv_grad = contract_rows(x_all, q_all, factor, 256)
     order = [(z + p + NZ) % NZ for p in (0, -1, 1, -2, 2, -3, 3, 4)]
-    wout_grad = ring_rows([(attn1, attn1_other), (attn2, attn2_other)], g_all, order, yh, factor, 256)
+    wout_grad = ring_rows([(attn1, attn1_other), (attn2, attn2_other), (attn3, attn3_other)], g_all, order, yh, factor, 256)
     return (input_grad, attn_grad, wqkv_grad, wout_grad)
 
 

time: 194 us -> 203 us (1.046)
  starting transfers between devices: 50.6 us -> 61.6 us
  other arithmetic: 22.7 us -> 16.6 us
  local copies, waits for them, and re-layouts: 6.61 us -> 10.1 us
    ppermute x3, starting transfers between devices: 4.15 us -> 17.6 us  [over_x(): return lax.ppermute(value, 'tensor', pairs)]
    ppermute x5 -> x6, waiting for transfers between devices: 14.2 us -> 8.04 us  [over_yh(): return lax.ppermute(value, 'dp', [(d, d ^ 1) for d in range(16)])]
    pallas_call x0 -> x1, Pallas kernels: none -> 5.35 us  [chip_parts(): pl.pallas_call(body, out_shape=(jax.ShapeDtypeStruct((2 * TB, n), jnp.bfl...]
    unnamed x26 -> x37, local copies, waits for them, and re-layouts: 2.07 us -> 6.85 us
    convert_element_type x1 -> x0, other arithmetic: 4.59 us -> none  [shards(): (kept.astype(jnp.float32) + sent.astype(jnp.float32)).astype(jnp.bfloat16)]
    ppermute x3, waiting for transfers between devices: 13.3 us -> 17.7 us  [over_x(): return lax.ppermute(value, 'tensor', pairs)]
    ppermute x5 -> x6, starting transfers between devices: 13.1 us -> 10.2 us  [over_yh(): return lax.ppermute(value, 'dp', [(d, d ^ 1) for d in range(16)])]
    dynamic_slice x1 -> x0, local copies, waits for them, and re-layouts: 2.31 us -> none  [shards(): lax.dynamic_slice_in_dim(chip, at % NX * 2 * TB, 2 * TB, 0)]
  transfers between devices with their start and end apart: 31 -> 32, of which waited for: 8 -> 10; matrix products, arithmetic and copies ran while one was open for 16% -> 13% of each run, Pallas kernels for 25% -> 24%
where the time goes in v1:
time: 203 us
  starting transfers between devices  61.6 us (30%)
  Pallas kernels  49 us (24%)
  waiting for transfers between devices  45.4 us (22%)
  other arithmetic  16.6 us (8%)
  between operations  14.3 us (7%)
  local copies, waits for them, and re-layouts  10.1 us (5%)
  matrix products  5.78 us (3%)
    ppermute x19, starting transfers between devices, over_z(): return lax.ppermute(value, 'dp', pairs)  32.3 us
    pallas_call x5, Pallas kernels, absorb(): pl.pallas_call(body, out_shape=tuple(out_shape), grid_spec=pltpu.Prefetch...  25.3 us
    ppermute x19, waiting for transfers between devices, over_z(): return lax.ppermute(value, 'dp', pairs)  18.3 us
    ppermute x3, waiting for transfers between devices, over_x(): return lax.ppermute(value, 'tensor', pairs)  17.7 us
    ppermute x3, starting transfers between devices, over_x(): return lax.ppermute(value, 'tensor', pairs)  17.6 us
    ppermute x6, starting transfers between devices, over_yh(): return lax.ppermute(value, 'dp', [(d, d ^ 1) for d in range(16)])  10.2 us
    ppermute x6, waiting for transfers between devices, over_yh(): return lax.ppermute(value, 'dp', [(d, d ^ 1) for d in range(16)])  8.04 us
    pallas_call x1, Pallas kernels, ring_rows(): pl.pallas_call(body, out_shape=jax.ShapeDtypeStruct((m, n), jnp.float32),...  7.29 us
  transfers between devices with their start and end apart: 32, of which 10 were waited for; matrix products, arithmetic and copies ran while one was open for 13% of the time, Pallas kernels for 24%

profile of v1, /device:TPU:2, one launch (start us, length us, event | category | flops | bytes accessed | tf_op | source)
XLA Modules:
  0.0 202.8 jit_solution(12893527314721305598)
XLA Ops:
  8.7 3.3 %collective-permute-start.1 = (s32[1,128]{1,0:T(1,128)}, s32[1,128]{1,0:T(1,128)S(1)}, u32[]{:S(2)}, u32[]{:S(2)}) collective-permute-start(s32[1,128]{1,0:T(1,128)} %bitcast.34), channel_id=1, source_target_pairs={{0,16},{16,0},{32,48},{48,32},{64,80},{80,64},{96,112},{112,96},{1... | collective-permute-start | bytes 1544 | tf_op jit(solution)/shard_map/ppermute | solution.py:26
  16.6 3.3 %collective-permute-start.3 = (s32[2,128]{1,0:T(2,128)S(1)}, s32[2,128]{1,0:T(2,128)S(1)}, u32[]{:S(2)}, u32[]{:S(2)}) collective-permute-start(s32[2,128]{1,0:T(2,128)S(1)} %add_select_fusion), channel_id=1, source_target_pairs={{0,64},{16,80},{32,96},{48,112},{64,128},{80,144},{96,160},{112,17... | collective-permute-start | bytes 3080 | tf_op jit(solution)/shard_map/ppermute | solution.py:22
  19.9 3.8 %copy.26 = bf16[1024,896]{0,1:T(8,128)(2,1)} copy(bf16[1024,896]{1,0:T(8,128)(2,1)} %param.11) | data formatting | bytes 3670016 | tf_op args[4]
  23.7 3.1 %collective-permute-start.5 = (bf16[128,768]{1,0:T(8,128)(2,1)S(1)}, bf16[128,768]{1,0:T(8,128)(2,1)S(1)}, u32[]{:S(2)}, u32[]{:S(2)}) collective-permute-start(bf16[128,768]{1,0:T(8,128)(2,1)S(1)} %copy-done.14), channel_id=1, source_target_pairs={{0,32},{16,48},{32,64},{48,80},{64,96},{80,112},{96,128},{112,144}... | collective-permute-start | bytes 589832 | tf_op jit(solution)/shard_map/ppermute | solution.py:22
  29.4 3.3 %collective-permute-done.4 = s32[4,128]{1,0:T(4,128)S(1)} collective-permute-done((s32[4,128]{1,0:T(4,128)S(1)}, s32[4,128]{1,0:T(4,128)S(1)}, u32[]{:S(2)}, u32[]{:S(2)}) %collective-permute-start.4) | collective-permute-done | bytes 2080 | tf_op jit(solution)/shard_map/ppermute | solution.py:22
  41.2 11.5 %collective-permute-done.7.refs_0_ = bf16[128,2560]{1,0:T(8,128)(2,1)S(1)} collective-permute-done((bf16[128,2560]{1,0:T(8,128)(2,1)}, bf16[128,2560]{1,0:T(8,128)(2,1)S(1)}, u32[]{:S(2)}, u32[]{:S(2)}) %collective-permute-start.7) | collective-permute-done | bytes 655392 | tf_op jit(solution)/shard_map/ppermute | solution.py:22
  59.5 5.2 %shard_map.104 = (bf16[2,8,128,896]{3,2,1,0:T(8,128)(2,1)}, bf16[8,128,1024]{2,1,0:T(8,128)(2,1)}, bf16[8,128,1024]{2,1,0:T(8,128)(2,1)}, bf16[3,128,768]{2,1,0:T(8,128)(2,1)}) custom-call(s32[3]{0:T(128)} %get-tuple-element.128.where_ref, bf16[128,2560]{1,0:T(8,128)(2,1)} %get-tuple-element.65.refs_0_, ...), custom_call_target="tpu_custom_call", output_to_operand_aliasing={{3}: (4, {})} | custom-call | flops 939524096 | bytes 5505024 | tf_op jit(solution)/shard_map/pallas_call | solution.py:149
  64.7 5.5 %shard_map.105 = (bf16[2,8,128,896]{3,2,1,0:T(8,128)(2,1)}, bf16[8,128,1024]{2,1,0:T(8,128)(2,1)}, bf16[8,128,1024]{2,1,0:T(8,128)(2,1)}, bf16[2,128,768]{2,1,0:T(8,128)(2,1)}) custom-call(s32[3]{0:T(128)} %get-tuple-element.129.where_ref, bf16[128,2560]{1,0:T(8,128)(2,1)} %copy-done.10, ...), custom_call_target="tpu_custom_call", output_to_operand_aliasing={{0}: (4, {}), {1}: (5, {}), {2}: (6, {})} | custom-call | flops 939524096 | bytes 5505024 | tf_op jit(solution)/shard_map/pallas_call | solution.py:149
  70.3 3.2 %collective-permute-start.12 = (bf16[128,2560]{1,0:T(8,128)(2,1)}, bf16[128,2560]{1,0:T(8,128)(2,1)}, u32[]{:S(2)}, u32[]{:S(2)}) collective-permute-start(bf16[128,2560]{1,0:T(8,128)(2,1)} %collective-permute-done.10.refs_1_), channel_id=1, source_target_pairs={{0,224},{16,240},{32,0},{48,16},{64,32},{80,48},{96,64},{112,80},{... | collective-permute-start | bytes 1966088 | tf_op jit(solution)/shard_map/ppermute | solution.py:22
  76.7 5.2 %shard_map.106 = (bf16[2,8,128,896]{3,2,1,0:T(8,128)(2,1)}, bf16[8,128,1024]{2,1,0:T(8,128)(2,1)}, bf16[8,128,1024]{2,1,0:T(8,128)(2,1)}, bf16[3,128,768]{2,1,0:T(8,128)(2,1)}) custom-call(s32[3]{0:T(128)} %get-tuple-element.130.where_ref, ...), custom_call_target="tpu_custom_call", output_to_operand_aliasing={{0}: (4, {}), {1}: (5, {}), {2}: (6, {})} | custom-call | flops 939524096 | bytes 5505024 | tf_op jit(solution)/shard_map/pallas_call | solution.py:149
  81.9 5.8 %convolution_convert_fusion = bf16[2048,768]{1,0:T(8,128)(2,1)S(1)} fusion(bf16[2048,1024]{1,0:T(8,128)(2,1)} %all-gather.3.cloned.1.call-done, bf16[768,1024]{1,0:T(8,128)(2,1)S(1)} %copy-done), kind=kOutput, calls=%fused_computation | convolution fusion | flops 3222798336 | bytes 8912896 | tf_op jit(solution)/shard_map/dot_general | solution.py:256
  90.9 3.2 %collective-permute-start.15 = (bf16[256,768]{1,0:T(8,128)(2,1)}, bf16[256,768]{1,0:T(8,128)(2,1)S(1)}, u32[]{:S(2)}, u32[]{:S(2)}) collective-permute-start(bf16[256,768]{1,0:T(8,128)(2,1)} %get-tuple-element.123), channel_id=1, source_target_pairs={{0,224},{16,240},{32,0},{48,16},{64,32},{80,48},{96,64},{112,80},{... | collective-permute-start | bytes 1179656 | tf_op jit(solution)/shard_map/ppermute | solution.py:22
  95.1 5.2 %shard_map.107 = (bf16[2,8,128,896]{3,2,1,0:T(8,128)(2,1)}, bf16[8,128,1024]{2,1,0:T(8,128)(2,1)}, bf16[8,128,1024]{2,1,0:T(8,128)(2,1)}, bf16[3,128,768]{2,1,0:T(8,128)(2,1)}) custom-call(s32[3]{0:T(128)} %get-tuple-element.131.where_ref, ...), custom_call_target="tpu_custom_call", output_to_operand_aliasing={{0}: (4, {}), {1}: (5, {}), {2}: (6, {}), {3}: (7, {})} | custom-call | flops 939524096 | bytes 5505024 | tf_op jit(solution)/shard_map/pallas_call | solution.py:149
  103.5 4.1 %shard_map.108 = (bf16[2,8,128,896]{3,2,1,0:T(8,128)(2,1)}, bf16[8,128,1024]{2,1,0:T(8,128)(2,1)}, bf16[8,128,1024]{2,1,0:T(8,128)(2,1)}) custom-call(s32[2]{0:T(128)} %pad_add_fusion.2.where_ref, bf16[128,1792]{1,0:T(8,128)(2,1)} %collective-permute-done.14.refs_0_, ...), custom_call_target="tpu_custom_call", output_to_operand_aliasing={{0}: (3, {}), {1}: (4, {}), {2}: (5, {})} | custom-call | flops 469762048 | bytes 3276800 | tf_op jit(solution)/shard_map/pallas_call | solution.py:149
  110.3 3.2 %collective-permute-start.23 = (bf16[256,768]{1,0:T(8,128)(2,1)}, bf16[256,768]{1,0:T(8,128)(2,1)}, u32[]{:S(2)}, u32[]{:S(2)}) collective-permute-start(bf16[256,768]{1,0:T(8,128)(2,1)} %add_convert_fusion.4), channel_id=1, source_target_pairs={{0,224},{16,240},{32,0},{48,16},{64,32},{80,48},{96,64},{112,80},{... | collective-permute-start | bytes 1179656 | tf_op jit(solution)/shard_map/ppermute | solution.py:22
  114.2 5.3 %shard_map.109 = (bf16[256,1024]{1,0:T(8,128)(2,1)}, bf16[256,1024]{1,0:T(8,128)(2,1)}, bf16[256,1024]{1,0:T(8,128)(2,1)}, bf16[256,1024]{1,0:T(8,128)(2,1)}) custom-call(s32[4]{0:T(128)} %pad_add_fusion.1.where_ref, bf16[8,128,1024]{2,1,0:T(8,128)(2,1)} %get-tuple-element.104.kept_ref, bf16[8,128,1024]{2,1,0:T(8,128)(2,1)} %collective-permute-done.17.sent_ref), custom_call_target="tpu_custom_call" | custom-call | flops 1048576 | bytes 6291456 | tf_op jit(solution)/shard_map/pallas_call | solution.py:178
  121.1 3.9 %collective-permute-done.24.refs_5_ = bf16[3,128,768]{2,1,0:T(8,128)(2,1)} collective-permute-done((bf16[3,128,768]{2,1,0:T(8,128)(2,1)S(1)}, bf16[3,128,768]{2,1,0:T(8,128)(2,1)}, u32[]{:S(2)}, u32[]{:S(2)}) %collective-permute-start.24) | collective-permute-done | bytes 589856 | tf_op jit(solution)/shard_map/ppermute | solution.py:26
  128.5 12.2 %collective-permute-start.19 = (bf16[256,1024]{1,0:T(8,128)(2,1)}, bf16[256,1024]{1,0:T(8,128)(2,1)}, u32[]{:S(2)}, u32[]{:S(2)}) collective-permute-start(bf16[256,1024]{1,0:T(8,128)(2,1)} %get-tuple-element.108), channel_id=1, source_target_pairs={{0,12},{1,13},{2,14},{3,15},{4,0},{5,1},{6,2},{7,3},{8,4},{9,5},{1... | collective-permute-start | bytes 1572872 | tf_op jit(solution)/shard_map/ppermute | solution.py:31
  140.7 3.8 %collective-permute-start.20 = (bf16[256,1024]{1,0:T(8,128)(2,1)}, bf16[256,1024]{1,0:T(8,128)(2,1)}, u32[]{:S(2)}, u32[]{:S(2)}) collective-permute-start(bf16[256,1024]{1,0:T(8,128)(2,1)} %get-tuple-element.109), channel_id=1, source_target_pairs={{0,8},{1,9},{2,10},{3,11},{4,12},{5,13},{6,14},{7,15},{8,0},{9,1},... | collective-permute-start | bytes 1572872 | tf_op jit(solution)/shard_map/ppermute | solution.py:31
  149.4 4.4 %collective-permute-done.18 = bf16[256,1024]{1,0:T(8,128)(2,1)} collective-permute-done((bf16[256,1024]{1,0:T(8,128)(2,1)}, bf16[256,1024]{1,0:T(8,128)(2,1)}, u32[]{:S(2)}, u32[]{:S(2)}) %collective-permute-start.18) | collective-permute-done | bytes 524320 | tf_op jit(solution)/shard_map/ppermute | solution.py:31
  155.3 11.8 %collective-permute-done.20 = bf16[256,1024]{1,0:T(8,128)(2,1)} collective-permute-done((bf16[256,1024]{1,0:T(8,128)(2,1)}, bf16[256,1024]{1,0:T(8,128)(2,1)}, u32[]{:S(2)}, u32[]{:S(2)}) %collective-permute-start.20) | collective-permute-done | bytes 524320 | tf_op jit(solution)/shard_map/ppermute | solution.py:31
  171.5 3.3 %collective-permute-start.28 = (bf16[256,768]{1,0:T(8,128)(2,1)S(1)}, bf16[256,768]{1,0:T(8,128)(2,1)S(1)}, u32[]{:S(2)}, u32[]{:S(2)}) collective-permute-start(bf16[256,768]{1,0:T(8,128)(2,1)S(1)} %add_convert_fusion), channel_id=1, source_target_pairs={{0,224},{16,240},{32,0},{48,16},{64,32},{80,48},{96,64},{112,80},{... | collective-permute-start | bytes 1179656 | tf_op jit(solution)/shard_map/ppermute | solution.py:22
  176.9 6.7 %shard_map.110 = f32[1024,896]{1,0:T(8,128)} custom-call(bf16[8,2,128,1024]{3,2,1,0:T(8,128)(2,1)S(1)} %bitcast.28, bf16[2,1024,896]{2,1,0:T(8,128)(2,1)S(1)} %bitcast.26), custom_call_target="tpu_custom_call" | custom-call | flops 3758096384 | bytes 11534336 | tf_op jit(solution)/shard_map/pallas_call | solution.py:203
  187.9 7.3 %shard_map.111 = f32[768,1024]{1,0:T(8,128)} custom-call(s32[9]{0:T(128)S(1)} %stack.105.where_ref, bf16[3,128,768]{2,1,0:T(8,128)(2,1)S(1)} %copy-done.2, bf16[3,128,768]{2,1,0:T(8,128)(2,1)S(1)} %collective-permute-done.13.refs_1_, bf16[2,128,768]{2,1,0:T(8,128)(2,1)S(1)} %copy-done.7, bf16[2,128,768]{2,1,0:T(8,128)(2,1)} %collective-permute-done.16.refs_3_, ...), custom_call_target="tpu_custom_call" | custom-call | flops 3221225472 | bytes 10485760 | tf_op jit(solution)/shard_map/pallas_call | solution.py:238
  (116 shorter events, 60.8 us)
Async XLA Ops:
  7.2 74.7 %all-gather.3.cloned.1.call-start = ((), (), s32[]{:S(2)}) async-start(), calls=%async_computation | async-start | bytes 4456448 | tf_op jit(solution)/shard_map/all_gather | solution.py:291
  7.9 111.6 %all-gather.5.cloned.1.call-start = ((), (), s32[]{:S(2)}) async-start(), calls=%async_computation.1 | async-start | bytes 4456448 | tf_op jit(solution)/shard_map/all_gather | solution.py:292
  12.0 22.3 %collective-permute-start = (bf16[128,896]{1,0:T(8,128)(2,1)}, bf16[128,896]{1,0:T(8,128)(2,1)S(1)}, u32[]{:S(2)}, u32[]{:S(2)}) collective-permute-start(bf16[128,896]{1,0:T(8,128)(2,1)} %own_ref.1), channel_id=1, source_target_pairs={{0,16},{16,0},{32,48},{48,32},{64,80},{80,64},{96,112},{112,96},{1... | collective-permute-start | bytes 688136 | tf_op jit(solution)/shard_map/ppermute | solution.py:26
  14.7 12.2 %collective-permute-start.2 = (s32[2,128]{1,0:T(2,128)S(1)}, s32[2,128]{1,0:T(2,128)S(1)}, u32[]{:S(2)}, u32[]{:S(2)}) collective-permute-start(s32[2,128]{1,0:T(2,128)S(1)} %add_select_fusion), channel_id=1, source_target_pairs={{0,32},{16,48},{32,64},{48,80},{64,96},{80,112},{96,128},{112,144}... | collective-permute-start | bytes 3080 | tf_op jit(solution)/shard_map/ppermute | solution.py:22
  23.7 10.6 %collective-permute-start.5 = (bf16[128,768]{1,0:T(8,128)(2,1)S(1)}, bf16[128,768]{1,0:T(8,128)(2,1)S(1)}, u32[]{:S(2)}, u32[]{:S(2)}) collective-permute-start(bf16[128,768]{1,0:T(8,128)(2,1)S(1)} %copy-done.14), channel_id=1, source_target_pairs={{0,32},{16,48},{32,64},{48,80},{64,96},{80,112},{96,128},{112,144}... | collective-permute-start | bytes 589832 | tf_op jit(solution)/shard_map/ppermute | solution.py:22
  37.9 14.7 %collective-permute-start.7 = (bf16[128,2560]{1,0:T(8,128)(2,1)}, bf16[128,2560]{1,0:T(8,128)(2,1)S(1)}, u32[]{:S(2)}, u32[]{:S(2)}) collective-permute-start(bf16[128,2560]{1,0:T(8,128)(2,1)} %get-tuple-element.65.refs_0_), channel_id=1, source_target_pairs={{0,32},{16,48},{32,64},{48,80},{64,96},{80,112},{96,128},{112,144}... | collective-permute-start | bytes 1966088 | tf_op jit(solution)/shard_map/ppermute | solution.py:22
  39.8 14.8 %collective-permute-start.8 = (bf16[128,2560]{1,0:T(8,128)(2,1)}, bf16[128,2560]{1,0:T(8,128)(2,1)S(1)}, u32[]{:S(2)}, u32[]{:S(2)}) collective-permute-start(bf16[128,2560]{1,0:T(8,128)(2,1)} %get-tuple-element.66.refs_1_), channel_id=1, source_target_pairs={{0,224},{16,240},{32,0},{48,16},{64,32},{80,48},{96,64},{112,80},{... | collective-permute-start | bytes 1966088 | tf_op jit(solution)/shard_map/ppermute | solution.py:22
  54.6 15.6 %collective-permute-start.10 = (bf16[128,2560]{1,0:T(8,128)(2,1)S(1)}, bf16[128,2560]{1,0:T(8,128)(2,1)}, u32[]{:S(2)}, u32[]{:S(2)}) collective-permute-start(bf16[128,2560]{1,0:T(8,128)(2,1)S(1)} %collective-permute-done.8.refs_1_), channel_id=1, source_target_pairs={{0,224},{16,240},{32,0},{48,16},{64,32},{80,48},{96,64},{112,80},{... | collective-permute-start | bytes 1966088 | tf_op jit(solution)/shard_map/ppermute | solution.py:22
  56.3 14.0 %collective-permute-start.9 = (bf16[128,2560]{1,0:T(8,128)(2,1)S(1)}, bf16[128,2560]{1,0:T(8,128)(2,1)}, u32[]{:S(2)}, u32[]{:S(2)}) collective-permute-start(bf16[128,2560]{1,0:T(8,128)(2,1)S(1)} %collective-permute-done.7.refs_0_), channel_id=1, source_target_pairs={{0,32},{16,48},{32,64},{48,80},{64,96},{80,112},{96,128},{112,144}... | collective-permute-start | bytes 1966088 | tf_op jit(solution)/shard_map/ppermute | solution.py:22
  70.2 17.5 %collective-permute-start.11 = (bf16[128,2560]{1,0:T(8,128)(2,1)}, bf16[128,2560]{1,0:T(8,128)(2,1)}, u32[]{:S(2)}, u32[]{:S(2)}) collective-permute-start(bf16[128,2560]{1,0:T(8,128)(2,1)} %collective-permute-done.9.refs_0_), channel_id=1, source_target_pairs={{0,32},{16,48},{32,64},{48,80},{64,96},{80,112},{96,128},{112,144}... | collective-permute-start | bytes 1966088 | tf_op jit(solution)/shard_map/ppermute | solution.py:22
  70.3 17.4 %collective-permute-start.12 = (bf16[128,2560]{1,0:T(8,128)(2,1)}, bf16[128,2560]{1,0:T(8,128)(2,1)}, u32[]{:S(2)}, u32[]{:S(2)}) collective-permute-start(bf16[128,2560]{1,0:T(8,128)(2,1)} %collective-permute-done.10.refs_1_), channel_id=1, source_target_pairs={{0,224},{16,240},{32,0},{48,16},{64,32},{80,48},{96,64},{112,80},{... | collective-permute-start | bytes 1966088 | tf_op jit(solution)/shard_map/ppermute | solution.py:22
  73.6 14.2 %collective-permute-start.13 = (bf16[3,128,768]{2,1,0:T(8,128)(2,1)S(1)}, bf16[3,128,768]{2,1,0:T(8,128)(2,1)S(1)}, u32[]{:S(2)}, u32[]{:S(2)}) collective-permute-start(bf16[3,128,768]{2,1,0:T(8,128)(2,1)S(1)} %copy-done.2), channel_id=1, source_target_pairs={{0,16},{16,0},{32,48},{48,32},{64,80},{80,64},{96,112},{112,96},{1... | collective-permute-start | bytes 1769480 | tf_op jit(solution)/shard_map/ppermute | solution.py:26
  89.9 13.6 %collective-permute-start.14 = (bf16[128,1792]{1,0:T(8,128)(2,1)}, bf16[128,1792]{1,0:T(8,128)(2,1)}, u32[]{:S(2)}, u32[]{:S(2)}) collective-permute-start(bf16[128,1792]{1,0:T(8,128)(2,1)} %slice.3), channel_id=1, source_target_pairs={{0,32},{16,48},{32,64},{48,80},{64,96},{80,112},{96,128},{112,144}... | collective-permute-start | bytes 1376264 | tf_op jit(solution)/shard_map/ppermute | solution.py:22
  107.6 17.4 %collective-permute-start.24 = (bf16[3,128,768]{2,1,0:T(8,128)(2,1)S(1)}, bf16[3,128,768]{2,1,0:T(8,128)(2,1)}, u32[]{:S(2)}, u32[]{:S(2)}) collective-permute-start(bf16[3,128,768]{2,1,0:T(8,128)(2,1)S(1)} %copy-done.3), channel_id=1, source_target_pairs={{0,16},{16,0},{32,48},{48,32},{64,80},{80,64},{96,112},{112,96},{1... | collective-permute-start | bytes 1769480 | tf_op jit(solution)/shard_map/ppermute | solution.py:26
  108.3 12.7 %collective-permute-start.22 = (bf16[256,768]{1,0:T(8,128)(2,1)}, bf16[256,768]{1,0:T(8,128)(2,1)}, u32[]{:S(2)}, u32[]{:S(2)}) collective-permute-start(bf16[256,768]{1,0:T(8,128)(2,1)} %get-tuple-element.122), channel_id=1, source_target_pairs={{0,32},{16,48},{32,64},{48,80},{64,96},{80,112},{96,128},{112,144}... | collective-permute-start | bytes 1179656 | tf_op jit(solution)/shard_map/ppermute | solution.py:22
  110.3 14.6 %collective-permute-start.23 = (bf16[256,768]{1,0:T(8,128)(2,1)}, bf16[256,768]{1,0:T(8,128)(2,1)}, u32[]{:S(2)}, u32[]{:S(2)}) collective-permute-start(bf16[256,768]{1,0:T(8,128)(2,1)} %add_convert_fusion.4), channel_id=1, source_target_pairs={{0,224},{16,240},{32,0},{48,16},{64,32},{80,48},{96,64},{112,80},{... | collective-permute-start | bytes 1179656 | tf_op jit(solution)/shard_map/ppermute | solution.py:22
  126.9 17.6 %collective-permute-start.25 = (bf16[256,768]{1,0:T(8,128)(2,1)}, bf16[256,768]{1,0:T(8,128)(2,1)}, u32[]{:S(2)}, u32[]{:S(2)}) collective-permute-start(bf16[256,768]{1,0:T(8,128)(2,1)} %add_convert_fusion.3), channel_id=1, source_target_pairs={{0,32},{16,48},{32,64},{48,80},{64,96},{80,112},{96,128},{112,144}... | collective-permute-start | bytes 1179656 | tf_op jit(solution)/shard_map/ppermute | solution.py:22
  126.9 26.8 %collective-permute-start.18 = (bf16[256,1024]{1,0:T(8,128)(2,1)}, bf16[256,1024]{1,0:T(8,128)(2,1)}, u32[]{:S(2)}, u32[]{:S(2)}) collective-permute-start(bf16[256,1024]{1,0:T(8,128)(2,1)} %get-tuple-element.107), channel_id=1, source_target_pairs={{0,4},{1,5},{2,6},{3,7},{4,8},{5,9},{6,10},{7,11},{8,12},{9,13},{1... | collective-permute-start | bytes 1572872 | tf_op jit(solution)/shard_map/ppermute | solution.py:31
  128.5 26.8 %collective-permute-start.19 = (bf16[256,1024]{1,0:T(8,128)(2,1)}, bf16[256,1024]{1,0:T(8,128)(2,1)}, u32[]{:S(2)}, u32[]{:S(2)}) collective-permute-start(bf16[256,1024]{1,0:T(8,128)(2,1)} %get-tuple-element.108), channel_id=1, source_target_pairs={{0,12},{1,13},{2,14},{3,15},{4,0},{5,1},{6,2},{7,3},{8,4},{9,5},{1... | collective-permute-start | bytes 1572872 | tf_op jit(solution)/shard_map/ppermute | solution.py:31
  140.7 26.4 %collective-permute-start.20 = (bf16[256,1024]{1,0:T(8,128)(2,1)}, bf16[256,1024]{1,0:T(8,128)(2,1)}, u32[]{:S(2)}, u32[]{:S(2)}) collective-permute-start(bf16[256,1024]{1,0:T(8,128)(2,1)} %get-tuple-element.109), channel_id=1, source_target_pairs={{0,8},{1,9},{2,10},{3,11},{4,12},{5,13},{6,14},{7,15},{8,0},{9,1},... | collective-permute-start | bytes 1572872 | tf_op jit(solution)/shard_map/ppermute | solution.py:31
  146.3 24.1 %collective-permute-start.27 = (bf16[256,768]{1,0:T(8,128)(2,1)S(1)}, bf16[256,768]{1,0:T(8,128)(2,1)S(1)}, u32[]{:S(2)}, u32[]{:S(2)}) collective-permute-start(bf16[256,768]{1,0:T(8,128)(2,1)S(1)} %get-tuple-element.121), channel_id=1, source_target_pairs={{0,224},{16,240},{32,0},{48,16},{64,32},{80,48},{96,64},{112,80},{... | collective-permute-start | bytes 1179656 | tf_op jit(solution)/shard_map/ppermute | solution.py:22
  149.4 35.1 %collective-permute-start.26 = (bf16[256,768]{1,0:T(8,128)(2,1)S(1)}, bf16[256,768]{1,0:T(8,128)(2,1)S(1)}, u32[]{:S(2)}, u32[]{:S(2)}) collective-permute-start(bf16[256,768]{1,0:T(8,128)(2,1)S(1)} %get-tuple-element.120), channel_id=1, source_target_pairs={{0,32},{16,48},{32,64},{48,80},{64,96},{80,112},{96,128},{112,144}... | collective-permute-start | bytes 1179656 | tf_op jit(solution)/shard_map/ppermute | solution.py:22
  169.0 14.7 %collective-permute-start.21 = (bf16[128,1024]{1,0:T(8,128)(2,1)S(1)}, bf16[128,1024]{1,0:T(8,128)(2,1)S(1)}, u32[]{:S(2)}, u32[]{:S(2)}) collective-permute-start(bf16[128,1024]{1,0:T(8,128)(2,1)S(1)} %dynamic-slice_convert_fusion), channel_id=1, source_target_pairs={{0,2},{1,3},{2,0},{3,1},{4,6},{5,7},{6,4},{7,5},{8,10},{9,11},{10,... | collective-permute-start | bytes 786440 | tf_op jit(solution)/shard_map/ppermute | solution.py:35
  171.5 13.0 %collective-permute-start.28 = (bf16[256,768]{1,0:T(8,128)(2,1)S(1)}, bf16[256,768]{1,0:T(8,128)(2,1)S(1)}, u32[]{:S(2)}, u32[]{:S(2)}) collective-permute-start(bf16[256,768]{1,0:T(8,128)(2,1)S(1)} %add_convert_fusion), channel_id=1, source_target_pairs={{0,224},{16,240},{32,0},{48,16},{64,32},{80,48},{96,64},{112,80},{... | collective-permute-start | bytes 1179656 | tf_op jit(solution)/shard_map/ppermute | solution.py:22
  (26 other events, 287.5 us)
Sparse Core Ops, SparseCore 0:
  9.9 42.6 all-gather.2
  54.5 46.9 all-gather.4

commit v2 on v0

--- a/solution.py
+++ b/solution.py
@@ -89,18 +89,21 @@
     )(jnp.stack([yh, t * (cols // HD)]).astype(jnp.int32), own, other, *tables, up_attn, down_attn)
 
 
-def place_first(block, count):
-    def body(block_ref, out_ref):
+def place_first(block, z):
+    def body(z_ref, block_ref, out_ref):
         out_ref[0] = block_ref[...]
 
     n = block.shape[1]
     return pl.pallas_call(
         body,
-        out_shape=jax.ShapeDtypeStruct((count, TB, n), jnp.bfloat16),
-        grid=(1,),
-        in_specs=[pl.BlockSpec((TB, n), lambda i: (0, 0))],
-        out_specs=pl.BlockSpec((1, TB, n), lambda i: (0, 0, 0)),
-    )(block)
+        out_shape=jax.ShapeDtypeStruct((NZ, TB, n), jnp.bfloat16),
+        grid_spec=pltpu.PrefetchScalarGridSpec(
+            num_scalar_prefetch=1,
+            grid=(1,),
+            in_specs=[pl.BlockSpec((TB, n), lambda i, s: (0, 0))],
+            out_specs=pl.BlockSpec((1, TB, n), lambda i, s: (s[0], 0, 0)),
+        ),
+    )(jnp.reshape(z, (1,)).astype(jnp.int32), block)
 
 
 def absorb(blocks, q_places, a_places, z, core, weights, wholes):
@@ -108,16 +111,15 @@
     width, cols = weights.shape
     attn_cols = blocks[0].shape[1] - 2 * cols
     at = lambda p: (z + p + NZ) % NZ
-    where = jnp.stack([*map(at, q_places), core]).astype(jnp.int32)
+    where = jnp.stack([*map(at, q_places), core, *map(at, a_places or ())]).astype(jnp.int32)
     q_spec = pl.BlockSpec((2, 1, TB, cols), lambda i, s: (0, s[i], 0, 0))
     share = pl.BlockSpec((1, TB, width), lambda i, s: (s[i], 0, 0))
     out_specs = [q_spec, share, share]
     out_shape = [jax.ShapeDtypeStruct((2, NZ, TB, cols), jnp.bfloat16)]
     out_shape += [jax.ShapeDtypeStruct((NZ, TB, width), jnp.bfloat16)] * 2
     if with_attn:
-        first, total = a_places
-        out_specs.append(pl.BlockSpec((1, TB, attn_cols), lambda i, s: (jnp.minimum(first + i, total - 1), 0, 0)))
-        out_shape.append(jax.ShapeDtypeStruct((total, TB, attn_cols), jnp.bfloat16))
+        out_specs.append(pl.BlockSpec((1, TB, attn_cols), lambda i, s: (s[count + 1 + i], 0, 0)))
+        out_shape.append(jax.ShapeDtypeStruct((NZ, TB, attn_cols), jnp.bfloat16))
     operands = [*blocks, weights]
     in_specs = [pl.BlockSpec(v.shape, lambda i, s: (0, 0)) for v in operands]
     aliases = {}
@@ -140,12 +142,7 @@
                 outs[0][0, 0], outs[0][1, 0] = halves
                 if with_attn:
                     outs[3][0] = refs[k][:, 2 * cols :]
-                product = lax.dot_general(
-                    jnp.concatenate(halves),
-                    weights_ref[...],
-                    (((1,), (1,)), ((), ())),
-                    preferred_element_type=jnp.float32,
-                ).astype(jnp.bfloat16)
+                product = contract_cols(jnp.concatenate(halves), weights_ref[...]).astype(jnp.bfloat16)
                 outs[1][0] = jnp.where(first, product[:TB], product[TB:])
                 outs[2][0] = jnp.where(first, product[TB:], product[:TB])
 
@@ -165,16 +162,18 @@
     )(where, *operands)
 
 
-def contract_rows(left, right, factor, tile):
-    m, n = left.shape[1], right.shape[2]
-
-    def body(left_ref, right_ref, out_ref):
+def contract_rows(halves, both, halves_left, factor, tile):
+    a, b = halves.shape[2], both.shape[1]
+    m, n = (a, b) if halves_left else (b, a)
+    half_tile, both_tile = (tile, b) if halves_left else (a, tile)
+    moving = (lambda i: (0, 0, i), lambda i: (0, 0, 0, 0)) if halves_left else (lambda i: (0, 0, 0), lambda i: (0, 0, 0, i))
+
+    def body(halves_ref, both_ref, out_ref):
         total = jnp.zeros(out_ref.shape, jnp.float32)
         for h in range(2):
-            tokens = left_ref[:, h].reshape(NZ * TB, tile)
-            total += lax.dot_general(
-                tokens, right_ref[h], (((0,), (0,)), ((), ())), preferred_element_type=jnp.float32
-            )
+            tokens = both_ref[:, h].reshape(NZ * TB, both_tile)
+            pair = (halves_ref[h], tokens) if halves_left else (tokens, halves_ref[h])
+            total += lax.dot_general(*pair, (((0,), (0,)), ((), ())), preferred_element_type=jnp.float32)
         out_ref[...] = total * factor
 
     return pl.pallas_call(
@@ -182,51 +181,41 @@
         out_shape=jax.ShapeDtypeStruct((m, n), jnp.float32),
         grid=(m // tile,),
         in_specs=[
-            pl.BlockSpec((NZ, 2, TB, tile), lambda i: (0, 0, 0, i)),
-            pl.BlockSpec(right.shape, lambda i: (0, 0, 0)),
+            pl.BlockSpec((2, NZ * TB, half_tile), moving[0]),
+            pl.BlockSpec((NZ, 2, TB, both_tile), moving[1]),
         ],
         out_specs=pl.BlockSpec((tile, n), lambda i: (i, 0)),
-        compiler_params=pltpu.CompilerParams(vmem_limit_bytes=60 * 2**20),
+        compiler_params=pltpu.CompilerParams(vmem_limit_bytes=40 * 2**20),
         cost_estimate=pl.CostEstimate(
             flops=4 * NZ * TB * m * n, bytes_accessed=4 * NZ * TB * (m + n) + 4 * m * n, transcendentals=0
         ),
-    )(left.reshape(NZ, 2, TB, m), right)
-
-
-def ring_rows(chunks, both, order, yh, factor, tile):
-    m, n = chunks[0][0].shape[2], both.shape[1]
-    operands = [v for chunk in chunks for v in chunk]
-
-    def body(where_ref, *refs):
-        both_ref, out_ref = refs[-2:]
-        total = jnp.zeros(out_ref.shape, jnp.float32)
-        for side in range(2):
-            h = where_ref[NZ] if side == 0 else 1 - where_ref[NZ]
-            first = 0
-            for c in range(len(chunks)):
-                part = refs[2 * c + side]
-                k = part.shape[0]
-                tokens = jnp.concatenate([both_ref[where_ref[first + j], h] for j in range(k)])
-                left = part[...].reshape(k * TB, tile)
-                total += lax.dot_general(left, tokens, (((0,), (0,)), ((), ())), preferred_element_type=jnp.float32)
-                first += k
-        out_ref[...] = total * factor
+    )(halves, both.reshape(NZ, 2, TB, b))
+
+
+def chip_parts(kept, sent, targets):
+    n = kept.shape[2]
+    count = len(targets)
+    pair = pl.BlockSpec((2, TB, n), lambda i, s: (s[i], 0, 0))
+
+    def body(where_ref, kept_ref, sent_ref, *outs):
+        total = (kept_ref[...].astype(jnp.float32) + sent_ref[...].astype(jnp.float32)).astype(jnp.bfloat16)
+        for k in range(count):
+
+            @pl.when(pl.program_id(0) == k)
+            def _():
+                outs[k][...] = total.reshape(2 * TB, n)
 
     return pl.pallas_call(
         body,
-        out_shape=jax.ShapeDtypeStruct((m, n), jnp.float32),
+        out_shape=(jax.ShapeDtypeStruct((2 * TB, n), jnp.bfloat16),) * count,
         grid_spec=pltpu.PrefetchScalarGridSpec(
             num_scalar_prefetch=1,
-            grid=(m // tile,),
-            in_specs=[pl.BlockSpec((v.shape[0], TB, tile), lambda i, s: (0, 0, i)) for v in operands]
-            + [pl.BlockSpec((NZ, 2, TB, n), lambda i, s: (0, 0, 0, 0))],
-            out_specs=pl.BlockSpec((tile, n), lambda i, s: (i, 0)),
-        ),
-        compiler_params=pltpu.CompilerParams(vmem_limit_bytes=60 * 2**20),
-        cost_estimate=pl.CostEstimate(
-            flops=4 * NZ * TB * m * n, bytes_accessed=4 * NZ * TB * (m + n) + 4 * m * n, transcendentals=0
-        ),
-    )(jnp.stack([*order, yh]).astype(jnp.int32), *operands, both.reshape(NZ, 2, TB, n))
+            grid=(count,),
+            in_specs=[pair, pair],
+            out_specs=(pl.BlockSpec((2 * TB, n), lambda i, s: (0, 0)),) * count,
+        ),
+        cost_estimate=pl.CostEstimate(flops=NZ * TB * n, bytes_accessed=6 * NZ * TB * n, transcendentals=0),
+    )(jnp.stack(targets).astype(jnp.int32), kept, sent)
 
 
 def contract_cols(left, right):
@@ -282,34 +271,37 @@
     up0, down0 = unrotate(qkv_grad, q_other, tables, up_attn, down_attn, yh, t)
     up1, down1 = tie(over_z(up0, 1), over_z(down0, -1))
 
-    attn1 = place_first(attn_out, 5)
-    *shares, attn1 = absorb([up0, down0], [0, 0], (1, 5), z, core, w_qkv, [None, None, None, attn1])
-    *shares, attn1 = absorb([up1, down1], [-1, 1], (3, 5), z, core, w_qkv, [*shares, attn1])
-    up2, down2, attn1, *shares = tie(over_z(up1, 1), over_z(down1, -1), attn1, *shares)
-
-    *shares, attn2 = absorb([up2, down2], [-2, 2], (0, 3), z, core, w_qkv, [*shares, None])
+    attn_all = place_first(attn_out, z)
+    *shares, attn_all = absorb([up0, down0], [0, 0], [-1, 1], z, core, w_qkv, [None, None, None, attn_all])
+    *shares, attn_all = absorb([up1, down1], [-1, 1], [-2, 2], z, core, w_qkv, [*shares, attn_all])
+    up2, down2, attn_all, *shares = tie(over_z(up1, 1), over_z(down1, -1), attn_all, *shares)
+
+    *shares, attn_all = absorb([up2, down2], [-2, 2], [-3, 3], z, core, w_qkv, [*shares, attn_all])
     attn_part = contract_cols(g_all, w_out).astype(jnp.bfloat16)
-    up3, down3, attn_part, attn2, *shares = tie(over_z(up2, 1), over_z(down2, -1), attn_part, attn2, *shares)
-
-    attn1_other = over_yh(attn1)
+    up3, down3, attn_part, attn_all, *shares = tie(over_z(up2, 1), over_z(down2, -1), attn_part, attn_all, *shares)
+
     fold = Fold(attn_part, z)
     fold.step()
     last = over_z(up3[:, : 2 * qkv_grad.shape[1]], 1)
-    *shares, attn2 = absorb([up3, down3], [-3, 3], (2, 3), z, core, w_qkv, [*shares, attn2])
-    last, fold.down, *shares = tie(last, fold.down, *shares)
+    *shares, attn_all = absorb([up3, down3], [-3, 3], [4, 4], z, core, w_qkv, [*shares, attn_all])
+    last, fold.down, attn_all, *shares = tie(last, fold.down, attn_all, *shares)
+    attn_all = lax.all_gather(
+        attn_all.reshape(1, NZ * TB, -1), "dp", axis=0, tiled=True, axis_index_groups=[[d, d + 1] for d in range(0, 16, 2)]
+    )
     q_all, kept, given = absorb([last], [4], None, z, core, w_qkv, shares)
 
     q_all = q_all.reshape(2, NZ * TB, -1)
     sent = over_core(given)
     fold.step()
-    chip = (kept.astype(jnp.float32) + sent.astype(jnp.float32)).astype(jnp.bfloat16).reshape(NZ * TB, -1)
-    fold.up, fold.down, x_all, attn1_other, attn2, _ = tie(fold.up, fold.down, x_all, attn1_other, attn2, chip)
-    attn2_other = over_yh(attn2)
+    steps = (1, -1, 2)
+    mine, *away = chip_parts(kept, sent, [(x + k + NX) % NX for k in (0, *steps)])
+    fold.up, fold.down, x_all, _ = tie(fold.up, fold.down, x_all, mine)
     fold.step()
-    toward = lambda at: lax.dynamic_slice_in_dim(chip, at % NX * 2 * TB, 2 * TB, 0)
-    total = toward(x).astype(jnp.float32)
-    for steps in (1, -1, 2):
-        total = total + over_x(toward(x + steps + NX), steps).astype(jnp.float32)
+    wqkv_grad = contract_rows(q_all, x_all, False, factor, 256)
+    *came, wqkv_grad = tie(*(over_x(part, k) for k, part in zip(steps, away)), wqkv_grad)
+    total = mine.astype(jnp.float32)
+    for part in came:
+        total = total + part.astype(jnp.float32)
     keep = lax.dynamic_slice_in_dim(total, yl * TB, TB, 0)
     give = lax.dynamic_slice_in_dim(total, (1 - yl) * TB, TB, 0).astype(jnp.bfloat16)
     summed = keep + over_yl(give).astype(jnp.float32)
@@ -321,10 +313,8 @@
     send = lax.dynamic_slice_in_dim(sums, (1 - yh) * TB, TB, 0).astype(jnp.bfloat16)
     attn_grad = (keep + over_yh(send).astype(jnp.float32)).astype(jnp.bfloat16)
 
-    attn2_other, _, _ = tie(attn2_other, give, send)
-    wqkv_grad = contract_rows(x_all, q_all, factor, 256)
-    order = [(z + p + NZ) % NZ for p in (0, -1, 1, -2, 2, -3, 3, 4)]
-    wout_grad = ring_rows([(attn1, attn1_other), (attn2, attn2_other)], g_all, order, yh, factor, 256)
+    attn_all, _, _ = tie(attn_all, give, send)
+    wout_grad = contract_rows(attn_all, g_all, True, factor, 256)
     return (input_grad, attn_grad, wqkv_grad, wout_grad)
 
 

time: 194 us -> 178 us (0.918)
  other arithmetic: 22.7 us -> 14.2 us
  local copies, waits for them, and re-layouts: 6.61 us -> 14.4 us
  starting transfers between devices: 50.6 us -> 43.4 us
  waiting for transfers between devices: 45.5 us -> 38.4 us
    ppermute x5 -> x3, waiting for transfers between devices: 14.2 us -> 1.04 us  [over_yh(): return lax.ppermute(value, 'dp', [(d, d ^ 1) for d in range(16)])]
    unnamed x26 -> x32, local copies, waits for them, and re-layouts: 2.07 us -> 10.3 us
    ppermute x5 -> x3, starting transfers between devices: 13.1 us -> 6.57 us  [over_yh(): return lax.ppermute(value, 'dp', [(d, d ^ 1) for d in range(16)])]
    ppermute x1, waiting for transfers between devices: 0.01 us -> 6.48 us  [over_yl(): return lax.ppermute(value, 'tensor', [(t, t ^ 2) for t in range(16)])]
    ppermute x3, waiting for transfers between devices: 13.3 us -> 7.39 us  [over_x(): return lax.ppermute(value, 'tensor', pairs)]
    ppermute x19, waiting for transfers between devices: 16.7 us -> 22.1 us  [over_z(): return lax.ppermute(value, 'dp', pairs)]
    convert_element_type x1 -> x0, other arithmetic: 4.59 us -> none  [shards(): (kept.astype(jnp.float32) + sent.astype(jnp.float32)).astype(jnp.bfloat16)]
    pallas_call x2, Pallas kernels: 10.6 us -> 7 us  [the longest x1 5.38 us: chip_parts(): pl.pallas_call(body, out_shape=(jax.ShapeDtypeStruct((2 * TB, n), jnp.bfl...]
  transfers between devices with their start and end apart: 31 -> 30, of which waited for: 8 -> 10; matrix products, arithmetic and copies ran while one was open for 16% -> 13% of each run, Pallas kernels for 25% -> 26%
where the time goes in v2:
time: 178 us; the launch traced here: 177 us
  Pallas kernels  46.6 us (26%)
  starting transfers between devices  43.4 us (24%)
  waiting for transfers between devices  38.4 us (22%)
  local copies, waits for them, and re-layouts  14.4 us (8%)
  other arithmetic  14.2 us (8%)
  between operations  13.9 us (8%)
  matrix products  5.71 us (3%)
    ppermute x19, starting transfers between devices, over_z(): return lax.ppermute(value, 'dp', pairs)  31 us
    pallas_call x5, Pallas kernels, absorb(): pl.pallas_call(body, out_shape=tuple(out_shape), grid_spec=pltpu.Prefetch...  25.1 us
    ppermute x19, waiting for transfers between devices, over_z(): return lax.ppermute(value, 'dp', pairs)  22.1 us
    pallas_call x2, Pallas kernels, contract_rows(): pl.pallas_call(body, out_shape=jax.ShapeDtypeStruct((m, n), jnp.float32),...  11.7 us
    unnamed x32, local copies, waits for them, and re-layouts  10.3 us
    ppermute x3, waiting for transfers between devices, over_x(): return lax.ppermute(value, 'tensor', pairs)  7.39 us
    ppermute x3, starting transfers between devices, over_yh(): return lax.ppermute(value, 'dp', [(d, d ^ 1) for d in range(16)])  6.57 us
    ppermute x1, waiting for transfers between devices, over_yl(): return lax.ppermute(value, 'tensor', [(t, t ^ 2) for t in range(16)])  6.48 us
  transfers between devices with their start and end apart: 30, of which 10 were waited for; matrix products, arithmetic and copies ran while one was open for 13% of the time, Pallas kernels for 26%

profile of v2, /device:TPU:2, one launch (start us, length us, event | category | flops | bytes accessed | tf_op | source)
XLA Modules:
  0.0 176.8 jit_solution(8912889091325180463)
XLA Ops:
  8.7 3.3 %collective-permute-start.1 = (s32[1,128]{1,0:T(1,128)}, s32[1,128]{1,0:T(1,128)S(1)}, u32[]{:S(2)}, u32[]{:S(2)}) collective-permute-start(s32[1,128]{1,0:T(1,128)} %bitcast.31), channel_id=1, source_target_pairs={{0,16},{16,0},{32,48},{48,32},{64,80},{80,64},{96,112},{112,96},{1... | collective-permute-start | bytes 1544 | tf_op jit(solution)/shard_map/ppermute | solution.py:26
  16.6 3.3 %collective-permute-start.3 = (s32[2,128]{1,0:T(2,128)S(1)}, s32[2,128]{1,0:T(2,128)S(1)}, u32[]{:S(2)}, u32[]{:S(2)}) collective-permute-start(s32[2,128]{1,0:T(2,128)S(1)} %add_select_fusion), channel_id=1, source_target_pairs={{0,64},{16,80},{32,96},{48,112},{64,128},{80,144},{96,160},{112,17... | collective-permute-start | bytes 3080 | tf_op jit(solution)/shard_map/ppermute | solution.py:22
  19.9 3.1 %collective-permute-start.5 = (bf16[128,768]{1,0:T(8,128)(2,1)}, bf16[128,768]{1,0:T(8,128)(2,1)S(1)}, u32[]{:S(2)}, u32[]{:S(2)}) collective-permute-start(bf16[128,768]{1,0:T(8,128)(2,1)} %block_ref.1), channel_id=1, source_target_pairs={{0,32},{16,48},{32,64},{48,80},{64,96},{80,112},{96,128},{112,144}... | collective-permute-start | bytes 589832 | tf_op jit(solution)/shard_map/ppermute | solution.py:22
  26.3 3.0 %collective-permute-done.4 = s32[4,128]{1,0:T(4,128)S(1)} collective-permute-done((s32[4,128]{1,0:T(4,128)S(1)}, s32[4,128]{1,0:T(4,128)S(1)}, u32[]{:S(2)}, u32[]{:S(2)}) %collective-permute-start.4) | collective-permute-done | bytes 2080 | tf_op jit(solution)/shard_map/ppermute | solution.py:22
  31.8 2.8 %shard_map.102 = (bf16[128,2560]{1,0:T(8,128)(2,1)}, bf16[128,2560]{1,0:T(8,128)(2,1)}) custom-call(s32[2]{0:T(128)} %pad_add_fusion.3.where_ref, bf16[128,896]{1,0:T(8,128)(2,1)} %own_ref.1, bf16[128,896]{1,0:T(8,128)(2,1)} %copy-done.13, f32[256,128]{1,0:T(8,128)} %get-tuple-element.119.cos_ref, f32[256,128]{1,0:T(8,128)} %get-tuple-element.118.sin_ref, ...), custom_call_target="tpu_custom_call" | custom-call | flops 2293760 | bytes 1835008 | tf_op jit(solution)/shard_map/pallas_call | solution.py:83
  37.8 11.2 %collective-permute-done.7.refs_0_ = bf16[128,2560]{1,0:T(8,128)(2,1)S(1)} collective-permute-done((bf16[128,2560]{1,0:T(8,128)(2,1)}, bf16[128,2560]{1,0:T(8,128)(2,1)S(1)}, u32[]{:S(2)}, u32[]{:S(2)}) %collective-permute-start.7) | collective-permute-done | bytes 655392 | tf_op jit(solution)/shard_map/ppermute | solution.py:22
  56.4 5.2 %shard_map.104 = (bf16[2,8,128,896]{3,2,1,0:T(8,128)(2,1)}, bf16[8,128,1024]{2,1,0:T(8,128)(2,1)}, bf16[8,128,1024]{2,1,0:T(8,128)(2,1)}, bf16[8,128,768]{2,1,0:T(8,128)(2,1)}) custom-call(s32[5]{0:T(128)} %stack.96.where_ref, bf16[128,2560]{1,0:T(8,128)(2,1)} %get-tuple-element.60.refs_0_, ...), custom_call_target="tpu_custom_call", output_to_operand_aliasing={{3}: (4, {})} | custom-call | flops 939524096 | bytes 5505024 | tf_op jit(solution)/shard_map/pallas_call | solution.py:149
  61.7 5.3 %shard_map.105 = (bf16[2,8,128,896]{3,2,1,0:T(8,128)(2,1)}, bf16[8,128,1024]{2,1,0:T(8,128)(2,1)}, bf16[8,128,1024]{2,1,0:T(8,128)(2,1)}, bf16[8,128,768]{2,1,0:T(8,128)(2,1)}) custom-call(s32[5]{0:T(128)} %stack.94.where_ref, bf16[128,2560]{1,0:T(8,128)(2,1)} %copy-done.10, ...), custom_call_target="tpu_custom_call", output_to_operand_aliasing={{0}: (4, {}), {1}: (5, {}), {2}: (6, {}), {3}: (7, {})} | custom-call | flops 939524096 | bytes 5505024 | tf_op jit(solution)/shard_map/pallas_call | solution.py:149
  67.5 2.9 %collective-permute-start.12 = (bf16[128,2560]{1,0:T(8,128)(2,1)S(1)}, bf16[128,2560]{1,0:T(8,128)(2,1)}, u32[]{:S(2)}, u32[]{:S(2)}) collective-permute-start(bf16[128,2560]{1,0:T(8,128)(2,1)S(1)} %collective-permute-done.10.refs_1_), channel_id=1, source_target_pairs={{0,224},{16,240},{32,0},{48,16},{64,32},{80,48},{96,64},{112,80},{... | collective-permute-start | bytes 1966088 | tf_op jit(solution)/shard_map/ppermute | solution.py:22
  70.4 5.3 %shard_map.106 = (bf16[2,8,128,896]{3,2,1,0:T(8,128)(2,1)}, bf16[8,128,1024]{2,1,0:T(8,128)(2,1)}, bf16[8,128,1024]{2,1,0:T(8,128)(2,1)}, bf16[8,128,768]{2,1,0:T(8,128)(2,1)}) custom-call(s32[5]{0:T(128)} %stack.99.where_ref, bf16[128,2560]{1,0:T(8,128)(2,1)} %copy-done.9, ...), custom_call_target="tpu_custom_call", output_to_operand_aliasing={{0}: (4, {}), {1}: (5, {}), {2}: (6, {}), {3}: (7, {})} | custom-call | flops 939524096 | bytes 5505024 | tf_op jit(solution)/shard_map/pallas_call | solution.py:149
  75.8 5.7 %convolution_convert_fusion = bf16[2048,768]{1,0:T(8,128)(2,1)S(1)} fusion(bf16[2048,1024]{1,0:T(8,128)(2,1)} %all-gather.4.cloned.1.call-done, bf16[768,1024]{1,0:T(8,128)(2,1)S(1)} %copy-done), kind=kOutput, calls=%fused_computation | convolution fusion | flops 3222798336 | bytes 8912896 | tf_op jit(solution)/shard_map/dot_general | solution.py:222
  87.1 5.3 %shard_map.107 = (bf16[2,8,128,896]{3,2,1,0:T(8,128)(2,1)}, bf16[8,128,1024]{2,1,0:T(8,128)(2,1)}, bf16[8,128,1024]{2,1,0:T(8,128)(2,1)}, bf16[8,128,768]{2,1,0:T(8,128)(2,1)}) custom-call(s32[5]{0:T(128)} %stack.100.where_ref, bf16[128,2560]{1,0:T(8,128)(2,1)} %copy-done.6, ...), custom_call_target="tpu_custom_call", output_to_operand_aliasing={{0}: (4, {}), {1}: (5, {}), {2}: (6, {}), {3}: (7, {})} | custom-call | flops 939524096 | bytes 5505024 | tf_op jit(solution)/shard_map/pallas_call | solution.py:149
  93.2 4.0 %shard_map.108 = (bf16[2,8,128,896]{3,2,1,0:T(8,128)(2,1)}, bf16[8,128,1024]{2,1,0:T(8,128)(2,1)}, bf16[8,128,1024]{2,1,0:T(8,128)(2,1)}) custom-call(s32[2]{0:T(128)} %pad_add_fusion.2.where_ref, bf16[128,1792]{1,0:T(8,128)(2,1)} %copy-done.12, bf16[1024,896]{1,0:T(8,128)(2,1)} %refs_1_.1, ...), custom_call_target="tpu_custom_call", output_to_operand_aliasing={{0}: (3, {}), {1}: (4, {}), {2}: (5, {})} | custom-call | flops 469762048 | bytes 3276800 | tf_op jit(solution)/shard_map/pallas_call | solution.py:149
  102.4 5.4 %shard_map.109 = (bf16[256,1024]{1,0:T(8,128)(2,1)}, bf16[256,1024]{1,0:T(8,128)(2,1)}, bf16[256,1024]{1,0:T(8,128)(2,1)}, bf16[256,1024]{1,0:T(8,128)(2,1)}) custom-call(s32[4]{0:T(128)} %pad_add_fusion.1.where_ref, bf16[8,128,1024]{2,1,0:T(8,128)(2,1)} %get-tuple-element.97.kept_ref, bf16[8,128,1024]{2,1,0:T(8,128)(2,1)} %collective-permute-done.15.sent_ref), custom_call_target="tpu_custom_call" | custom-call | flops 1048576 | bytes 6291456 | tf_op jit(solution)/shard_map/pallas_call | solution.py:208
  107.8 2.2 %collective-permute-done.19 = bf16[256,768]{1,0:T(8,128)(2,1)S(1)} collective-permute-done((bf16[256,768]{1,0:T(8,128)(2,1)S(1)}, bf16[256,768]{1,0:T(8,128)(2,1)S(1)}, u32[]{:S(2)}, u32[]{:S(2)}) %collective-permute-start.19) | collective-permute-done | bytes 393248 | tf_op jit(solution)/shard_map/ppermute | solution.py:22
  112.7 3.0 %collective-permute-start.22 = (bf16[256,768]{1,0:T(8,128)(2,1)S(1)}, bf16[256,768]{1,0:T(8,128)(2,1)S(1)}, u32[]{:S(2)}, u32[]{:S(2)}) collective-permute-start(bf16[256,768]{1,0:T(8,128)(2,1)S(1)} %add_convert_fusion.3), channel_id=1, source_target_pairs={{0,32},{16,48},{32,64},{48,80},{64,96},{80,112},{96,128},{112,144}... | collective-permute-start | bytes 1179656 | tf_op jit(solution)/shard_map/ppermute | solution.py:22
  117.7 2.2 %collective-permute-start.18 = (bf16[256,1024]{1,0:T(8,128)(2,1)}, bf16[256,1024]{1,0:T(8,128)(2,1)S(1)}, u32[]{:S(2)}, u32[]{:S(2)}) collective-permute-start(bf16[256,1024]{1,0:T(8,128)(2,1)} %get-tuple-element.102), channel_id=1, source_target_pairs={{0,8},{1,9},{2,10},{3,11},{4,12},{5,13},{6,14},{7,15},{8,0},{9,1},... | collective-permute-start | bytes 1572872 | tf_op jit(solution)/shard_map/ppermute | solution.py:31
  121.9 2.2 %copy-done.3 = bf16[2048,1024]{1,0:T(8,128)(2,1)S(1)} copy-done((bf16[2048,1024]{1,0:T(8,128)(2,1)S(1)}, bf16[2048,1024]{1,0:T(8,128)(2,1)}, u32[]{:S(2)}) %copy-start.3) | copy-done | bytes 4194328
  124.1 6.7 %shard_map.110 = f32[1024,896]{1,0:T(8,128)} custom-call(bf16[2,1024,896]{2,1,0:T(8,128)(2,1)S(1)} %bitcast.27, bf16[8,2,128,1024]{3,2,1,0:T(8,128)(2,1)S(1)} %bitcast.29), custom_call_target="tpu_custom_call" | custom-call | flops 3758096384 | bytes 11534336 | tf_op jit(solution)/shard_map/pallas_call | solution.py:179
  134.9 7.4 %collective-permute-done.18 = bf16[256,1024]{1,0:T(8,128)(2,1)S(1)} collective-permute-done((bf16[256,1024]{1,0:T(8,128)(2,1)}, bf16[256,1024]{1,0:T(8,128)(2,1)S(1)}, u32[]{:S(2)}, u32[]{:S(2)}) %collective-permute-start.18) | collective-permute-done | bytes 524320 | tf_op jit(solution)/shard_map/ppermute | solution.py:31
  147.2 6.5 %collective-permute-done.21 = bf16[128,1024]{1,0:T(8,128)(2,1)S(1)} collective-permute-done((bf16[128,1024]{1,0:T(8,128)(2,1)}, bf16[128,1024]{1,0:T(8,128)(2,1)S(1)}, u32[]{:S(2)}, u32[]{:S(2)}) %collective-permute-start.21) | collective-permute-done | bytes 262176 | tf_op jit(solution)/shard_map/ppermute | solution.py:35
  157.5 3.0 %collective-permute-start.26 = (bf16[128,768]{1,0:T(8,128)(2,1)S(1)}, bf16[128,768]{1,0:T(8,128)(2,1)S(1)}, u32[]{:S(2)}, u32[]{:S(2)}) collective-permute-start(bf16[128,768]{1,0:T(8,128)(2,1)S(1)} %dynamic-slice_convert_fusion.1), channel_id=1, source_target_pairs={{0,16},{16,0},{32,48},{48,32},{64,80},{80,64},{96,112},{112,96},{1... | collective-permute-start | bytes 589832 | tf_op jit(solution)/shard_map/ppermute | solution.py:26
  160.5 2.2 %copy-done.2 = bf16[2048,1024]{1,0:T(8,128)(2,1)S(1)} copy-done((bf16[2048,1024]{1,0:T(8,128)(2,1)S(1)}, bf16[2048,1024]{1,0:T(8,128)(2,1)}, u32[]{:S(2)}) %copy-start.2) | copy-done | bytes 4194328
  164.5 5.0 %shard_map.111 = f32[768,1024]{1,0:T(8,128)} custom-call(bf16[2,1024,768]{2,1,0:T(8,128)(2,1)S(1)} %copy-done.4, bf16[8,2,128,1024]{3,2,1,0:T(8,128)(2,1)S(1)} %bitcast.28), custom_call_target="tpu_custom_call" | custom-call | flops 3221225472 | bytes 10485760 | tf_op jit(solution)/shard_map/pallas_call | solution.py:179
  (109 shorter events, 56.7 us)
Async XLA Ops:
  7.2 68.6 %all-gather.4.cloned.1.call-start = ((), (), s32[]{:S(2)}) async-start(), calls=%async_computation | async-start | bytes 4456448 | tf_op jit(solution)/shard_map/all_gather | solution.py:257
  7.9 99.9 %all-gather.6.cloned.1.call-start = ((), (), s32[]{:S(2)}) async-start(), calls=%async_computation.1 | async-start | bytes 4456448 | tf_op jit(solution)/shard_map/all_gather | solution.py:258
  8.7 151.8 %all-gather.8.cloned.1.call-start = ((), (), s32[]{:S(2)}) async-start(), calls=%async_computation.2 | async-start | bytes 4718592 | tf_op jit(solution)/shard_map/all_gather | solution.py:288
  12.0 19.0 %collective-permute-start = (bf16[128,896]{1,0:T(8,128)(2,1)}, bf16[128,896]{1,0:T(8,128)(2,1)S(1)}, u32[]{:S(2)}, u32[]{:S(2)}) collective-permute-start(bf16[128,896]{1,0:T(8,128)(2,1)} %own_ref.1), channel_id=1, source_target_pairs={{0,16},{16,0},{32,48},{48,32},{64,80},{80,64},{96,112},{112,96},{1... | collective-permute-start | bytes 688136 | tf_op jit(solution)/shard_map/ppermute | solution.py:26
  19.9 11.0 %collective-permute-start.5 = (bf16[128,768]{1,0:T(8,128)(2,1)}, bf16[128,768]{1,0:T(8,128)(2,1)S(1)}, u32[]{:S(2)}, u32[]{:S(2)}) collective-permute-start(bf16[128,768]{1,0:T(8,128)(2,1)} %block_ref.1), channel_id=1, source_target_pairs={{0,32},{16,48},{32,64},{48,80},{64,96},{80,112},{96,128},{112,144}... | collective-permute-start | bytes 589832 | tf_op jit(solution)/shard_map/ppermute | solution.py:22
  34.6 14.4 %collective-permute-start.7 = (bf16[128,2560]{1,0:T(8,128)(2,1)}, bf16[128,2560]{1,0:T(8,128)(2,1)S(1)}, u32[]{:S(2)}, u32[]{:S(2)}) collective-permute-start(bf16[128,2560]{1,0:T(8,128)(2,1)} %get-tuple-element.60.refs_0_), channel_id=1, source_target_pairs={{0,32},{16,48},{32,64},{48,80},{64,96},{80,112},{96,128},{112,144}... | collective-permute-start | bytes 1966088 | tf_op jit(solution)/shard_map/ppermute | solution.py:22
  36.0 14.8 %collective-permute-start.8 = (bf16[128,2560]{1,0:T(8,128)(2,1)}, bf16[128,2560]{1,0:T(8,128)(2,1)}, u32[]{:S(2)}, u32[]{:S(2)}) collective-permute-start(bf16[128,2560]{1,0:T(8,128)(2,1)} %get-tuple-element.61.refs_1_), channel_id=1, source_target_pairs={{0,224},{16,240},{32,0},{48,16},{64,32},{80,48},{96,64},{112,80},{... | collective-permute-start | bytes 1966088 | tf_op jit(solution)/shard_map/ppermute | solution.py:22
  50.9 16.1 %collective-permute-start.10 = (bf16[128,2560]{1,0:T(8,128)(2,1)}, bf16[128,2560]{1,0:T(8,128)(2,1)S(1)}, u32[]{:S(2)}, u32[]{:S(2)}) collective-permute-start(bf16[128,2560]{1,0:T(8,128)(2,1)} %collective-permute-done.8.refs_1_), channel_id=1, source_target_pairs={{0,224},{16,240},{32,0},{48,16},{64,32},{80,48},{96,64},{112,80},{... | collective-permute-start | bytes 1966088 | tf_op jit(solution)/shard_map/ppermute | solution.py:22
  52.7 14.2 %collective-permute-start.9 = (bf16[128,2560]{1,0:T(8,128)(2,1)S(1)}, bf16[128,2560]{1,0:T(8,128)(2,1)S(1)}, u32[]{:S(2)}, u32[]{:S(2)}) collective-permute-start(bf16[128,2560]{1,0:T(8,128)(2,1)S(1)} %collective-permute-done.7.refs_0_), channel_id=1, source_target_pairs={{0,32},{16,48},{32,64},{48,80},{64,96},{80,112},{96,128},{112,144}... | collective-permute-start | bytes 1966088 | tf_op jit(solution)/shard_map/ppermute | solution.py:22
  66.9 14.5 %collective-permute-start.11 = (bf16[128,2560]{1,0:T(8,128)(2,1)S(1)}, bf16[128,2560]{1,0:T(8,128)(2,1)S(1)}, u32[]{:S(2)}, u32[]{:S(2)}) collective-permute-start(bf16[128,2560]{1,0:T(8,128)(2,1)S(1)} %collective-permute-done.9.refs_0_), channel_id=1, source_target_pairs={{0,32},{16,48},{32,64},{48,80},{64,96},{80,112},{96,128},{112,144}... | collective-permute-start | bytes 1966088 | tf_op jit(solution)/shard_map/ppermute | solution.py:22
  67.5 14.0 %collective-permute-start.12 = (bf16[128,2560]{1,0:T(8,128)(2,1)S(1)}, bf16[128,2560]{1,0:T(8,128)(2,1)}, u32[]{:S(2)}, u32[]{:S(2)}) collective-permute-start(bf16[128,2560]{1,0:T(8,128)(2,1)S(1)} %collective-permute-done.10.refs_1_), channel_id=1, source_target_pairs={{0,224},{16,240},{32,0},{48,16},{64,32},{80,48},{96,64},{112,80},{... | collective-permute-start | bytes 1966088 | tf_op jit(solution)/shard_map/ppermute | solution.py:22
  81.6 10.8 %collective-permute-start.13 = (bf16[128,1792]{1,0:T(8,128)(2,1)S(1)}, bf16[128,1792]{1,0:T(8,128)(2,1)S(1)}, u32[]{:S(2)}, u32[]{:S(2)}) collective-permute-start(bf16[128,1792]{1,0:T(8,128)(2,1)S(1)} %slice.3), channel_id=1, source_target_pairs={{0,32},{16,48},{32,64},{48,80},{64,96},{80,112},{96,128},{112,144}... | collective-permute-start | bytes 1376264 | tf_op jit(solution)/shard_map/ppermute | solution.py:22
  83.9 8.4 %collective-permute-start.14 = (bf16[256,768]{1,0:T(8,128)(2,1)}, bf16[256,768]{1,0:T(8,128)(2,1)}, u32[]{:S(2)}, u32[]{:S(2)}) collective-permute-start(bf16[256,768]{1,0:T(8,128)(2,1)} %get-tuple-element.117), channel_id=1, source_target_pairs={{0,224},{16,240},{32,0},{48,16},{64,32},{80,48},{96,64},{112,80},{... | collective-permute-start | bytes 1179656 | tf_op jit(solution)/shard_map/ppermute | solution.py:22
  97.2 12.8 %collective-permute-start.19 = (bf16[256,768]{1,0:T(8,128)(2,1)S(1)}, bf16[256,768]{1,0:T(8,128)(2,1)S(1)}, u32[]{:S(2)}, u32[]{:S(2)}) collective-permute-start(bf16[256,768]{1,0:T(8,128)(2,1)S(1)} %get-tuple-element.116), channel_id=1, source_target_pairs={{0,32},{16,48},{32,64},{48,80},{64,96},{80,112},{96,128},{112,144}... | collective-permute-start | bytes 1179656 | tf_op jit(solution)/shard_map/ppermute | solution.py:22
  100.0 11.6 %collective-permute-start.20 = (bf16[256,768]{1,0:T(8,128)(2,1)S(1)}, bf16[256,768]{1,0:T(8,128)(2,1)S(1)}, u32[]{:S(2)}, u32[]{:S(2)}) collective-permute-start(bf16[256,768]{1,0:T(8,128)(2,1)S(1)} %add_convert_fusion.4), channel_id=1, source_target_pairs={{0,224},{16,240},{32,0},{48,16},{64,32},{80,48},{96,64},{112,80},{... | collective-permute-start | bytes 1179656 | tf_op jit(solution)/shard_map/ppermute | solution.py:22
  112.7 18.1 %collective-permute-start.22 = (bf16[256,768]{1,0:T(8,128)(2,1)S(1)}, bf16[256,768]{1,0:T(8,128)(2,1)S(1)}, u32[]{:S(2)}, u32[]{:S(2)}) collective-permute-start(bf16[256,768]{1,0:T(8,128)(2,1)S(1)} %add_convert_fusion.3), channel_id=1, source_target_pairs={{0,32},{16,48},{32,64},{48,80},{64,96},{80,112},{96,128},{112,144}... | collective-permute-start | bytes 1179656 | tf_op jit(solution)/shard_map/ppermute | solution.py:22
  115.7 19.2 %collective-permute-start.16 = (bf16[256,1024]{1,0:T(8,128)(2,1)}, bf16[256,1024]{1,0:T(8,128)(2,1)S(1)}, u32[]{:S(2)}, u32[]{:S(2)}) collective-permute-start(bf16[256,1024]{1,0:T(8,128)(2,1)} %get-tuple-element.100), channel_id=1, source_target_pairs={{0,4},{1,5},{2,6},{3,7},{4,8},{5,9},{6,10},{7,11},{8,12},{9,13},{1... | collective-permute-start | bytes 1572872 | tf_op jit(solution)/shard_map/ppermute | solution.py:31
  117.2 17.7 %collective-permute-start.17 = (bf16[256,1024]{1,0:T(8,128)(2,1)}, bf16[256,1024]{1,0:T(8,128)(2,1)S(1)}, u32[]{:S(2)}, u32[]{:S(2)}) collective-permute-start(bf16[256,1024]{1,0:T(8,128)(2,1)} %get-tuple-element.101), channel_id=1, source_target_pairs={{0,12},{1,13},{2,14},{3,15},{4,0},{5,1},{6,2},{7,3},{8,4},{9,5},{1... | collective-permute-start | bytes 1572872 | tf_op jit(solution)/shard_map/ppermute | solution.py:31
  117.7 24.6 %collective-permute-start.18 = (bf16[256,1024]{1,0:T(8,128)(2,1)}, bf16[256,1024]{1,0:T(8,128)(2,1)S(1)}, u32[]{:S(2)}, u32[]{:S(2)}) collective-permute-start(bf16[256,1024]{1,0:T(8,128)(2,1)} %get-tuple-element.102), channel_id=1, source_target_pairs={{0,8},{1,9},{2,10},{3,11},{4,12},{5,13},{6,14},{7,15},{8,0},{9,1},... | collective-permute-start | bytes 1572872 | tf_op jit(solution)/shard_map/ppermute | solution.py:31
  132.9 12.1 %collective-permute-start.24 = (bf16[256,768]{1,0:T(8,128)(2,1)S(1)}, bf16[256,768]{1,0:T(8,128)(2,1)S(1)}, u32[]{:S(2)}, u32[]{:S(2)}) collective-permute-start(bf16[256,768]{1,0:T(8,128)(2,1)S(1)} %get-tuple-element.115), channel_id=1, source_target_pairs={{0,224},{16,240},{32,0},{48,16},{64,32},{80,48},{96,64},{112,80},{... | collective-permute-start | bytes 1179656 | tf_op jit(solution)/shard_map/ppermute | solution.py:22
  133.4 21.2 %collective-permute-start.23 = (bf16[256,768]{1,0:T(8,128)(2,1)}, bf16[256,768]{1,0:T(8,128)(2,1)S(1)}, u32[]{:S(2)}, u32[]{:S(2)}) collective-permute-start(bf16[256,768]{1,0:T(8,128)(2,1)} %get-tuple-element.114), channel_id=1, source_target_pairs={{0,32},{16,48},{32,64},{48,80},{64,96},{80,112},{96,128},{112,144}... | collective-permute-start | bytes 1179656 | tf_op jit(solution)/shard_map/ppermute | solution.py:22
  143.4 10.4 %collective-permute-start.21 = (bf16[128,1024]{1,0:T(8,128)(2,1)}, bf16[128,1024]{1,0:T(8,128)(2,1)S(1)}, u32[]{:S(2)}, u32[]{:S(2)}) collective-permute-start(bf16[128,1024]{1,0:T(8,128)(2,1)} %dynamic-slice_convert_fusion), channel_id=1, source_target_pairs={{0,2},{1,3},{2,0},{3,1},{4,6},{5,7},{6,4},{7,5},{8,10},{9,11},{10,... | collective-permute-start | bytes 786440 | tf_op jit(solution)/shard_map/ppermute | solution.py:35
  146.8 9.4 %collective-permute-start.25 = (bf16[256,768]{1,0:T(8,128)(2,1)}, bf16[256,768]{1,0:T(8,128)(2,1)}, u32[]{:S(2)}, u32[]{:S(2)}) collective-permute-start(bf16[256,768]{1,0:T(8,128)(2,1)} %add_convert_fusion), channel_id=1, source_target_pairs={{0,224},{16,240},{32,0},{48,16},{64,32},{80,48},{96,64},{112,80},{... | collective-permute-start | bytes 1179656 | tf_op jit(solution)/shard_map/ppermute | solution.py:22
  157.5 12.1 %collective-permute-start.26 = (bf16[128,768]{1,0:T(8,128)(2,1)S(1)}, bf16[128,768]{1,0:T(8,128)(2,1)S(1)}, u32[]{:S(2)}, u32[]{:S(2)}) collective-permute-start(bf16[128,768]{1,0:T(8,128)(2,1)S(1)} %dynamic-slice_convert_fusion.1), channel_id=1, source_target_pairs={{0,16},{16,0},{32,48},{48,32},{64,80},{80,64},{96,112},{112,96},{1... | collective-permute-start | bytes 589832 | tf_op jit(solution)/shard_map/ppermute | solution.py:26
  (22 other events, 178.3 us)
Sparse Core Ops, SparseCore 0:
  9.9 42.6 all-gather.3
  54.4 39.8 all-gather.5
  97.3 54.5 all-gather.7

commit v3 on v2

--- a/solution.py
+++ b/solution.py
@@ -162,36 +162,6 @@
     )(where, *operands)
 
 
-def contract_rows(halves, both, halves_left, factor, tile):
-    a, b = halves.shape[2], both.shape[1]
-    m, n = (a, b) if halves_left else (b, a)
-    half_tile, both_tile = (tile, b) if halves_left else (a, tile)
-    moving = (lambda i: (0, 0, i), lambda i: (0, 0, 0, 0)) if halves_left else (lambda i: (0, 0, 0), lambda i: (0, 0, 0, i))
-
-    def body(halves_ref, both_ref, out_ref):
-        total = jnp.zeros(out_ref.shape, jnp.float32)
-        for h in range(2):
-            tokens = both_ref[:, h].reshape(NZ * TB, both_tile)
-            pair = (halves_ref[h], tokens) if halves_left else (tokens, halves_ref[h])
-            total += lax.dot_general(*pair, (((0,), (0,)), ((), ())), preferred_element_type=jnp.float32)
-        out_ref[...] = total * factor
-
-    return pl.pallas_call(
-        body,
-        out_shape=jax.ShapeDtypeStruct((m, n), jnp.float32),
-        grid=(m // tile,),
-        in_specs=[
-            pl.BlockSpec((2, NZ * TB, half_tile), moving[0]),
-            pl.BlockSpec((NZ, 2, TB, both_tile), moving[1]),
-        ],
-        out_specs=pl.BlockSpec((tile, n), lambda i: (i, 0)),
-        compiler_params=pltpu.CompilerParams(vmem_limit_bytes=40 * 2**20),
-        cost_estimate=pl.CostEstimate(
-            flops=4 * NZ * TB * m * n, bytes_accessed=4 * NZ * TB * (m + n) + 4 * m * n, transcendentals=0
-        ),
-    )(halves, both.reshape(NZ, 2, TB, b))
-
-
 def chip_parts(kept, sent, targets):
     n = kept.shape[2]
     count = len(targets)
@@ -216,6 +186,42 @@
         ),
         cost_estimate=pl.CostEstimate(flops=NZ * TB * n, bytes_accessed=6 * NZ * TB * n, transcendentals=0),
     )(jnp.stack(targets).astype(jnp.int32), kept, sent)
+
+
+def contract_rows(halves, first, both, halves_left, factor, tile):
+    a, b = halves[0].shape[2], both.shape[1]
+    m, n = (a, b) if halves_left else (b, a)
+    half_tile, both_tile = (tile, b) if halves_left else (a, tile)
+    if halves_left:
+        moving = (lambda i, s: (0, 0, i), lambda i, s: (0, 0, 0, 0))
+    else:
+        moving = (lambda i, s: (0, 0, 0), lambda i, s: (0, 0, 0, i))
+
+    def body(first_ref, *refs):
+        both_ref, out_ref = refs[-2:]
+        total = jnp.zeros(out_ref.shape, jnp.float32)
+        parts = [ref[k] for ref in refs[:-2] for k in range(ref.shape[0])]
+        for part, h in zip(parts, (first_ref[0], 1 - first_ref[0])):
+            tokens = both_ref[:, h].reshape(NZ * TB, both_tile)
+            pair = (part, tokens) if halves_left else (tokens, part)
+            total += lax.dot_general(*pair, (((0,), (0,)), ((), ())), preferred_element_type=jnp.float32)
+        out_ref[...] = total * factor
+
+    return pl.pallas_call(
+        body,
+        out_shape=jax.ShapeDtypeStruct((m, n), jnp.float32),
+        grid_spec=pltpu.PrefetchScalarGridSpec(
+            num_scalar_prefetch=1,
+            grid=(m // tile,),
+            in_specs=[pl.BlockSpec((v.shape[0], NZ * TB, half_tile), moving[0]) for v in halves]
+            + [pl.BlockSpec((NZ, 2, TB, both_tile), moving[1])],
+            out_specs=pl.BlockSpec((tile, n), lambda i, s: (i, 0)),
+        ),
+        compiler_params=pltpu.CompilerParams(vmem_limit_bytes=40 * 2**20),
+        cost_estimate=pl.CostEstimate(
+            flops=4 * NZ * TB * m * n, bytes_accessed=4 * NZ * TB * (m + n) + 4 * m * n, transcendentals=0
+        ),
+    )(jnp.reshape(first, (1,)).astype(jnp.int32), *halves, both.reshape(NZ, 2, TB, b))
 
 
 def contract_cols(left, right):
@@ -285,36 +291,38 @@
     last = over_z(up3[:, : 2 * qkv_grad.shape[1]], 1)
     *shares, attn_all = absorb([up3, down3], [-3, 3], [4, 4], z, core, w_qkv, [*shares, attn_all])
     last, fold.down, attn_all, *shares = tie(last, fold.down, attn_all, *shares)
-    attn_all = lax.all_gather(
-        attn_all.reshape(1, NZ * TB, -1), "dp", axis=0, tiled=True, axis_index_groups=[[d, d + 1] for d in range(0, 16, 2)]
-    )
     q_all, kept, given = absorb([last], [4], None, z, core, w_qkv, shares)
 
     q_all = q_all.reshape(2, NZ * TB, -1)
     sent = over_core(given)
+    attn_all = attn_all.reshape(1, NZ * TB, -1)
+    attn_other = over_yh(attn_all)
     fold.step()
-    steps = (1, -1, 2)
-    mine, *away = chip_parts(kept, sent, [(x + k + NX) % NX for k in (0, *steps)])
+    mine, ahead, behind, across = chip_parts(kept, sent, [(x + k) % NX for k in (0, 1, 3, 2)])
     fold.up, fold.down, x_all, _ = tie(fold.up, fold.down, x_all, mine)
     fold.step()
-    wqkv_grad = contract_rows(q_all, x_all, False, factor, 256)
-    *came, wqkv_grad = tie(*(over_x(part, k) for k, part in zip(steps, away)), wqkv_grad)
-    total = mine.astype(jnp.float32)
-    for part in came:
-        total = total + part.astype(jnp.float32)
+    a, b = over_x(across[:TB], 1), over_x(across[TB:], -1)
+    plus = lambda part, got: (part.astype(jnp.float32) + got.astype(jnp.float32)).astype(jnp.bfloat16)
+    ahead = jnp.concatenate([plus(ahead[:TB], a), ahead[TB:]])
+    behind = jnp.concatenate([behind[:TB], plus(behind[TB:], b)])
+    ahead, behind = tie(ahead, behind)
+    wqkv_grad = contract_rows([q_all], jnp.int32(0), x_all, False, factor, 256)
+    came1, came2 = over_x(ahead, 1), over_x(behind, -1)
+    total = mine.astype(jnp.float32) + came1.astype(jnp.float32) + came2.astype(jnp.float32)
     keep = lax.dynamic_slice_in_dim(total, yl * TB, TB, 0)
     give = lax.dynamic_slice_in_dim(total, (1 - yl) * TB, TB, 0).astype(jnp.bfloat16)
     summed = keep + over_yl(give).astype(jnp.float32)
     input_grad = (out_grad.astype(jnp.float32) + summed).astype(jnp.bfloat16)
 
+    fold.up, fold.down, attn_other, wqkv_grad, _ = tie(fold.up, fold.down, attn_other, wqkv_grad, ahead)
     fold.step()
+    wout_grad = contract_rows([attn_all, attn_other], yh, g_all, True, factor, 256)
+    fold.up, fold.down, wout_grad = tie(fold.up, fold.down, wout_grad)
     sums = fold.sums()
     keep = lax.dynamic_slice_in_dim(sums, yh * TB, TB, 0)
     send = lax.dynamic_slice_in_dim(sums, (1 - yh) * TB, TB, 0).astype(jnp.bfloat16)
     attn_grad = (keep + over_yh(send).astype(jnp.float32)).astype(jnp.bfloat16)
 
-    attn_all, _, _ = tie(attn_all, give, send)
-    wout_grad = contract_rows(attn_all, g_all, True, factor, 256)
     return (input_grad, attn_grad, wqkv_grad, wout_grad)
 
 

time: 178 us -> 182 us (1.022)
  waiting for transfers between devices: 38.4 us -> 34.4 us
  other arithmetic: 14.2 us -> 17.7 us
  starting transfers between devices: 43.4 us -> 46.9 us
    ppermute x3 -> x4, waiting for transfers between devices: 1.04 us -> 14.2 us  [over_yh(): return lax.ppermute(value, 'dp', [(d, d ^ 1) for d in range(16)])]
    ppermute x3 -> x4, waiting for transfers between devices: 7.39 us -> 0.01 us  [over_x(): return lax.ppermute(value, 'tensor', pairs)]
    ppermute x1, waiting for transfers between devices: 6.48 us -> 1.33 us  [over_yl(): return lax.ppermute(value, 'tensor', [(t, t ^ 2) for t in range(16)])]
    ppermute x19, waiting for transfers between devices: 22.1 us -> 17.4 us  [over_z(): return lax.ppermute(value, 'dp', pairs)]
    unnamed x32 -> x34, local copies, waits for them, and re-layouts: 10.3 us -> 6.45 us
    ppermute x3 -> x4, starting transfers between devices: 6.57 us -> 10.1 us  [over_yh(): return lax.ppermute(value, 'dp', [(d, d ^ 1) for d in range(16)])]
    slice x0 -> x3, local copies, waits for them, and re-layouts: none -> 2.05 us  [the longest x1 1.06 us: shards(): a, b = (over_x(across[:TB], 1), over_x(across[TB:], -1))]
    convert_element_type x4 -> x3, other arithmetic: 6.3 us -> 5.88 us  [add(): (part if got is None else part + got.astype(jnp.float32)).astype(jnp.bflo...]
  transfers between devices with their start and end apart: 30 -> 31, of which waited for: 10 -> 9; matrix products, arithmetic and copies ran while one was open for 13% -> 15% of each run, Pallas kernels for 26% -> 27%
where the time goes in v3:
time: 182 us; the launch traced here: 180 us
  Pallas kernels  47.8 us (26%)
  starting transfers between devices  46.9 us (26%)
  waiting for transfers between devices  34.4 us (19%)
  other arithmetic  17.7 us (10%)
  between operations  14.3 us (8%)
  local copies, waits for them, and re-layouts  13.3 us (7%)
  matrix products  5.72 us (3%)
    ppermute x19, starting transfers between devices, over_z(): return lax.ppermute(value, 'dp', pairs)  31.9 us
    pallas_call x5, Pallas kernels, absorb(): pl.pallas_call(body, out_shape=tuple(out_shape), grid_spec=pltpu.Prefetch...  25.3 us
    ppermute x19, waiting for transfers between devices, over_z(): return lax.ppermute(value, 'dp', pairs)  17.4 us
    ppermute x4, waiting for transfers between devices, over_yh(): return lax.ppermute(value, 'dp', [(d, d ^ 1) for d in range(16)])  14.2 us
    pallas_call x2, Pallas kernels, contract_rows(): pl.pallas_call(body, out_shape=jax.ShapeDtypeStruct((m, n), jnp.float32),...  12.7 us
    ppermute x4, starting transfers between devices, over_yh(): return lax.ppermute(value, 'dp', [(d, d ^ 1) for d in range(16)])  10.1 us
    unnamed x34, local copies, waits for them, and re-layouts  6.45 us
    convert_element_type x3, other arithmetic, add(): (part if got is None else part + got.astype(jnp.float32)).astype(jnp.bflo...  5.88 us
  transfers between devices with their start and end apart: 31, of which 9 were waited for; matrix products, arithmetic and copies ran while one was open for 15% of the time, Pallas kernels for 27%

profile of v3, /device:TPU:2, one launch (start us, length us, event | category | flops | bytes accessed | tf_op | source)
XLA Modules:
  0.0 180.0 jit_solution(13947036860205278472)
XLA Ops:
  8.7 3.3 %collective-permute-start.1 = (s32[1,128]{1,0:T(1,128)}, s32[1,128]{1,0:T(1,128)S(1)}, u32[]{:S(2)}, u32[]{:S(2)}) collective-permute-start(s32[1,128]{1,0:T(1,128)} %bitcast.32), channel_id=1, source_target_pairs={{0,16},{16,0},{32,48},{48,32},{64,80},{80,64},{96,112},{112,96},{1... | collective-permute-start | bytes 1544 | tf_op jit(solution)/shard_map/ppermute | solution.py:26
  16.6 3.3 %collective-permute-start.3 = (s32[2,128]{1,0:T(2,128)S(1)}, s32[2,128]{1,0:T(2,128)S(1)}, u32[]{:S(2)}, u32[]{:S(2)}) collective-permute-start(s32[2,128]{1,0:T(2,128)S(1)} %add_select_fusion), channel_id=1, source_target_pairs={{0,64},{16,80},{32,96},{48,112},{64,128},{80,144},{96,160},{112,17... | collective-permute-start | bytes 3080 | tf_op jit(solution)/shard_map/ppermute | solution.py:22
  19.9 3.1 %collective-permute-start.5 = (bf16[128,768]{1,0:T(8,128)(2,1)}, bf16[128,768]{1,0:T(8,128)(2,1)S(1)}, u32[]{:S(2)}, u32[]{:S(2)}) collective-permute-start(bf16[128,768]{1,0:T(8,128)(2,1)} %block_ref.1), channel_id=1, source_target_pairs={{0,32},{16,48},{32,64},{48,80},{64,96},{80,112},{96,128},{112,144}... | collective-permute-start | bytes 589832 | tf_op jit(solution)/shard_map/ppermute | solution.py:22
  26.3 3.0 %collective-permute-done.4 = s32[4,128]{1,0:T(4,128)S(1)} collective-permute-done((s32[4,128]{1,0:T(4,128)S(1)}, s32[4,128]{1,0:T(4,128)S(1)}, u32[]{:S(2)}, u32[]{:S(2)}) %collective-permute-start.4) | collective-permute-done | bytes 2080 | tf_op jit(solution)/shard_map/ppermute | solution.py:22
  31.7 2.8 %shard_map.102 = (bf16[128,2560]{1,0:T(8,128)(2,1)}, bf16[128,2560]{1,0:T(8,128)(2,1)}) custom-call(s32[2]{0:T(128)} %pad_add_fusion.3.where_ref, bf16[128,896]{1,0:T(8,128)(2,1)} %own_ref.1, bf16[128,896]{1,0:T(8,128)(2,1)} %copy-done.14, f32[256,128]{1,0:T(8,128)} %get-tuple-element.131.cos_ref, f32[256,128]{1,0:T(8,128)} %get-tuple-element.130.sin_ref, ...), custom_call_target="tpu_custom_call" | custom-call | flops 2293760 | bytes 1835008 | tf_op jit(solution)/shard_map/pallas_call | solution.py:83
  37.7 11.2 %collective-permute-done.7.refs_0_ = bf16[128,2560]{1,0:T(8,128)(2,1)S(1)} collective-permute-done((bf16[128,2560]{1,0:T(8,128)(2,1)}, bf16[128,2560]{1,0:T(8,128)(2,1)S(1)}, u32[]{:S(2)}, u32[]{:S(2)}) %collective-permute-start.7) | collective-permute-done | bytes 655392 | tf_op jit(solution)/shard_map/ppermute | solution.py:22
  56.4 5.3 %shard_map.104 = (bf16[2,8,128,896]{3,2,1,0:T(8,128)(2,1)}, bf16[8,128,1024]{2,1,0:T(8,128)(2,1)}, bf16[8,128,1024]{2,1,0:T(8,128)(2,1)}, bf16[8,128,768]{2,1,0:T(8,128)(2,1)}) custom-call(s32[5]{0:T(128)} %stack.96.where_ref, bf16[128,2560]{1,0:T(8,128)(2,1)} %get-tuple-element.64.refs_0_, ...), custom_call_target="tpu_custom_call", output_to_operand_aliasing={{3}: (4, {})} | custom-call | flops 939524096 | bytes 5505024 | tf_op jit(solution)/shard_map/pallas_call | solution.py:149
  61.6 5.3 %shard_map.105 = (bf16[2,8,128,896]{3,2,1,0:T(8,128)(2,1)}, bf16[8,128,1024]{2,1,0:T(8,128)(2,1)}, bf16[8,128,1024]{2,1,0:T(8,128)(2,1)}, bf16[8,128,768]{2,1,0:T(8,128)(2,1)}) custom-call(s32[5]{0:T(128)} %stack.94.where_ref, bf16[128,2560]{1,0:T(8,128)(2,1)} %copy-done.9, ...), custom_call_target="tpu_custom_call", output_to_operand_aliasing={{0}: (4, {}), {1}: (5, {}), {2}: (6, {}), {3}: (7, {})} | custom-call | flops 939524096 | bytes 5505024 | tf_op jit(solution)/shard_map/pallas_call | solution.py:149
  67.5 2.9 %collective-permute-start.12 = (bf16[128,2560]{1,0:T(8,128)(2,1)S(1)}, bf16[128,2560]{1,0:T(8,128)(2,1)}, u32[]{:S(2)}, u32[]{:S(2)}) collective-permute-start(bf16[128,2560]{1,0:T(8,128)(2,1)S(1)} %collective-permute-done.10.refs_1_), channel_id=1, source_target_pairs={{0,224},{16,240},{32,0},{48,16},{64,32},{80,48},{96,64},{112,80},{... | collective-permute-start | bytes 1966088 | tf_op jit(solution)/shard_map/ppermute | solution.py:22
  70.4 5.3 %shard_map.106 = (bf16[2,8,128,896]{3,2,1,0:T(8,128)(2,1)}, bf16[8,128,1024]{2,1,0:T(8,128)(2,1)}, bf16[8,128,1024]{2,1,0:T(8,128)(2,1)}, bf16[8,128,768]{2,1,0:T(8,128)(2,1)}) custom-call(s32[5]{0:T(128)} %stack.99.where_ref, bf16[128,2560]{1,0:T(8,128)(2,1)} %copy-done.8, ...), custom_call_target="tpu_custom_call", output_to_operand_aliasing={{0}: (4, {}), {1}: (5, {}), {2}: (6, {}), {3}: (7, {})} | custom-call | flops 939524096 | bytes 5505024 | tf_op jit(solution)/shard_map/pallas_call | solution.py:149
  75.7 5.7 %convolution_convert_fusion = bf16[2048,768]{1,0:T(8,128)(2,1)S(1)} fusion(bf16[2048,1024]{1,0:T(8,128)(2,1)} %all-gather.3.cloned.1.call-done, bf16[768,1024]{1,0:T(8,128)(2,1)S(1)} %copy-done), kind=kOutput, calls=%fused_computation | convolution fusion | flops 3222798336 | bytes 8912896 | tf_op jit(solution)/shard_map/dot_general | solution.py:228
  87.1 5.3 %shard_map.107 = (bf16[2,8,128,896]{3,2,1,0:T(8,128)(2,1)}, bf16[8,128,1024]{2,1,0:T(8,128)(2,1)}, bf16[8,128,1024]{2,1,0:T(8,128)(2,1)}, bf16[8,128,768]{2,1,0:T(8,128)(2,1)}) custom-call(s32[5]{0:T(128)} %stack.100.where_ref, bf16[128,2560]{1,0:T(8,128)(2,1)} %copy-done.6, ...), custom_call_target="tpu_custom_call", output_to_operand_aliasing={{0}: (4, {}), {1}: (5, {}), {2}: (6, {}), {3}: (7, {})} | custom-call | flops 939524096 | bytes 5505024 | tf_op jit(solution)/shard_map/pallas_call | solution.py:149
  93.2 4.1 %shard_map.108 = (bf16[2,8,128,896]{3,2,1,0:T(8,128)(2,1)}, bf16[8,128,1024]{2,1,0:T(8,128)(2,1)}, bf16[8,128,1024]{2,1,0:T(8,128)(2,1)}) custom-call(s32[2]{0:T(128)} %pad_add_fusion.2.where_ref, bf16[128,1792]{1,0:T(8,128)(2,1)} %copy-done.13, bf16[1024,896]{1,0:T(8,128)(2,1)} %refs_1_.1, ...), custom_call_target="tpu_custom_call", output_to_operand_aliasing={{0}: (3, {}), {1}: (4, {}), {2}: (5, {})} | custom-call | flops 469762048 | bytes 3276800 | tf_op jit(solution)/shard_map/pallas_call | solution.py:149
  103.2 3.2 %collective-permute-start.25 = (bf16[1,1024,768]{2,1,0:T(8,128)(2,1)S(1)}, bf16[1,1024,768]{2,1,0:T(8,128)(2,1)}, u32[]{:S(2)}, u32[]{:S(2)}) collective-permute-start(bf16[1,1024,768]{2,1,0:T(8,128)(2,1)S(1)} %bitcast.28), channel_id=1, source_target_pairs={{0,16},{16,0},{32,48},{48,32},{64,80},{80,64},{96,112},{112,96},{1... | collective-permute-start | bytes 4718600 | tf_op jit(solution)/shard_map/ppermute | solution.py:26
  106.4 5.4 %shard_map.109 = (bf16[256,1024]{1,0:T(8,128)(2,1)}, bf16[256,1024]{1,0:T(8,128)(2,1)}, bf16[256,1024]{1,0:T(8,128)(2,1)}, bf16[256,1024]{1,0:T(8,128)(2,1)}) custom-call(s32[4]{0:T(128)} %pad_add_fusion.1.where_ref, bf16[8,128,1024]{2,1,0:T(8,128)(2,1)} %get-tuple-element.101.kept_ref, bf16[8,128,1024]{2,1,0:T(8,128)(2,1)} %collective-permute-done.15.sent_ref), custom_call_target="tpu_custom_call" | custom-call | flops 1048576 | bytes 6291456 | tf_op jit(solution)/shard_map/pallas_call | solution.py:178
  114.2 2.8 %collective-permute-start.23 = (bf16[256,768]{1,0:T(8,128)(2,1)S(1)}, bf16[256,768]{1,0:T(8,128)(2,1)S(1)}, u32[]{:S(2)}, u32[]{:S(2)}) collective-permute-start(bf16[256,768]{1,0:T(8,128)(2,1)S(1)} %get-tuple-element.125), channel_id=1, source_target_pairs={{0,32},{16,48},{32,64},{48,80},{64,96},{80,112},{96,128},{112,144}... | collective-permute-start | bytes 1179656 | tf_op jit(solution)/shard_map/ppermute | solution.py:22
  124.0 6.7 %shard_map.110 = f32[1024,896]{1,0:T(8,128)} custom-call(s32[1]{0:T(128)} %constant.234.clone.1.first_ref, bf16[2,1024,896]{2,1,0:T(8,128)(2,1)S(1)} %bitcast.27, bf16[8,2,128,1024]{3,2,1,0:T(8,128)(2,1)S(1)} %bitcast.31), custom_call_target="tpu_custom_call" | custom-call | flops 3758096384 | bytes 11534336 | tf_op jit(solution)/shard_map/pallas_call | solution.py:210
  132.5 8.6 %collective-permute-done.25.refs_1_ = bf16[1,1024,768]{2,1,0:T(8,128)(2,1)} collective-permute-done((bf16[1,1024,768]{2,1,0:T(8,128)(2,1)S(1)}, bf16[1,1024,768]{2,1,0:T(8,128)(2,1)}, u32[]{:S(2)}, u32[]{:S(2)}) %collective-permute-start.25) | collective-permute-done | bytes 1572896 | tf_op jit(solution)/shard_map/ppermute | solution.py:26
  141.0 2.2 %add_convert_fusion = (bf16[256,768]{1,0:T(8,128)(2,1)}, bf16[256,768]{1,0:T(8,128)(2,1)}) fusion(bf16[256,768]{1,0:T(8,128)(2,1)S(1)} %collective-permute-done.24, bf16[2048,768]{1,0:T(8,128)(2,1)} %copy-done.5, s32[]{:T(128)S(6)} %select_n.233, bf16[256,768]{1,0:T(8,128)(2,1)S(1)} %collective-permute-done.23, s32[]{:T(128)S(6)} %select_n.226), kind=kLoop, calls=%fused_computation.4 | loop fusion | flops 1572864 | bytes 2359304 | tf_op jit(solution)/shard_map/convert_element_type | solution.py:244
  144.1 2.4 %collective-permute-start.27 = (bf16[256,768]{1,0:T(8,128)(2,1)}, bf16[256,768]{1,0:T(8,128)(2,1)}, u32[]{:S(2)}, u32[]{:S(2)}) collective-permute-start(bf16[256,768]{1,0:T(8,128)(2,1)} %get-tuple-element.122), channel_id=1, source_target_pairs={{0,224},{16,240},{32,0},{48,16},{64,32},{80,48},{96,64},{112,80},{... | collective-permute-start | bytes 1179656 | tf_op jit(solution)/shard_map/ppermute | solution.py:22
  148.5 2.2 %copy-done.3 = bf16[2048,1024]{1,0:T(8,128)(2,1)S(1)} copy-done((bf16[2048,1024]{1,0:T(8,128)(2,1)S(1)}, bf16[2048,1024]{1,0:T(8,128)(2,1)}, u32[]{:S(2)}) %copy-start.3) | copy-done | bytes 4194328
  150.7 6.0 %shard_map.111 = f32[768,1024]{1,0:T(8,128)} custom-call(s32[1]{0:T(128)} %bitcast.6.first_ref, bf16[1,1024,768]{2,1,0:T(8,128)(2,1)S(1)} %bitcast.29, bf16[1,1024,768]{2,1,0:T(8,128)(2,1)} %collective-permute-done.25.refs_1_, bf16[8,2,128,1024]{3,2,1,0:T(8,128)(2,1)S(1)} %bitcast.30), custom_call_target="tpu_custom_call" | custom-call | flops 3221225472 | bytes 10485760 | tf_op jit(solution)/shard_map/pallas_call | solution.py:210
  158.8 3.2 %collective-permute-start.28 = (bf16[128,768]{1,0:T(8,128)(2,1)}, bf16[128,768]{1,0:T(8,128)(2,1)}, u32[]{:S(2)}, u32[]{:S(2)}) collective-permute-start(bf16[128,768]{1,0:T(8,128)(2,1)} %dynamic-slice_convert_fusion.1), channel_id=1, source_target_pairs={{0,16},{16,0},{32,48},{48,32},{64,80},{80,64},{96,112},{112,96},{1... | collective-permute-start | bytes 589832 | tf_op jit(solution)/shard_map/ppermute | solution.py:26
  163.7 4.7 %collective-permute-done.28 = bf16[128,768]{1,0:T(8,128)(2,1)} collective-permute-done((bf16[128,768]{1,0:T(8,128)(2,1)}, bf16[128,768]{1,0:T(8,128)(2,1)}, u32[]{:S(2)}, u32[]{:S(2)}) %collective-permute-start.28) | collective-permute-done | bytes 196640 | tf_op jit(solution)/shard_map/ppermute | solution.py:26
  (118 shorter events, 57.7 us)
Async XLA Ops:
  7.2 68.5 %all-gather.3.cloned.1.call-start = ((), (), s32[]{:S(2)}) async-start(), calls=%async_computation | async-start | bytes 4456448 | tf_op jit(solution)/shard_map/all_gather | solution.py:263
  7.9 103.9 %all-gather.5.cloned.1.call-start = ((), (), s32[]{:S(2)}) async-start(), calls=%async_computation.1 | async-start | bytes 4456448 | tf_op jit(solution)/shard_map/all_gather | solution.py:264
  11.9 19.0 %collective-permute-start = (bf16[128,896]{1,0:T(8,128)(2,1)}, bf16[128,896]{1,0:T(8,128)(2,1)S(1)}, u32[]{:S(2)}, u32[]{:S(2)}) collective-permute-start(bf16[128,896]{1,0:T(8,128)(2,1)} %own_ref.1), channel_id=1, source_target_pairs={{0,16},{16,0},{32,48},{48,32},{64,80},{80,64},{96,112},{112,96},{1... | collective-permute-start | bytes 688136 | tf_op jit(solution)/shard_map/ppermute | solution.py:26
  19.9 11.0 %collective-permute-start.5 = (bf16[128,768]{1,0:T(8,128)(2,1)}, bf16[128,768]{1,0:T(8,128)(2,1)S(1)}, u32[]{:S(2)}, u32[]{:S(2)}) collective-permute-start(bf16[128,768]{1,0:T(8,128)(2,1)} %block_ref.1), channel_id=1, source_target_pairs={{0,32},{16,48},{32,64},{48,80},{64,96},{80,112},{96,128},{112,144}... | collective-permute-start | bytes 589832 | tf_op jit(solution)/shard_map/ppermute | solution.py:22
  34.5 14.5 %collective-permute-start.7 = (bf16[128,2560]{1,0:T(8,128)(2,1)}, bf16[128,2560]{1,0:T(8,128)(2,1)S(1)}, u32[]{:S(2)}, u32[]{:S(2)}) collective-permute-start(bf16[128,2560]{1,0:T(8,128)(2,1)} %get-tuple-element.64.refs_0_), channel_id=1, source_target_pairs={{0,32},{16,48},{32,64},{48,80},{64,96},{80,112},{96,128},{112,144}... | collective-permute-start | bytes 1966088 | tf_op jit(solution)/shard_map/ppermute | solution.py:22
  36.0 14.8 %collective-permute-start.8 = (bf16[128,2560]{1,0:T(8,128)(2,1)}, bf16[128,2560]{1,0:T(8,128)(2,1)}, u32[]{:S(2)}, u32[]{:S(2)}) collective-permute-start(bf16[128,2560]{1,0:T(8,128)(2,1)} %get-tuple-element.65.refs_1_), channel_id=1, source_target_pairs={{0,224},{16,240},{32,0},{48,16},{64,32},{80,48},{96,64},{112,80},{... | collective-permute-start | bytes 1966088 | tf_op jit(solution)/shard_map/ppermute | solution.py:22
  50.8 16.1 %collective-permute-start.10 = (bf16[128,2560]{1,0:T(8,128)(2,1)}, bf16[128,2560]{1,0:T(8,128)(2,1)S(1)}, u32[]{:S(2)}, u32[]{:S(2)}) collective-permute-start(bf16[128,2560]{1,0:T(8,128)(2,1)} %collective-permute-done.8.refs_1_), channel_id=1, source_target_pairs={{0,224},{16,240},{32,0},{48,16},{64,32},{80,48},{96,64},{112,80},{... | collective-permute-start | bytes 1966088 | tf_op jit(solution)/shard_map/ppermute | solution.py:22
  52.6 14.3 %collective-permute-start.9 = (bf16[128,2560]{1,0:T(8,128)(2,1)S(1)}, bf16[128,2560]{1,0:T(8,128)(2,1)S(1)}, u32[]{:S(2)}, u32[]{:S(2)}) collective-permute-start(bf16[128,2560]{1,0:T(8,128)(2,1)S(1)} %collective-permute-done.7.refs_0_), channel_id=1, source_target_pairs={{0,32},{16,48},{32,64},{48,80},{64,96},{80,112},{96,128},{112,144}... | collective-permute-start | bytes 1966088 | tf_op jit(solution)/shard_map/ppermute | solution.py:22
  66.9 14.5 %collective-permute-start.11 = (bf16[128,2560]{1,0:T(8,128)(2,1)S(1)}, bf16[128,2560]{1,0:T(8,128)(2,1)S(1)}, u32[]{:S(2)}, u32[]{:S(2)}) collective-permute-start(bf16[128,2560]{1,0:T(8,128)(2,1)S(1)} %collective-permute-done.9.refs_0_), channel_id=1, source_target_pairs={{0,32},{16,48},{32,64},{48,80},{64,96},{80,112},{96,128},{112,144}... | collective-permute-start | bytes 1966088 | tf_op jit(solution)/shard_map/ppermute | solution.py:22
  67.5 14.0 %collective-permute-start.12 = (bf16[128,2560]{1,0:T(8,128)(2,1)S(1)}, bf16[128,2560]{1,0:T(8,128)(2,1)}, u32[]{:S(2)}, u32[]{:S(2)}) collective-permute-start(bf16[128,2560]{1,0:T(8,128)(2,1)S(1)} %collective-permute-done.10.refs_1_), channel_id=1, source_target_pairs={{0,224},{16,240},{32,0},{48,16},{64,32},{80,48},{96,64},{112,80},{... | collective-permute-start | bytes 1966088 | tf_op jit(solution)/shard_map/ppermute | solution.py:22
  81.5 10.9 %collective-permute-start.13 = (bf16[128,1792]{1,0:T(8,128)(2,1)S(1)}, bf16[128,1792]{1,0:T(8,128)(2,1)S(1)}, u32[]{:S(2)}, u32[]{:S(2)}) collective-permute-start(bf16[128,1792]{1,0:T(8,128)(2,1)S(1)} %slice.21), channel_id=1, source_target_pairs={{0,32},{16,48},{32,64},{48,80},{64,96},{80,112},{96,128},{112,144}... | collective-permute-start | bytes 1376264 | tf_op jit(solution)/shard_map/ppermute | solution.py:22
  97.3 9.1 %collective-permute-start.15 = (bf16[8,128,1024]{2,1,0:T(8,128)(2,1)}, bf16[8,128,1024]{2,1,0:T(8,128)(2,1)}, u32[]{:S(2)}, u32[]{:S(2)}) collective-permute-start(bf16[8,128,1024]{2,1,0:T(8,128)(2,1)} %get-tuple-element.102), channel_id=1, source_target_pairs={{0,1},{1,0},{2,3},{3,2},{4,5},{5,4},{6,7},{7,6},{8,9},{9,8},{10,11... | collective-permute-start | bytes 6291464 | tf_op jit(solution)/shard_map/ppermute | solution.py:39
  97.3 14.4 %collective-permute-start.21 = (bf16[256,768]{1,0:T(8,128)(2,1)S(1)}, bf16[256,768]{1,0:T(8,128)(2,1)}, u32[]{:S(2)}, u32[]{:S(2)}) collective-permute-start(bf16[256,768]{1,0:T(8,128)(2,1)S(1)} %get-tuple-element.126), channel_id=1, source_target_pairs={{0,32},{16,48},{32,64},{48,80},{64,96},{80,112},{96,128},{112,144}... | collective-permute-start | bytes 1179656 | tf_op jit(solution)/shard_map/ppermute | solution.py:22
  100.7 11.8 %collective-permute-start.22 = (bf16[256,768]{1,0:T(8,128)(2,1)}, bf16[256,768]{1,0:T(8,128)(2,1)}, u32[]{:S(2)}, u32[]{:S(2)}) collective-permute-start(bf16[256,768]{1,0:T(8,128)(2,1)} %add_convert_fusion.4), channel_id=1, source_target_pairs={{0,224},{16,240},{32,0},{48,16},{64,32},{80,48},{96,64},{112,80},{... | collective-permute-start | bytes 1179656 | tf_op jit(solution)/shard_map/ppermute | solution.py:22
  103.2 37.9 %collective-permute-start.25 = (bf16[1,1024,768]{2,1,0:T(8,128)(2,1)S(1)}, bf16[1,1024,768]{2,1,0:T(8,128)(2,1)}, u32[]{:S(2)}, u32[]{:S(2)}) collective-permute-start(bf16[1,1024,768]{2,1,0:T(8,128)(2,1)S(1)} %bitcast.28), channel_id=1, source_target_pairs={{0,16},{16,0},{32,48},{48,32},{64,80},{80,64},{96,112},{112,96},{1... | collective-permute-start | bytes 4718600 | tf_op jit(solution)/shard_map/ppermute | solution.py:26
  114.2 26.8 %collective-permute-start.23 = (bf16[256,768]{1,0:T(8,128)(2,1)S(1)}, bf16[256,768]{1,0:T(8,128)(2,1)S(1)}, u32[]{:S(2)}, u32[]{:S(2)}) collective-permute-start(bf16[256,768]{1,0:T(8,128)(2,1)S(1)} %get-tuple-element.125), channel_id=1, source_target_pairs={{0,32},{16,48},{32,64},{48,80},{64,96},{80,112},{96,128},{112,144}... | collective-permute-start | bytes 1179656 | tf_op jit(solution)/shard_map/ppermute | solution.py:22
  117.0 24.1 %collective-permute-start.24 = (bf16[256,768]{1,0:T(8,128)(2,1)S(1)}, bf16[256,768]{1,0:T(8,128)(2,1)S(1)}, u32[]{:S(2)}, u32[]{:S(2)}) collective-permute-start(bf16[256,768]{1,0:T(8,128)(2,1)S(1)} %get-tuple-element.124), channel_id=1, source_target_pairs={{0,224},{16,240},{32,0},{48,16},{64,32},{80,48},{96,64},{112,80},{... | collective-permute-start | bytes 1179656 | tf_op jit(solution)/shard_map/ppermute | solution.py:22
  118.6 12.1 %collective-permute-start.17 = (bf16[128,1024]{1,0:T(8,128)(2,1)S(1)}, bf16[128,1024]{1,0:T(8,128)(2,1)S(1)}, u32[]{:S(2)}, u32[]{:S(2)}) collective-permute-start(bf16[128,1024]{1,0:T(8,128)(2,1)S(1)} %get-tuple-element.128), channel_id=1, source_target_pairs={{0,12},{1,13},{2,14},{3,15},{4,0},{5,1},{6,2},{7,3},{8,4},{9,5},{1... | collective-permute-start | bytes 786440 | tf_op jit(solution)/shard_map/ppermute | solution.py:31
  120.1 11.5 %collective-permute-start.16 = (bf16[128,1024]{1,0:T(8,128)(2,1)S(1)}, bf16[128,1024]{1,0:T(8,128)(2,1)S(1)}, u32[]{:S(2)}, u32[]{:S(2)}) collective-permute-start(bf16[128,1024]{1,0:T(8,128)(2,1)S(1)} %get-tuple-element.129), channel_id=1, source_target_pairs={{0,4},{1,5},{2,6},{3,7},{4,8},{5,9},{6,10},{7,11},{8,12},{9,13},{1... | collective-permute-start | bytes 786440 | tf_op jit(solution)/shard_map/ppermute | solution.py:31
  143.3 13.5 %collective-permute-start.26 = (bf16[256,768]{1,0:T(8,128)(2,1)}, bf16[256,768]{1,0:T(8,128)(2,1)S(1)}, u32[]{:S(2)}, u32[]{:S(2)}) collective-permute-start(bf16[256,768]{1,0:T(8,128)(2,1)} %get-tuple-element.123), channel_id=1, source_target_pairs={{0,32},{16,48},{32,64},{48,80},{64,96},{80,112},{96,128},{112,144}... | collective-permute-start | bytes 1179656 | tf_op jit(solution)/shard_map/ppermute | solution.py:22
  144.1 12.7 %collective-permute-start.27 = (bf16[256,768]{1,0:T(8,128)(2,1)}, bf16[256,768]{1,0:T(8,128)(2,1)}, u32[]{:S(2)}, u32[]{:S(2)}) collective-permute-start(bf16[256,768]{1,0:T(8,128)(2,1)} %get-tuple-element.122), channel_id=1, source_target_pairs={{0,224},{16,240},{32,0},{48,16},{64,32},{80,48},{96,64},{112,80},{... | collective-permute-start | bytes 1179656 | tf_op jit(solution)/shard_map/ppermute | solution.py:22
  146.5 15.5 %collective-permute-start.18 = (bf16[256,1024]{1,0:T(8,128)(2,1)}, bf16[256,1024]{1,0:T(8,128)(2,1)S(1)}, u32[]{:S(2)}, u32[]{:S(2)}) collective-permute-start(bf16[256,1024]{1,0:T(8,128)(2,1)} %pad_maximum_fusion), channel_id=1, source_target_pairs={{0,4},{1,5},{2,6},{3,7},{4,8},{5,9},{6,10},{7,11},{8,12},{9,13},{1... | collective-permute-start | bytes 1572872 | tf_op jit(solution)/shard_map/ppermute | solution.py:31
  148.0 14.1 %collective-permute-start.19 = (bf16[256,1024]{1,0:T(8,128)(2,1)}, bf16[256,1024]{1,0:T(8,128)(2,1)S(1)}, u32[]{:S(2)}, u32[]{:S(2)}) collective-permute-start(bf16[256,1024]{1,0:T(8,128)(2,1)} %pad_maximum_fusion.1), channel_id=1, source_target_pairs={{0,12},{1,13},{2,14},{3,15},{4,0},{5,1},{6,2},{7,3},{8,4},{9,5},{1... | collective-permute-start | bytes 1572872 | tf_op jit(solution)/shard_map/ppermute | solution.py:31
  158.8 9.6 %collective-permute-start.28 = (bf16[128,768]{1,0:T(8,128)(2,1)}, bf16[128,768]{1,0:T(8,128)(2,1)}, u32[]{:S(2)}, u32[]{:S(2)}) collective-permute-start(bf16[128,768]{1,0:T(8,128)(2,1)} %dynamic-slice_convert_fusion.1), channel_id=1, source_target_pairs={{0,16},{16,0},{32,48},{48,32},{64,80},{80,64},{96,112},{112,96},{1... | collective-permute-start | bytes 589832 | tf_op jit(solution)/shard_map/ppermute | solution.py:26
  (24 other events, 195.2 us)
Sparse Core Ops, SparseCore 0:
  9.9 42.6 all-gather.2
  54.4 39.8 all-gather.4

commit v4 on v3

--- a/solution.py
+++ b/solution.py
@@ -308,21 +308,22 @@
     ahead, behind = tie(ahead, behind)
     wqkv_grad = contract_rows([q_all], jnp.int32(0), x_all, False, factor, 256)
     came1, came2 = over_x(ahead, 1), over_x(behind, -1)
+    came1, came2, attn_other = tie(came1, came2, attn_other)
     total = mine.astype(jnp.float32) + came1.astype(jnp.float32) + came2.astype(jnp.float32)
     keep = lax.dynamic_slice_in_dim(total, yl * TB, TB, 0)
     give = lax.dynamic_slice_in_dim(total, (1 - yl) * TB, TB, 0).astype(jnp.bfloat16)
     summed = keep + over_yl(give).astype(jnp.float32)
     input_grad = (out_grad.astype(jnp.float32) + summed).astype(jnp.bfloat16)
 
-    fold.up, fold.down, attn_other, wqkv_grad, _ = tie(fold.up, fold.down, attn_other, wqkv_grad, ahead)
+    fold.up, fold.down, wqkv_grad, _ = tie(fold.up, fold.down, wqkv_grad, ahead)
     fold.step()
-    wout_grad = contract_rows([attn_all, attn_other], yh, g_all, True, factor, 256)
-    fold.up, fold.down, wout_grad = tie(fold.up, fold.down, wout_grad)
     sums = fold.sums()
     keep = lax.dynamic_slice_in_dim(sums, yh * TB, TB, 0)
     send = lax.dynamic_slice_in_dim(sums, (1 - yh) * TB, TB, 0).astype(jnp.bfloat16)
     attn_grad = (keep + over_yh(send).astype(jnp.float32)).astype(jnp.bfloat16)
 
+    attn_other, _, _ = tie(attn_other, give, send)
+    wout_grad = contract_rows([attn_all, attn_other], yh, g_all, True, factor, 256)
     return (input_grad, attn_grad, wqkv_grad, wout_grad)
 
 

time: 182 us -> 172 us (0.945)
  waiting for transfers between devices: 34.4 us -> 27.3 us
  local copies, waits for them, and re-layouts: 13.3 us -> 9.81 us
    ppermute x4, waiting for transfers between devices: 14.2 us -> 1.91 us  [over_yh(): return lax.ppermute(value, 'dp', [(d, d ^ 1) for d in range(16)])]
    ppermute x4, waiting for transfers between devices: 0.01 us -> 6.24 us  [over_x(): return lax.ppermute(value, 'tensor', pairs)]
    unnamed x34 -> x36, local copies, waits for them, and re-layouts: 6.45 us -> 4.28 us
  transfers between devices with their start and end apart: 31 -> 31, of which waited for: 9 -> 11; matrix products, arithmetic and copies ran while one was open for 15% -> 15% of each run, Pallas kernels for 27% -> 28%
where the time goes in v4:
time: 172 us; the launch traced here: 169 us
  Pallas kernels  47.7 us (28%)
  starting transfers between devices  47 us (27%)
  waiting for transfers between devices  27.3 us (16%)
  other arithmetic  16.9 us (10%)
  between operations  14.3 us (8%)
  local copies, waits for them, and re-layouts  9.81 us (6%)
  matrix products  5.71 us (3%)
    ppermute x19, starting transfers between devices, over_z(): return lax.ppermute(value, 'dp', pairs)  31.9 us
    pallas_call x5, Pallas kernels, absorb(): pl.pallas_call(body, out_shape=tuple(out_shape), grid_spec=pltpu.Prefetch...  25.2 us
    ppermute x19, waiting for transfers between devices, over_z(): return lax.ppermute(value, 'dp', pairs)  17.8 us
    pallas_call x2, Pallas kernels, contract_rows(): pl.pallas_call(body, out_shape=jax.ShapeDtypeStruct((m, n), jnp.float32),...  12.8 us
    ppermute x4, starting transfers between devices, over_yh(): return lax.ppermute(value, 'dp', [(d, d ^ 1) for d in range(16)])  10.1 us
    ppermute x4, waiting for transfers between devices, over_x(): return lax.ppermute(value, 'tensor', pairs)  6.24 us
    convert_element_type x3, other arithmetic, add(): (part if got is None else part + got.astype(jnp.float32)).astype(jnp.bflo...  5.85 us
    dot_general x1, matrix products, contract_cols(): lax.dot_general(left, right, (((1,), (1,)), ((), ())), preferred_element_...  5.71 us
  transfers between devices with their start and end apart: 31, of which 11 were waited for; matrix products, arithmetic and copies ran while one was open for 15% of the time, Pallas kernels for 28%

profile of v4, /device:TPU:2, one launch (start us, length us, event | category | flops | bytes accessed | tf_op | source)
XLA Modules:
  0.0 168.8 jit_solution(544178284698770088)
XLA Ops:
  8.7 3.3 %collective-permute-start.1 = (s32[1,128]{1,0:T(1,128)}, s32[1,128]{1,0:T(1,128)S(1)}, u32[]{:S(2)}, u32[]{:S(2)}) collective-permute-start(s32[1,128]{1,0:T(1,128)} %bitcast.32), channel_id=1, source_target_pairs={{0,16},{16,0},{32,48},{48,32},{64,80},{80,64},{96,112},{112,96},{1... | collective-permute-start | bytes 1544 | tf_op jit(solution)/shard_map/ppermute | solution.py:26
  16.6 3.3 %collective-permute-start.3 = (s32[2,128]{1,0:T(2,128)S(1)}, s32[2,128]{1,0:T(2,128)S(1)}, u32[]{:S(2)}, u32[]{:S(2)}) collective-permute-start(s32[2,128]{1,0:T(2,128)S(1)} %add_select_fusion), channel_id=1, source_target_pairs={{0,64},{16,80},{32,96},{48,112},{64,128},{80,144},{96,160},{112,17... | collective-permute-start | bytes 3080 | tf_op jit(solution)/shard_map/ppermute | solution.py:22
  19.9 3.1 %collective-permute-start.5 = (bf16[128,768]{1,0:T(8,128)(2,1)}, bf16[128,768]{1,0:T(8,128)(2,1)S(1)}, u32[]{:S(2)}, u32[]{:S(2)}) collective-permute-start(bf16[128,768]{1,0:T(8,128)(2,1)} %block_ref.1), channel_id=1, source_target_pairs={{0,32},{16,48},{32,64},{48,80},{64,96},{80,112},{96,128},{112,144}... | collective-permute-start | bytes 589832 | tf_op jit(solution)/shard_map/ppermute | solution.py:22
  23.6 1.9 %collective-permute-start.4 = (s32[4,128]{1,0:T(4,128)S(1)}, s32[4,128]{1,0:T(4,128)S(1)}, u32[]{:S(2)}, u32[]{:S(2)}) collective-permute-start(s32[4,128]{1,0:T(4,128)S(1)} %pad_add_fusion), channel_id=1, source_target_pairs={{0,64},{16,80},{32,96},{48,112},{64,128},{80,144},{96,160},{112,17... | collective-permute-start | bytes 6152 | tf_op jit(solution)/shard_map/ppermute | solution.py:22
  26.3 3.0 %collective-permute-done.4 = s32[4,128]{1,0:T(4,128)S(1)} collective-permute-done((s32[4,128]{1,0:T(4,128)S(1)}, s32[4,128]{1,0:T(4,128)S(1)}, u32[]{:S(2)}, u32[]{:S(2)}) %collective-permute-start.4) | collective-permute-done | bytes 2080 | tf_op jit(solution)/shard_map/ppermute | solution.py:22
  31.7 2.8 %shard_map.102 = (bf16[128,2560]{1,0:T(8,128)(2,1)}, bf16[128,2560]{1,0:T(8,128)(2,1)}) custom-call(s32[2]{0:T(128)} %pad_add_fusion.3.where_ref, bf16[128,896]{1,0:T(8,128)(2,1)} %own_ref.1, bf16[128,896]{1,0:T(8,128)(2,1)} %copy-done.15, f32[256,128]{1,0:T(8,128)} %get-tuple-element.131.cos_ref, f32[256,128]{1,0:T(8,128)} %get-tuple-element.130.sin_ref, ...), custom_call_target="tpu_custom_call" | custom-call | flops 2293760 | bytes 1835008 | tf_op jit(solution)/shard_map/pallas_call | solution.py:83
  37.7 11.2 %collective-permute-done.7.refs_0_ = bf16[128,2560]{1,0:T(8,128)(2,1)S(1)} collective-permute-done((bf16[128,2560]{1,0:T(8,128)(2,1)}, bf16[128,2560]{1,0:T(8,128)(2,1)S(1)}, u32[]{:S(2)}, u32[]{:S(2)}) %collective-permute-start.7) | collective-permute-done | bytes 655392 | tf_op jit(solution)/shard_map/ppermute | solution.py:22
  56.4 5.2 %shard_map.104 = (bf16[2,8,128,896]{3,2,1,0:T(8,128)(2,1)}, bf16[8,128,1024]{2,1,0:T(8,128)(2,1)}, bf16[8,128,1024]{2,1,0:T(8,128)(2,1)}, bf16[8,128,768]{2,1,0:T(8,128)(2,1)}) custom-call(s32[5]{0:T(128)} %stack.96.where_ref, bf16[128,2560]{1,0:T(8,128)(2,1)} %get-tuple-element.64.refs_0_, ...), custom_call_target="tpu_custom_call", output_to_operand_aliasing={{3}: (4, {})} | custom-call | flops 939524096 | bytes 5505024 | tf_op jit(solution)/shard_map/pallas_call | solution.py:149
  61.6 5.2 %shard_map.105 = (bf16[2,8,128,896]{3,2,1,0:T(8,128)(2,1)}, bf16[8,128,1024]{2,1,0:T(8,128)(2,1)}, bf16[8,128,1024]{2,1,0:T(8,128)(2,1)}, bf16[8,128,768]{2,1,0:T(8,128)(2,1)}) custom-call(s32[5]{0:T(128)} %stack.94.where_ref, bf16[128,2560]{1,0:T(8,128)(2,1)} %copy-done.10, ...), custom_call_target="tpu_custom_call", output_to_operand_aliasing={{0}: (4, {}), {1}: (5, {}), {2}: (6, {}), {3}: (7, {})} | custom-call | flops 939524096 | bytes 5505024 | tf_op jit(solution)/shard_map/pallas_call | solution.py:149
  67.5 2.9 %collective-permute-start.12 = (bf16[128,2560]{1,0:T(8,128)(2,1)S(1)}, bf16[128,2560]{1,0:T(8,128)(2,1)}, u32[]{:S(2)}, u32[]{:S(2)}) collective-permute-start(bf16[128,2560]{1,0:T(8,128)(2,1)S(1)} %collective-permute-done.10.refs_1_), channel_id=1, source_target_pairs={{0,224},{16,240},{32,0},{48,16},{64,32},{80,48},{96,64},{112,80},{... | collective-permute-start | bytes 1966088 | tf_op jit(solution)/shard_map/ppermute | solution.py:22
  70.4 5.3 %shard_map.106 = (bf16[2,8,128,896]{3,2,1,0:T(8,128)(2,1)}, bf16[8,128,1024]{2,1,0:T(8,128)(2,1)}, bf16[8,128,1024]{2,1,0:T(8,128)(2,1)}, bf16[8,128,768]{2,1,0:T(8,128)(2,1)}) custom-call(s32[5]{0:T(128)} %stack.99.where_ref, bf16[128,2560]{1,0:T(8,128)(2,1)} %copy-done.9, ...), custom_call_target="tpu_custom_call", output_to_operand_aliasing={{0}: (4, {}), {1}: (5, {}), {2}: (6, {}), {3}: (7, {})} | custom-call | flops 939524096 | bytes 5505024 | tf_op jit(solution)/shard_map/pallas_call | solution.py:149
  75.7 5.7 %convolution_convert_fusion = bf16[2048,768]{1,0:T(8,128)(2,1)S(1)} fusion(bf16[2048,1024]{1,0:T(8,128)(2,1)} %all-gather.3.cloned.1.call-done, bf16[768,1024]{1,0:T(8,128)(2,1)S(1)} %copy-done), kind=kOutput, calls=%fused_computation | convolution fusion | flops 3222798336 | bytes 8912896 | tf_op jit(solution)/shard_map/dot_general | solution.py:228
  87.0 5.3 %shard_map.107 = (bf16[2,8,128,896]{3,2,1,0:T(8,128)(2,1)}, bf16[8,128,1024]{2,1,0:T(8,128)(2,1)}, bf16[8,128,1024]{2,1,0:T(8,128)(2,1)}, bf16[8,128,768]{2,1,0:T(8,128)(2,1)}) custom-call(s32[5]{0:T(128)} %stack.100.where_ref, bf16[128,2560]{1,0:T(8,128)(2,1)} %copy-done.6, ...), custom_call_target="tpu_custom_call", output_to_operand_aliasing={{0}: (4, {}), {1}: (5, {}), {2}: (6, {}), {3}: (7, {})} | custom-call | flops 939524096 | bytes 5505024 | tf_op jit(solution)/shard_map/pallas_call | solution.py:149
  93.1 4.1 %shard_map.108 = (bf16[2,8,128,896]{3,2,1,0:T(8,128)(2,1)}, bf16[8,128,1024]{2,1,0:T(8,128)(2,1)}, bf16[8,128,1024]{2,1,0:T(8,128)(2,1)}) custom-call(s32[2]{0:T(128)} %pad_add_fusion.2.where_ref, bf16[128,1792]{1,0:T(8,128)(2,1)} %copy-done.14, bf16[1024,896]{1,0:T(8,128)(2,1)} %refs_1_.1, ...), custom_call_target="tpu_custom_call", output_to_operand_aliasing={{0}: (3, {}), {1}: (4, {}), {2}: (5, {})} | custom-call | flops 469762048 | bytes 3276800 | tf_op jit(solution)/shard_map/pallas_call | solution.py:149
  98.7 2.0 %add_convert_fusion.4 = bf16[256,768]{1,0:T(8,128)(2,1)} fusion(bf16[256,768]{1,0:T(8,128)(2,1)} %collective-permute-done.14, bf16[2048,768]{1,0:T(8,128)(2,1)} %copy-done.5, s32[]{:T(128)S(6)} %select_n.231), kind=kLoop, calls=%fused_computation.8 | loop fusion | flops 786432 | bytes 1179652 | tf_op jit(solution)/shard_map/convert_element_type | solution.py:244
  103.0 3.2 %collective-permute-start.20 = (bf16[1,1024,768]{2,1,0:T(8,128)(2,1)S(1)}, bf16[1,1024,768]{2,1,0:T(8,128)(2,1)}, u32[]{:S(2)}, u32[]{:S(2)}) collective-permute-start(bf16[1,1024,768]{2,1,0:T(8,128)(2,1)S(1)} %bitcast.28), channel_id=1, source_target_pairs={{0,16},{16,0},{32,48},{48,32},{64,80},{80,64},{96,112},{112,96},{1... | collective-permute-start | bytes 4718600 | tf_op jit(solution)/shard_map/ppermute | solution.py:26
  106.2 5.3 %shard_map.109 = (bf16[256,1024]{1,0:T(8,128)(2,1)}, bf16[256,1024]{1,0:T(8,128)(2,1)}, bf16[256,1024]{1,0:T(8,128)(2,1)}, bf16[256,1024]{1,0:T(8,128)(2,1)}) custom-call(s32[4]{0:T(128)} %pad_add_fusion.1.where_ref, bf16[8,128,1024]{2,1,0:T(8,128)(2,1)} %get-tuple-element.101.kept_ref, bf16[8,128,1024]{2,1,0:T(8,128)(2,1)} %collective-permute-done.15.sent_ref), custom_call_target="tpu_custom_call" | custom-call | flops 1048576 | bytes 6291456 | tf_op jit(solution)/shard_map/pallas_call | solution.py:178
  114.2 2.8 %collective-permute-start.24 = (bf16[256,768]{1,0:T(8,128)(2,1)S(1)}, bf16[256,768]{1,0:T(8,128)(2,1)S(1)}, u32[]{:S(2)}, u32[]{:S(2)}) collective-permute-start(bf16[256,768]{1,0:T(8,128)(2,1)S(1)} %get-tuple-element.125), channel_id=1, source_target_pairs={{0,32},{16,48},{32,64},{48,80},{64,96},{80,112},{96,128},{112,144}... | collective-permute-start | bytes 1179656 | tf_op jit(solution)/shard_map/ppermute | solution.py:22
  121.8 2.2 %copy-done.4 = bf16[2048,1024]{1,0:T(8,128)(2,1)S(1)} copy-done((bf16[2048,1024]{1,0:T(8,128)(2,1)S(1)}, bf16[2048,1024]{1,0:T(8,128)(2,1)}, u32[]{:S(2)}) %copy-start.4) | copy-done | bytes 4194328
  124.0 6.7 %shard_map.110 = f32[1024,896]{1,0:T(8,128)} custom-call(s32[1]{0:T(128)} %constant.234.clone.1.first_ref, bf16[2,1024,896]{2,1,0:T(8,128)(2,1)S(1)} %bitcast.27, bf16[8,2,128,1024]{3,2,1,0:T(8,128)(2,1)S(1)} %bitcast.31), custom_call_target="tpu_custom_call" | custom-call | flops 3758096384 | bytes 11534336 | tf_op jit(solution)/shard_map/pallas_call | solution.py:210
  134.5 2.2 %add_convert_fusion.1 = (bf16[256,768]{1,0:T(8,128)(2,1)}, bf16[256,768]{1,0:T(8,128)(2,1)}) fusion(bf16[256,768]{1,0:T(8,128)(2,1)S(1)} %collective-permute-done.24, bf16[2048,768]{1,0:T(8,128)(2,1)} %copy-done.5, s32[]{:T(128)S(6)} %select_n.226, bf16[256,768]{1,0:T(8,128)(2,1)S(1)} %collective-permute-done.25, s32[]{:T(128)S(6)} %select_n.233), kind=kLoop, calls=%fused_computation.5 | loop fusion | flops 1572864 | bytes 2359304 | tf_op jit(solution)/shard_map/convert_element_type | solution.py:244
  140.9 4.3 %collective-permute-done.18 = bf16[256,1024]{1,0:T(8,128)(2,1)} collective-permute-done((bf16[256,1024]{1,0:T(8,128)(2,1)}, bf16[256,1024]{1,0:T(8,128)(2,1)}, u32[]{:S(2)}, u32[]{:S(2)}) %collective-permute-start.18) | collective-permute-done | bytes 524320 | tf_op jit(solution)/shard_map/ppermute | solution.py:31
  148.7 3.3 %collective-permute-start.28 = (bf16[128,768]{1,0:T(8,128)(2,1)S(1)}, bf16[128,768]{1,0:T(8,128)(2,1)S(1)}, u32[]{:S(2)}, u32[]{:S(2)}) collective-permute-start(bf16[128,768]{1,0:T(8,128)(2,1)S(1)} %dynamic-slice_convert_fusion.1), channel_id=1, source_target_pairs={{0,16},{16,0},{32,48},{48,32},{64,80},{80,64},{96,112},{112,96},{1... | collective-permute-start | bytes 589832 | tf_op jit(solution)/shard_map/ppermute | solution.py:26
  154.3 6.1 %shard_map.111 = f32[768,1024]{1,0:T(8,128)} custom-call(s32[1]{0:T(128)} %bitcast.6.first_ref, bf16[1,1024,768]{2,1,0:T(8,128)(2,1)S(1)} %bitcast.29, bf16[1,1024,768]{2,1,0:T(8,128)(2,1)} %collective-permute-done.20.refs_1_, bf16[8,2,128,1024]{3,2,1,0:T(8,128)(2,1)S(1)} %bitcast.30), custom_call_target="tpu_custom_call" | custom-call | flops 3221225472 | bytes 10485760 | tf_op jit(solution)/shard_map/pallas_call | solution.py:210
  (120 shorter events, 53.9 us)
Async XLA Ops:
  7.2 68.5 %all-gather.3.cloned.1.call-start = ((), (), s32[]{:S(2)}) async-start(), calls=%async_computation | async-start | bytes 4456448 | tf_op jit(solution)/shard_map/all_gather | solution.py:263
  7.9 103.7 %all-gather.5.cloned.1.call-start = ((), (), s32[]{:S(2)}) async-start(), calls=%async_computation.1 | async-start | bytes 4456448 | tf_op jit(solution)/shard_map/all_gather | solution.py:264
  11.9 19.0 %collective-permute-start = (bf16[128,896]{1,0:T(8,128)(2,1)}, bf16[128,896]{1,0:T(8,128)(2,1)S(1)}, u32[]{:S(2)}, u32[]{:S(2)}) collective-permute-start(bf16[128,896]{1,0:T(8,128)(2,1)} %own_ref.1), channel_id=1, source_target_pairs={{0,16},{16,0},{32,48},{48,32},{64,80},{80,64},{96,112},{112,96},{1... | collective-permute-start | bytes 688136 | tf_op jit(solution)/shard_map/ppermute | solution.py:26
  19.9 11.0 %collective-permute-start.5 = (bf16[128,768]{1,0:T(8,128)(2,1)}, bf16[128,768]{1,0:T(8,128)(2,1)S(1)}, u32[]{:S(2)}, u32[]{:S(2)}) collective-permute-start(bf16[128,768]{1,0:T(8,128)(2,1)} %block_ref.1), channel_id=1, source_target_pairs={{0,32},{16,48},{32,64},{48,80},{64,96},{80,112},{96,128},{112,144}... | collective-permute-start | bytes 589832 | tf_op jit(solution)/shard_map/ppermute | solution.py:22
  34.5 14.5 %collective-permute-start.7 = (bf16[128,2560]{1,0:T(8,128)(2,1)}, bf16[128,2560]{1,0:T(8,128)(2,1)S(1)}, u32[]{:S(2)}, u32[]{:S(2)}) collective-permute-start(bf16[128,2560]{1,0:T(8,128)(2,1)} %get-tuple-element.64.refs_0_), channel_id=1, source_target_pairs={{0,32},{16,48},{32,64},{48,80},{64,96},{80,112},{96,128},{112,144}... | collective-permute-start | bytes 1966088 | tf_op jit(solution)/shard_map/ppermute | solution.py:22
  36.0 14.8 %collective-permute-start.8 = (bf16[128,2560]{1,0:T(8,128)(2,1)}, bf16[128,2560]{1,0:T(8,128)(2,1)}, u32[]{:S(2)}, u32[]{:S(2)}) collective-permute-start(bf16[128,2560]{1,0:T(8,128)(2,1)} %get-tuple-element.65.refs_1_), channel_id=1, source_target_pairs={{0,224},{16,240},{32,0},{48,16},{64,32},{80,48},{96,64},{112,80},{... | collective-permute-start | bytes 1966088 | tf_op jit(solution)/shard_map/ppermute | solution.py:22
  50.8 16.1 %collective-permute-start.10 = (bf16[128,2560]{1,0:T(8,128)(2,1)}, bf16[128,2560]{1,0:T(8,128)(2,1)S(1)}, u32[]{:S(2)}, u32[]{:S(2)}) collective-permute-start(bf16[128,2560]{1,0:T(8,128)(2,1)} %collective-permute-done.8.refs_1_), channel_id=1, source_target_pairs={{0,224},{16,240},{32,0},{48,16},{64,32},{80,48},{96,64},{112,80},{... | collective-permute-start | bytes 1966088 | tf_op jit(solution)/shard_map/ppermute | solution.py:22
  52.6 14.2 %collective-permute-start.9 = (bf16[128,2560]{1,0:T(8,128)(2,1)S(1)}, bf16[128,2560]{1,0:T(8,128)(2,1)S(1)}, u32[]{:S(2)}, u32[]{:S(2)}) collective-permute-start(bf16[128,2560]{1,0:T(8,128)(2,1)S(1)} %collective-permute-done.7.refs_0_), channel_id=1, source_target_pairs={{0,32},{16,48},{32,64},{48,80},{64,96},{80,112},{96,128},{112,144}... | collective-permute-start | bytes 1966088 | tf_op jit(solution)/shard_map/ppermute | solution.py:22
  66.9 14.5 %collective-permute-start.11 = (bf16[128,2560]{1,0:T(8,128)(2,1)S(1)}, bf16[128,2560]{1,0:T(8,128)(2,1)S(1)}, u32[]{:S(2)}, u32[]{:S(2)}) collective-permute-start(bf16[128,2560]{1,0:T(8,128)(2,1)S(1)} %collective-permute-done.9.refs_0_), channel_id=1, source_target_pairs={{0,32},{16,48},{32,64},{48,80},{64,96},{80,112},{96,128},{112,144}... | collective-permute-start | bytes 1966088 | tf_op jit(solution)/shard_map/ppermute | solution.py:22
  67.5 14.0 %collective-permute-start.12 = (bf16[128,2560]{1,0:T(8,128)(2,1)S(1)}, bf16[128,2560]{1,0:T(8,128)(2,1)}, u32[]{:S(2)}, u32[]{:S(2)}) collective-permute-start(bf16[128,2560]{1,0:T(8,128)(2,1)S(1)} %collective-permute-done.10.refs_1_), channel_id=1, source_target_pairs={{0,224},{16,240},{32,0},{48,16},{64,32},{80,48},{96,64},{112,80},{... | collective-permute-start | bytes 1966088 | tf_op jit(solution)/shard_map/ppermute | solution.py:22
  81.5 10.9 %collective-permute-start.13 = (bf16[128,1792]{1,0:T(8,128)(2,1)S(1)}, bf16[128,1792]{1,0:T(8,128)(2,1)S(1)}, u32[]{:S(2)}, u32[]{:S(2)}) collective-permute-start(bf16[128,1792]{1,0:T(8,128)(2,1)S(1)} %slice.21), channel_id=1, source_target_pairs={{0,32},{16,48},{32,64},{48,80},{64,96},{80,112},{96,128},{112,144}... | collective-permute-start | bytes 1376264 | tf_op jit(solution)/shard_map/ppermute | solution.py:22
  97.3 9.0 %collective-permute-start.15 = (bf16[8,128,1024]{2,1,0:T(8,128)(2,1)}, bf16[8,128,1024]{2,1,0:T(8,128)(2,1)}, u32[]{:S(2)}, u32[]{:S(2)}) collective-permute-start(bf16[8,128,1024]{2,1,0:T(8,128)(2,1)} %get-tuple-element.102), channel_id=1, source_target_pairs={{0,1},{1,0},{2,3},{3,2},{4,5},{5,4},{6,7},{7,6},{8,9},{9,8},{10,11... | collective-permute-start | bytes 6291464 | tf_op jit(solution)/shard_map/ppermute | solution.py:39
  97.3 14.3 %collective-permute-start.22 = (bf16[256,768]{1,0:T(8,128)(2,1)S(1)}, bf16[256,768]{1,0:T(8,128)(2,1)}, u32[]{:S(2)}, u32[]{:S(2)}) collective-permute-start(bf16[256,768]{1,0:T(8,128)(2,1)S(1)} %get-tuple-element.126), channel_id=1, source_target_pairs={{0,32},{16,48},{32,64},{48,80},{64,96},{80,112},{96,128},{112,144}... | collective-permute-start | bytes 1179656 | tf_op jit(solution)/shard_map/ppermute | solution.py:22
  100.7 11.8 %collective-permute-start.23 = (bf16[256,768]{1,0:T(8,128)(2,1)}, bf16[256,768]{1,0:T(8,128)(2,1)}, u32[]{:S(2)}, u32[]{:S(2)}) collective-permute-start(bf16[256,768]{1,0:T(8,128)(2,1)} %add_convert_fusion.4), channel_id=1, source_target_pairs={{0,224},{16,240},{32,0},{48,16},{64,32},{80,48},{96,64},{112,80},{... | collective-permute-start | bytes 1179656 | tf_op jit(solution)/shard_map/ppermute | solution.py:22
  103.0 37.9 %collective-permute-start.20 = (bf16[1,1024,768]{2,1,0:T(8,128)(2,1)S(1)}, bf16[1,1024,768]{2,1,0:T(8,128)(2,1)}, u32[]{:S(2)}, u32[]{:S(2)}) collective-permute-start(bf16[1,1024,768]{2,1,0:T(8,128)(2,1)S(1)} %bitcast.28), channel_id=1, source_target_pairs={{0,16},{16,0},{32,48},{48,32},{64,80},{80,64},{96,112},{112,96},{1... | collective-permute-start | bytes 4718600 | tf_op jit(solution)/shard_map/ppermute | solution.py:26
  114.2 20.3 %collective-permute-start.24 = (bf16[256,768]{1,0:T(8,128)(2,1)S(1)}, bf16[256,768]{1,0:T(8,128)(2,1)S(1)}, u32[]{:S(2)}, u32[]{:S(2)}) collective-permute-start(bf16[256,768]{1,0:T(8,128)(2,1)S(1)} %get-tuple-element.125), channel_id=1, source_target_pairs={{0,32},{16,48},{32,64},{48,80},{64,96},{80,112},{96,128},{112,144}... | collective-permute-start | bytes 1179656 | tf_op jit(solution)/shard_map/ppermute | solution.py:22
  117.0 17.5 %collective-permute-start.25 = (bf16[256,768]{1,0:T(8,128)(2,1)S(1)}, bf16[256,768]{1,0:T(8,128)(2,1)S(1)}, u32[]{:S(2)}, u32[]{:S(2)}) collective-permute-start(bf16[256,768]{1,0:T(8,128)(2,1)S(1)} %get-tuple-element.124), channel_id=1, source_target_pairs={{0,224},{16,240},{32,0},{48,16},{64,32},{80,48},{96,64},{112,80},{... | collective-permute-start | bytes 1179656 | tf_op jit(solution)/shard_map/ppermute | solution.py:22
  118.6 12.1 %collective-permute-start.17 = (bf16[128,1024]{1,0:T(8,128)(2,1)S(1)}, bf16[128,1024]{1,0:T(8,128)(2,1)S(1)}, u32[]{:S(2)}, u32[]{:S(2)}) collective-permute-start(bf16[128,1024]{1,0:T(8,128)(2,1)S(1)} %get-tuple-element.128), channel_id=1, source_target_pairs={{0,12},{1,13},{2,14},{3,15},{4,0},{5,1},{6,2},{7,3},{8,4},{9,5},{1... | collective-permute-start | bytes 786440 | tf_op jit(solution)/shard_map/ppermute | solution.py:31
  120.1 11.5 %collective-permute-start.16 = (bf16[128,1024]{1,0:T(8,128)(2,1)S(1)}, bf16[128,1024]{1,0:T(8,128)(2,1)S(1)}, u32[]{:S(2)}, u32[]{:S(2)}) collective-permute-start(bf16[128,1024]{1,0:T(8,128)(2,1)S(1)} %get-tuple-element.129), channel_id=1, source_target_pairs={{0,4},{1,5},{2,6},{3,7},{4,8},{5,9},{6,10},{7,11},{8,12},{9,13},{1... | collective-permute-start | bytes 786440 | tf_op jit(solution)/shard_map/ppermute | solution.py:31
  132.5 12.8 %collective-permute-start.18 = (bf16[256,1024]{1,0:T(8,128)(2,1)}, bf16[256,1024]{1,0:T(8,128)(2,1)}, u32[]{:S(2)}, u32[]{:S(2)}) collective-permute-start(bf16[256,1024]{1,0:T(8,128)(2,1)} %pad_maximum_fusion), channel_id=1, source_target_pairs={{0,4},{1,5},{2,6},{3,7},{4,8},{5,9},{6,10},{7,11},{8,12},{9,13},{1... | collective-permute-start | bytes 1572872 | tf_op jit(solution)/shard_map/ppermute | solution.py:31
  134.0 13.1 %collective-permute-start.19 = (bf16[256,1024]{1,0:T(8,128)(2,1)}, bf16[256,1024]{1,0:T(8,128)(2,1)}, u32[]{:S(2)}, u32[]{:S(2)}) collective-permute-start(bf16[256,1024]{1,0:T(8,128)(2,1)} %pad_maximum_fusion.1), channel_id=1, source_target_pairs={{0,12},{1,13},{2,14},{3,15},{4,0},{5,1},{6,2},{7,3},{8,4},{9,5},{1... | collective-permute-start | bytes 1572872 | tf_op jit(solution)/shard_map/ppermute | solution.py:31
  136.7 10.5 %collective-permute-start.26 = (bf16[256,768]{1,0:T(8,128)(2,1)}, bf16[256,768]{1,0:T(8,128)(2,1)S(1)}, u32[]{:S(2)}, u32[]{:S(2)}) collective-permute-start(bf16[256,768]{1,0:T(8,128)(2,1)} %get-tuple-element.122), channel_id=1, source_target_pairs={{0,32},{16,48},{32,64},{48,80},{64,96},{80,112},{96,128},{112,144}... | collective-permute-start | bytes 1179656 | tf_op jit(solution)/shard_map/ppermute | solution.py:22
  138.2 9.1 %collective-permute-start.27 = (bf16[256,768]{1,0:T(8,128)(2,1)}, bf16[256,768]{1,0:T(8,128)(2,1)}, u32[]{:S(2)}, u32[]{:S(2)}) collective-permute-start(bf16[256,768]{1,0:T(8,128)(2,1)} %get-tuple-element.123), channel_id=1, source_target_pairs={{0,224},{16,240},{32,0},{48,16},{64,32},{80,48},{96,64},{112,80},{... | collective-permute-start | bytes 1179656 | tf_op jit(solution)/shard_map/ppermute | solution.py:22
  148.7 11.6 %collective-permute-start.28 = (bf16[128,768]{1,0:T(8,128)(2,1)S(1)}, bf16[128,768]{1,0:T(8,128)(2,1)S(1)}, u32[]{:S(2)}, u32[]{:S(2)}) collective-permute-start(bf16[128,768]{1,0:T(8,128)(2,1)S(1)} %dynamic-slice_convert_fusion.1), channel_id=1, source_target_pairs={{0,16},{16,0},{32,48},{48,32},{64,80},{80,64},{96,112},{112,96},{1... | collective-permute-start | bytes 589832 | tf_op jit(solution)/shard_map/ppermute | solution.py:26
  (25 other events, 212.9 us)
Sparse Core Ops, SparseCore 0:
  9.9 42.6 all-gather.2
  54.4 39.8 all-gather.4

commit v5 on v4

--- a/solution.py
+++ b/solution.py
@@ -14,6 +14,7 @@
 NZ = 8
 NX = 4
 TB = 128
+Z, YH, X, CORE, T = range(5)
 BEHIND = 4
 
 
@@ -56,11 +57,11 @@
 
 def unrotate_kernel(where_ref, own_ref, other_ref, cos_ref, sin_ref, up_attn_ref, down_attn_ref, up_ref, down_ref):
     even = lax.broadcasted_iota(jnp.int32, (TB, HD), 1) % 2 == 0
-    swapped = where_ref[0] == 1
+    swapped = where_ref[YH] == 1
     cols = own_ref.shape[1]
     for h in range(cols // HD):
         part = slice(h * HD, (h + 1) * HD)
-        rotated = where_ref[1] + h < HQ + HK
+        rotated = where_ref[T] * (cols // HD) + h < HQ + HK
         own, other = own_ref[:, part], other_ref[:, part]
         for half in range(2):
             rows = slice(half * TB, (half + 1) * TB)
@@ -76,7 +77,7 @@
     down_ref[:, 2 * cols :] = down_attn_ref[...]
 
 
-def unrotate(own, other, tables, up_attn, down_attn, yh, t):
+def unrotate(own, other, tables, up_attn, down_attn, spot):
     cols = own.shape[1]
     vmem = pl.BlockSpec(memory_space=pltpu.VMEM)
     shape = jax.ShapeDtypeStruct((TB, 2 * cols + up_attn.shape[1]), jnp.bfloat16)
@@ -86,10 +87,10 @@
         in_specs=[pl.BlockSpec(memory_space=pltpu.SMEM)] + [vmem] * 6,
         out_specs=(vmem, vmem),
         cost_estimate=pl.CostEstimate(flops=20 * TB * cols, bytes_accessed=16 * TB * cols, transcendentals=0),
-    )(jnp.stack([yh, t * (cols // HD)]).astype(jnp.int32), own, other, *tables, up_attn, down_attn)
-
-
-def place_first(block, z):
+    )(spot, own, other, *tables, up_attn, down_attn)
+
+
+def place_first(block, spot):
     def body(z_ref, block_ref, out_ref):
         out_ref[0] = block_ref[...]
 
@@ -101,24 +102,23 @@
             num_scalar_prefetch=1,
             grid=(1,),
             in_specs=[pl.BlockSpec((TB, n), lambda i, s: (0, 0))],
-            out_specs=pl.BlockSpec((1, TB, n), lambda i, s: (s[0], 0, 0)),
-        ),
-    )(jnp.reshape(z, (1,)).astype(jnp.int32), block)
-
-
-def absorb(blocks, q_places, a_places, z, core, weights, wholes):
+            out_specs=pl.BlockSpec((1, TB, n), lambda i, s: (s[Z], 0, 0)),
+        ),
+    )(spot, block)
+
+
+def absorb(blocks, q_places, a_places, spot, weights, wholes):
     count, with_attn = len(blocks), bool(a_places)
     width, cols = weights.shape
     attn_cols = blocks[0].shape[1] - 2 * cols
-    at = lambda p: (z + p + NZ) % NZ
-    where = jnp.stack([*map(at, q_places), core, *map(at, a_places or ())]).astype(jnp.int32)
-    q_spec = pl.BlockSpec((2, 1, TB, cols), lambda i, s: (0, s[i], 0, 0))
-    share = pl.BlockSpec((1, TB, width), lambda i, s: (s[i], 0, 0))
+    at = lambda places, i, s: lax.rem(s[Z] + NZ + jnp.where(i == 0, places[0], places[-1]), NZ)
+    q_spec = pl.BlockSpec((2, 1, TB, cols), lambda i, s: (0, at(q_places, i, s), 0, 0))
+    share = pl.BlockSpec((1, TB, width), lambda i, s: (at(q_places, i, s), 0, 0))
     out_specs = [q_spec, share, share]
     out_shape = [jax.ShapeDtypeStruct((2, NZ, TB, cols), jnp.bfloat16)]
     out_shape += [jax.ShapeDtypeStruct((NZ, TB, width), jnp.bfloat16)] * 2
     if with_attn:
-        out_specs.append(pl.BlockSpec((1, TB, attn_cols), lambda i, s: (s[count + 1 + i], 0, 0)))
+        out_specs.append(pl.BlockSpec((1, TB, attn_cols), lambda i, s: (at(a_places, i, s), 0, 0)))
         out_shape.append(jax.ShapeDtypeStruct((NZ, TB, attn_cols), jnp.bfloat16))
     operands = [*blocks, weights]
     in_specs = [pl.BlockSpec(v.shape, lambda i, s: (0, 0)) for v in operands]
@@ -133,7 +133,7 @@
     def body(where_ref, *refs):
         weights_ref = refs[count]
         outs = refs[-n_out:]
-        first = where_ref[count] == 0
+        first = where_ref[CORE] == 0
         for k in range(count):
 
             @pl.when(pl.program_id(0) == k)
@@ -159,13 +159,14 @@
             bytes_accessed=2 * width * cols + 4 * count * TB * (2 * cols + attn_cols + width),
             transcendentals=0,
         ),
-    )(where, *operands)
-
-
-def chip_parts(kept, sent, targets):
+    )(spot, *operands)
+
+
+def chip_parts(kept, sent, spot):
     n = kept.shape[2]
-    count = len(targets)
-    pair = pl.BlockSpec((2, TB, n), lambda i, s: (s[i], 0, 0))
+    count = NX
+    hops = lambda i: jnp.where(i < 2, i, NX + 1 - i)
+    pair = pl.BlockSpec((2, TB, n), lambda i, s: (lax.rem(s[X] + hops(i), NX), 0, 0))
 
     def body(where_ref, kept_ref, sent_ref, *outs):
         total = (kept_ref[...].astype(jnp.float32) + sent_ref[...].astype(jnp.float32)).astype(jnp.bfloat16)
@@ -185,10 +186,10 @@
             out_specs=(pl.BlockSpec((2 * TB, n), lambda i, s: (0, 0)),) * count,
         ),
         cost_estimate=pl.CostEstimate(flops=NZ * TB * n, bytes_accessed=6 * NZ * TB * n, transcendentals=0),
-    )(jnp.stack(targets).astype(jnp.int32), kept, sent)
-
-
-def contract_rows(halves, first, both, halves_left, factor, tile):
+    )(spot, kept, sent)
+
+
+def contract_rows(halves, turn, both, halves_left, factor, tile, spot):
     a, b = halves[0].shape[2], both.shape[1]
     m, n = (a, b) if halves_left else (b, a)
     half_tile, both_tile = (tile, b) if halves_left else (a, tile)
@@ -197,11 +198,12 @@
     else:
         moving = (lambda i, s: (0, 0, 0), lambda i, s: (0, 0, 0, i))
 
-    def body(first_ref, *refs):
+    def body(where_ref, *refs):
         both_ref, out_ref = refs[-2:]
+        first = where_ref[YH] if turn else 0
         total = jnp.zeros(out_ref.shape, jnp.float32)
         parts = [ref[k] for ref in refs[:-2] for k in range(ref.shape[0])]
-        for part, h in zip(parts, (first_ref[0], 1 - first_ref[0])):
+        for part, h in zip(parts, (first, 1 - first)):
             tokens = both_ref[:, h].reshape(NZ * TB, both_tile)
             pair = (part, tokens) if halves_left else (tokens, part)
             total += lax.dot_general(*pair, (((0,), (0,)), ((), ())), preferred_element_type=jnp.float32)
@@ -221,7 +223,7 @@
         cost_estimate=pl.CostEstimate(
             flops=4 * NZ * TB * m * n, bytes_accessed=4 * NZ * TB * (m + n) + 4 * m * n, transcendentals=0
         ),
-    )(jnp.reshape(first, (1,)).astype(jnp.int32), *halves, both.reshape(NZ, 2, TB, b))
+    )(spot, *halves, both.reshape(NZ, 2, TB, b))
 
 
 def contract_cols(left, right):
@@ -258,6 +260,7 @@
     d, t = lax.axis_index("dp"), lax.axis_index("tensor")
     z, yh = d // 2, d % 2
     x, yl, core = t // 4, t // 2 % 2, t % 2
+    spot = jnp.stack([z, yh, x, core, t]).astype(jnp.int32)
     factor = 1.0 / math.sqrt(NZ * 2 * TB)
 
     g_all = lax.all_gather(out_grad, "tensor", axis=0, tiled=True)
@@ -274,56 +277,57 @@
     window = jnp.concatenate([pair_ids, *near, far]).reshape(-1)
     tables = rotary_tables(pair_ids.reshape(-1), window, z)
 
-    up0, down0 = unrotate(qkv_grad, q_other, tables, up_attn, down_attn, yh, t)
+    up0, down0 = unrotate(qkv_grad, q_other, tables, up_attn, down_attn, spot)
     up1, down1 = tie(over_z(up0, 1), over_z(down0, -1))
 
-    attn_all = place_first(attn_out, z)
-    *shares, attn_all = absorb([up0, down0], [0, 0], [-1, 1], z, core, w_qkv, [None, None, None, attn_all])
-    *shares, attn_all = absorb([up1, down1], [-1, 1], [-2, 2], z, core, w_qkv, [*shares, attn_all])
+    attn_all = place_first(attn_out, spot)
+    *shares, attn_all = absorb([up0, down0], [0, 0], [-1, 1], spot, w_qkv, [None, None, None, attn_all])
+    *shares, attn_all = absorb([up1, down1], [-1, 1], [-2, 2], spot, w_qkv, [*shares, attn_all])
     up2, down2, attn_all, *shares = tie(over_z(up1, 1), over_z(down1, -1), attn_all, *shares)
 
-    *shares, attn_all = absorb([up2, down2], [-2, 2], [-3, 3], z, core, w_qkv, [*shares, attn_all])
+    *shares, attn_all = absorb([up2, down2], [-2, 2], [-3, 3], spot, w_qkv, [*shares, attn_all])
     attn_part = contract_cols(g_all, w_out).astype(jnp.bfloat16)
     up3, down3, attn_part, attn_all, *shares = tie(over_z(up2, 1), over_z(down2, -1), attn_part, attn_all, *shares)
 
     fold = Fold(attn_part, z)
     fold.step()
     last = over_z(up3[:, : 2 * qkv_grad.shape[1]], 1)
-    *shares, attn_all = absorb([up3, down3], [-3, 3], [4, 4], z, core, w_qkv, [*shares, attn_all])
+    *shares, attn_all = absorb([up3, down3], [-3, 3], [4, 4], spot, w_qkv, [*shares, attn_all])
     last, fold.down, attn_all, *shares = tie(last, fold.down, attn_all, *shares)
-    q_all, kept, given = absorb([last], [4], None, z, core, w_qkv, shares)
+    q_all, kept, given = absorb([last], [4], None, spot, w_qkv, shares)
 
     q_all = q_all.reshape(2, NZ * TB, -1)
     sent = over_core(given)
+    fold.step()
+    mine, ahead, behind, across = chip_parts(kept, sent, spot)
+    fold.up, fold.down, x_all, _ = tie(fold.up, fold.down, x_all, mine)
     attn_all = attn_all.reshape(1, NZ * TB, -1)
     attn_other = over_yh(attn_all)
-    fold.step()
-    mine, ahead, behind, across = chip_parts(kept, sent, [(x + k) % NX for k in (0, 1, 3, 2)])
-    fold.up, fold.down, x_all, _ = tie(fold.up, fold.down, x_all, mine)
     fold.step()
     a, b = over_x(across[:TB], 1), over_x(across[TB:], -1)
     plus = lambda part, got: (part.astype(jnp.float32) + got.astype(jnp.float32)).astype(jnp.bfloat16)
     ahead = jnp.concatenate([plus(ahead[:TB], a), ahead[TB:]])
     behind = jnp.concatenate([behind[:TB], plus(behind[TB:], b)])
     ahead, behind = tie(ahead, behind)
-    wqkv_grad = contract_rows([q_all], jnp.int32(0), x_all, False, factor, 256)
+    x_all, _ = tie(x_all, ahead)
+    wqkv_grad = contract_rows([q_all], False, x_all, False, factor, 256, spot)
     came1, came2 = over_x(ahead, 1), over_x(behind, -1)
-    came1, came2, attn_other = tie(came1, came2, attn_other)
     total = mine.astype(jnp.float32) + came1.astype(jnp.float32) + came2.astype(jnp.float32)
     keep = lax.dynamic_slice_in_dim(total, yl * TB, TB, 0)
     give = lax.dynamic_slice_in_dim(total, (1 - yl) * TB, TB, 0).astype(jnp.bfloat16)
     summed = keep + over_yl(give).astype(jnp.float32)
     input_grad = (out_grad.astype(jnp.float32) + summed).astype(jnp.bfloat16)
 
-    fold.up, fold.down, wqkv_grad, _ = tie(fold.up, fold.down, wqkv_grad, ahead)
+    fold.up, fold.down, _ = tie(fold.up, fold.down, ahead)
     fold.step()
+    fold.up, fold.down, wqkv_grad = tie(fold.up, fold.down, wqkv_grad)
     sums = fold.sums()
     keep = lax.dynamic_slice_in_dim(sums, yh * TB, TB, 0)
     send = lax.dynamic_slice_in_dim(sums, (1 - yh) * TB, TB, 0).astype(jnp.bfloat16)
     attn_grad = (keep + over_yh(send).astype(jnp.float32)).astype(jnp.bfloat16)
 
     attn_other, _, _ = tie(attn_other, give, send)
-    wout_grad = contract_rows([attn_all, attn_other], yh, g_all, True, factor, 256)
+    wout_grad = contract_rows([attn_all, attn_other], True, g_all, True, factor, 256, spot)
     return (input_grad, attn_grad, wqkv_grad, wout_grad)
 
 

time: 172 us -> 173 us (level)
  other arithmetic: 16.9 us -> 13.8 us
  Pallas kernels: 47.7 us -> 49.7 us
    ppermute x19, waiting for transfers between devices: 17.8 us -> 25.2 us  [over_z(): return lax.ppermute(value, 'dp', pairs)]
    ppermute x4, waiting for transfers between devices: 6.24 us -> 0.37 us  [over_x(): return lax.ppermute(value, 'tensor', pairs)]
    unnamed x36 -> x42, local copies, waits for them, and re-layouts: 4.28 us -> 6.6 us
    another operation x4 -> x1, local copies, waits for them, and re-layouts: 2.56 us -> 0.63 us  [shards(): spot = jnp.stack([z, yh, x, core, t]).astype(jnp.int32)]
    another operation x3 -> x0, other arithmetic: 1.84 us -> none  [the longest x1 0.67 us: unrotate(): jnp.stack([yh, t * (cols // HD)]).astype(jnp.int32)]
  transfers between devices with their start and end apart: 31 -> 31, of which waited for: 11 -> 10; matrix products, arithmetic and copies ran while one was open for 15% -> 14% of each run, Pallas kernels for 28% -> 29%
where the time goes in v5:
time: 173 us; the launch traced here: 171 us
  Pallas kernels  49.7 us (29%)
  starting transfers between devices  47.3 us (27%)
  waiting for transfers between devices  28.6 us (17%)
  between operations  14.3 us (8%)
  other arithmetic  13.8 us (8%)
  local copies, waits for them, and re-layouts  11.2 us (6%)
  matrix products  5.72 us (3%)
    ppermute x19, starting transfers between devices, over_z(): return lax.ppermute(value, 'dp', pairs)  32 us
    pallas_call x5, Pallas kernels, absorb(): pl.pallas_call(body, out_shape=tuple(out_shape), grid_spec=pltpu.Prefetch...  25.4 us
    ppermute x19, waiting for transfers between devices, over_z(): return lax.ppermute(value, 'dp', pairs)  25.2 us
    pallas_call x2, Pallas kernels, contract_rows(): pl.pallas_call(body, out_shape=jax.ShapeDtypeStruct((m, n), jnp.float32),...  13.8 us
    ppermute x4, starting transfers between devices, over_yh(): return lax.ppermute(value, 'dp', [(d, d ^ 1) for d in range(16)])  10 us
    unnamed x42, local copies, waits for them, and re-layouts  6.6 us
    convert_element_type x3, other arithmetic, add(): (part if got is None else part + got.astype(jnp.float32)).astype(jnp.bflo...  5.79 us
    dot_general x1, matrix products, contract_cols(): lax.dot_general(left, right, (((1,), (1,)), ((), ())), preferred_element_...  5.72 us
  transfers between devices with their start and end apart: 31, of which 10 were waited for; matrix products, arithmetic and copies ran while one was open for 14% of the time, Pallas kernels for 29%

profile of v5, /device:TPU:2, one launch (start us, length us, event | category | flops | bytes accessed | tf_op | source)
XLA Modules:
  0.0 170.6 jit_solution(3199889404302272343)
XLA Ops:
  8.7 3.3 %collective-permute-start.1 = (s32[1,128]{1,0:T(1,128)}, s32[1,128]{1,0:T(1,128)S(1)}, u32[]{:S(2)}, u32[]{:S(2)}) collective-permute-start(s32[1,128]{1,0:T(1,128)} %bitcast.21), channel_id=1, source_target_pairs={{0,16},{16,0},{32,48},{48,32},{64,80},{80,64},{96,112},{112,96},{1... | collective-permute-start | bytes 1544 | tf_op jit(solution)/shard_map/ppermute | solution.py:27
  16.6 3.3 %collective-permute-start.3 = (s32[2,128]{1,0:T(2,128)S(1)}, s32[2,128]{1,0:T(2,128)S(1)}, u32[]{:S(2)}, u32[]{:S(2)}) collective-permute-start(s32[2,128]{1,0:T(2,128)S(1)} %add_select_fusion), channel_id=1, source_target_pairs={{0,64},{16,80},{32,96},{48,112},{64,128},{80,144},{96,160},{112,17... | collective-permute-start | bytes 3080 | tf_op jit(solution)/shard_map/ppermute | solution.py:23
  20.5 3.1 %collective-permute-start.5 = (bf16[128,768]{1,0:T(8,128)(2,1)}, bf16[128,768]{1,0:T(8,128)(2,1)S(1)}, u32[]{:S(2)}, u32[]{:S(2)}) collective-permute-start(bf16[128,768]{1,0:T(8,128)(2,1)} %block_ref.1), channel_id=1, source_target_pairs={{0,32},{16,48},{32,64},{48,80},{64,96},{80,112},{96,128},{112,144}... | collective-permute-start | bytes 589832 | tf_op jit(solution)/shard_map/ppermute | solution.py:23
  23.7 2.4 %collective-permute-start.4 = (s32[4,128]{1,0:T(4,128)S(1)}, s32[4,128]{1,0:T(4,128)S(1)}, u32[]{:S(2)}, u32[]{:S(2)}) collective-permute-start(s32[4,128]{1,0:T(4,128)S(1)} %pad_add_fusion), channel_id=1, source_target_pairs={{0,64},{16,80},{32,96},{48,112},{64,128},{80,144},{96,160},{112,17... | collective-permute-start | bytes 6152 | tf_op jit(solution)/shard_map/ppermute | solution.py:23
  26.9 2.6 %collective-permute-done.4 = s32[4,128]{1,0:T(4,128)S(1)} collective-permute-done((s32[4,128]{1,0:T(4,128)S(1)}, s32[4,128]{1,0:T(4,128)S(1)}, u32[]{:S(2)}, u32[]{:S(2)}) %collective-permute-start.4) | collective-permute-done | bytes 2080 | tf_op jit(solution)/shard_map/ppermute | solution.py:23
  31.9 2.8 %shard_map.102 = (bf16[128,2560]{1,0:T(8,128)(2,1)}, bf16[128,2560]{1,0:T(8,128)(2,1)}) custom-call(s32[5]{0:T(128)} %stack.23.where_ref.z_ref, bf16[128,896]{1,0:T(8,128)(2,1)} %own_ref.1, bf16[128,896]{1,0:T(8,128)(2,1)} %copy-done.18, f32[256,128]{1,0:T(8,128)} %get-tuple-element.131.cos_ref, f32[256,128]{1,0:T(8,128)} %get-tuple-element.130.sin_ref, ...), custom_call_target="tpu_custom_call" | custom-call | flops 2293760 | bytes 1835008 | tf_op jit(solution)/shard_map/pallas_call | solution.py:84
  37.9 11.5 %collective-permute-done.7.refs_0_ = bf16[128,2560]{1,0:T(8,128)(2,1)S(1)} collective-permute-done((bf16[128,2560]{1,0:T(8,128)(2,1)}, bf16[128,2560]{1,0:T(8,128)(2,1)S(1)}, u32[]{:S(2)}, u32[]{:S(2)}) %collective-permute-start.7) | collective-permute-done | bytes 655392 | tf_op jit(solution)/shard_map/ppermute | solution.py:23
  53.4 2.3 %shard_map.103.refs_3_ = bf16[8,128,768]{2,1,0:T(8,128)(2,1)} custom-call(s32[5]{0:T(128)} %stack.23.where_ref.z_ref, bf16[128,768]{1,0:T(8,128)(2,1)} %block_ref.1), custom_call_target="tpu_custom_call" | custom-call | tf_op jit(solution)/shard_map/pallas_call | solution.py:98
  55.7 5.2 %shard_map.104 = (bf16[2,8,128,896]{3,2,1,0:T(8,128)(2,1)}, bf16[8,128,1024]{2,1,0:T(8,128)(2,1)}, bf16[8,128,1024]{2,1,0:T(8,128)(2,1)}, bf16[8,128,768]{2,1,0:T(8,128)(2,1)}) custom-call(s32[5]{0:T(128)} %stack.23.where_ref.z_ref, bf16[128,2560]{1,0:T(8,128)(2,1)} %get-tuple-element.64.refs_0_, ...), custom_call_target="tpu_custom_call", output_to_operand_aliasing={{3}: (4, {})} | custom-call | flops 939524096 | bytes 5505024 | tf_op jit(solution)/shard_map/pallas_call | solution.py:149
  60.9 5.3 %shard_map.105 = (bf16[2,8,128,896]{3,2,1,0:T(8,128)(2,1)}, bf16[8,128,1024]{2,1,0:T(8,128)(2,1)}, bf16[8,128,1024]{2,1,0:T(8,128)(2,1)}, bf16[8,128,768]{2,1,0:T(8,128)(2,1)}) custom-call(s32[5]{0:T(128)} %stack.23.where_ref.z_ref, bf16[128,2560]{1,0:T(8,128)(2,1)} %copy-done.11, ...), custom_call_target="tpu_custom_call", output_to_operand_aliasing={{0}: (4, {}), {1}: (5, {}), {2}: (6, {}), {3}: (7, {})} | custom-call | flops 939524096 | bytes 5505024 | tf_op jit(solution)/shard_map/pallas_call | solution.py:149
  66.5 3.2 %collective-permute-start.12 = (bf16[128,2560]{1,0:T(8,128)(2,1)S(1)}, bf16[128,2560]{1,0:T(8,128)(2,1)}, u32[]{:S(2)}, u32[]{:S(2)}) collective-permute-start(bf16[128,2560]{1,0:T(8,128)(2,1)S(1)} %collective-permute-done.10.refs_1_), channel_id=1, source_target_pairs={{0,224},{16,240},{32,0},{48,16},{64,32},{80,48},{96,64},{112,80},{... | collective-permute-start | bytes 1966088 | tf_op jit(solution)/shard_map/ppermute | solution.py:23
  69.7 5.4 %shard_map.106 = (bf16[2,8,128,896]{3,2,1,0:T(8,128)(2,1)}, bf16[8,128,1024]{2,1,0:T(8,128)(2,1)}, bf16[8,128,1024]{2,1,0:T(8,128)(2,1)}, bf16[8,128,768]{2,1,0:T(8,128)(2,1)}) custom-call(s32[5]{0:T(128)} %stack.23.where_ref.z_ref, bf16[128,2560]{1,0:T(8,128)(2,1)} %copy-done.10, ...), custom_call_target="tpu_custom_call", output_to_operand_aliasing={{0}: (4, {}), {1}: (5, {}), {2}: (6, {}), {3}: (7, {})} | custom-call | flops 939524096 | bytes 5505024 | tf_op jit(solution)/shard_map/pallas_call | solution.py:149
  75.1 5.7 %convolution_convert_fusion = bf16[2048,768]{1,0:T(8,128)(2,1)S(1)} fusion(bf16[2048,1024]{1,0:T(8,128)(2,1)} %all-gather.3.cloned.1.call-done, bf16[768,1024]{1,0:T(8,128)(2,1)S(1)} %copy-done), kind=kOutput, calls=%fused_computation | convolution fusion | flops 3222798336 | bytes 8912896 | tf_op jit(solution)/shard_map/dot_general | solution.py:230
  85.0 5.3 %shard_map.107 = (bf16[2,8,128,896]{3,2,1,0:T(8,128)(2,1)}, bf16[8,128,1024]{2,1,0:T(8,128)(2,1)}, bf16[8,128,1024]{2,1,0:T(8,128)(2,1)}, bf16[8,128,768]{2,1,0:T(8,128)(2,1)}) custom-call(s32[5]{0:T(128)} %stack.23.where_ref.z_ref, bf16[128,2560]{1,0:T(8,128)(2,1)} %copy-done.7, ...), custom_call_target="tpu_custom_call", output_to_operand_aliasing={{0}: (4, {}), {1}: (5, {}), {2}: (6, {}), {3}: (7, {})} | custom-call | flops 939524096 | bytes 5505024 | tf_op jit(solution)/shard_map/pallas_call | solution.py:149
  92.0 4.2 %shard_map.108 = (bf16[2,8,128,896]{3,2,1,0:T(8,128)(2,1)}, bf16[8,128,1024]{2,1,0:T(8,128)(2,1)}, bf16[8,128,1024]{2,1,0:T(8,128)(2,1)}) custom-call(s32[5]{0:T(128)} %stack.23.where_ref.z_ref, bf16[128,1792]{1,0:T(8,128)(2,1)} %copy-done.15, bf16[1024,896]{1,0:T(8,128)(2,1)} %refs_1_.1, ...), custom_call_target="tpu_custom_call", output_to_operand_aliasing={{0}: (3, {}), {1}: (4, {}), {2}: (5, {})} | custom-call | flops 469762048 | bytes 3276800 | tf_op jit(solution)/shard_map/pallas_call | solution.py:149
  101.4 3.1 %collective-permute-start.28 = (bf16[1,1024,768]{2,1,0:T(8,128)(2,1)S(1)}, bf16[1,1024,768]{2,1,0:T(8,128)(2,1)}, u32[]{:S(2)}, u32[]{:S(2)}) collective-permute-start(bf16[1,1024,768]{2,1,0:T(8,128)(2,1)S(1)} %bitcast.17), channel_id=1, source_target_pairs={{0,16},{16,0},{32,48},{48,32},{64,80},{80,64},{96,112},{112,96},{1... | collective-permute-start | bytes 4718600 | tf_op jit(solution)/shard_map/ppermute | solution.py:27
  104.5 5.4 %shard_map.109 = (bf16[256,1024]{1,0:T(8,128)(2,1)}, bf16[256,1024]{1,0:T(8,128)(2,1)}, bf16[256,1024]{1,0:T(8,128)(2,1)}, bf16[256,1024]{1,0:T(8,128)(2,1)}) custom-call(s32[5]{0:T(128)} %stack.23.where_ref.z_ref, bf16[8,128,1024]{2,1,0:T(8,128)(2,1)} %get-tuple-element.101.kept_ref, bf16[8,128,1024]{2,1,0:T(8,128)(2,1)} %collective-permute-done.15.sent_ref), custom_call_target="tpu_custom_call" | custom-call | flops 1048576 | bytes 6291456 | tf_op jit(solution)/shard_map/pallas_call | solution.py:179
  118.2 2.8 %collective-permute-start.23 = (bf16[256,768]{1,0:T(8,128)(2,1)S(1)}, bf16[256,768]{1,0:T(8,128)(2,1)S(1)}, u32[]{:S(2)}, u32[]{:S(2)}) collective-permute-start(bf16[256,768]{1,0:T(8,128)(2,1)S(1)} %get-tuple-element.125), channel_id=1, source_target_pairs={{0,32},{16,48},{32,64},{48,80},{64,96},{80,112},{96,128},{112,144}... | collective-permute-start | bytes 1179656 | tf_op jit(solution)/shard_map/ppermute | solution.py:23
  123.7 5.9 %collective-permute-done.23 = bf16[256,768]{1,0:T(8,128)(2,1)S(1)} collective-permute-done((bf16[256,768]{1,0:T(8,128)(2,1)S(1)}, bf16[256,768]{1,0:T(8,128)(2,1)S(1)}, u32[]{:S(2)}, u32[]{:S(2)}) %collective-permute-start.23) | collective-permute-done | bytes 393248 | tf_op jit(solution)/shard_map/ppermute | solution.py:23
  130.8 2.2 %add_convert_fusion = (bf16[256,768]{1,0:T(8,128)(2,1)}, bf16[256,768]{1,0:T(8,128)(2,1)}) fusion(bf16[256,768]{1,0:T(8,128)(2,1)S(1)} %collective-permute-done.24, bf16[2048,768]{1,0:T(8,128)(2,1)} %copy-done.6, s32[]{:T(128)S(6)} %select_n.164, bf16[256,768]{1,0:T(8,128)(2,1)S(1)} %collective-permute-done.23, s32[]{:T(128)S(6)} %select_n.154), kind=kLoop, calls=%fused_computation.4 | loop fusion | flops 1572864 | bytes 2359304 | tf_op jit(solution)/shard_map/convert_element_type | solution.py:246
  140.3 2.2 %copy-done.5 = bf16[2048,1024]{1,0:T(8,128)(2,1)S(1)} copy-done((bf16[2048,1024]{1,0:T(8,128)(2,1)S(1)}, bf16[2048,1024]{1,0:T(8,128)(2,1)}, u32[]{:S(2)}) %copy-start.5) | copy-done | bytes 4194328
  142.5 7.2 %shard_map.110 = f32[1024,896]{1,0:T(8,128)} custom-call(s32[5]{0:T(128)S(1)} %copy-done.3, bf16[2,1024,896]{2,1,0:T(8,128)(2,1)S(1)} %bitcast.16, bf16[8,2,128,1024]{3,2,1,0:T(8,128)(2,1)S(1)} %bitcast.20), custom_call_target="tpu_custom_call" | custom-call | flops 3758096384 | bytes 11534336 | tf_op jit(solution)/shard_map/pallas_call | solution.py:212
  151.2 3.3 %collective-permute-start.27 = (bf16[128,768]{1,0:T(8,128)(2,1)S(1)}, bf16[128,768]{1,0:T(8,128)(2,1)S(1)}, u32[]{:S(2)}, u32[]{:S(2)}) collective-permute-start(bf16[128,768]{1,0:T(8,128)(2,1)S(1)} %dynamic-slice_convert_fusion.1), channel_id=1, source_target_pairs={{0,16},{16,0},{32,48},{48,32},{64,80},{80,64},{96,112},{112,96},{1... | collective-permute-start | bytes 589832 | tf_op jit(solution)/shard_map/ppermute | solution.py:27
  155.6 6.6 %shard_map.111 = f32[768,1024]{1,0:T(8,128)} custom-call(s32[5]{0:T(128)S(1)} %copy-done.3, bf16[1,1024,768]{2,1,0:T(8,128)(2,1)S(1)} %bitcast.18, bf16[1,1024,768]{2,1,0:T(8,128)(2,1)} %collective-permute-done.28.refs_1_, bf16[8,2,128,1024]{3,2,1,0:T(8,128)(2,1)S(1)} %bitcast.19), custom_call_target="tpu_custom_call" | custom-call | flops 3221225472 | bytes 10485760 | tf_op jit(solution)/shard_map/pallas_call | solution.py:212
  (120 shorter events, 52.0 us)
Async XLA Ops:
  7.2 67.9 %all-gather.3.cloned.1.call-start = ((), (), s32[]{:S(2)}) async-start(), calls=%async_computation | async-start | bytes 4456448 | tf_op jit(solution)/shard_map/all_gather | solution.py:266
  7.9 102.0 %all-gather.5.cloned.1.call-start = ((), (), s32[]{:S(2)}) async-start(), calls=%async_computation.1 | async-start | bytes 4456448 | tf_op jit(solution)/shard_map/all_gather | solution.py:267
  11.9 19.1 %collective-permute-start = (bf16[128,896]{1,0:T(8,128)(2,1)}, bf16[128,896]{1,0:T(8,128)(2,1)S(1)}, u32[]{:S(2)}, u32[]{:S(2)}) collective-permute-start(bf16[128,896]{1,0:T(8,128)(2,1)} %own_ref.1), channel_id=1, source_target_pairs={{0,16},{16,0},{32,48},{48,32},{64,80},{80,64},{96,112},{112,96},{1... | collective-permute-start | bytes 688136 | tf_op jit(solution)/shard_map/ppermute | solution.py:27
  14.7 9.1 %collective-permute-start.2 = (s32[2,128]{1,0:T(2,128)S(1)}, s32[2,128]{1,0:T(2,128)S(1)}, u32[]{:S(2)}, u32[]{:S(2)}) collective-permute-start(s32[2,128]{1,0:T(2,128)S(1)} %add_select_fusion), channel_id=1, source_target_pairs={{0,32},{16,48},{32,64},{48,80},{64,96},{80,112},{96,128},{112,144}... | collective-permute-start | bytes 3080 | tf_op jit(solution)/shard_map/ppermute | solution.py:23
  20.5 10.6 %collective-permute-start.5 = (bf16[128,768]{1,0:T(8,128)(2,1)}, bf16[128,768]{1,0:T(8,128)(2,1)S(1)}, u32[]{:S(2)}, u32[]{:S(2)}) collective-permute-start(bf16[128,768]{1,0:T(8,128)(2,1)} %block_ref.1), channel_id=1, source_target_pairs={{0,32},{16,48},{32,64},{48,80},{64,96},{80,112},{96,128},{112,144}... | collective-permute-start | bytes 589832 | tf_op jit(solution)/shard_map/ppermute | solution.py:23
  34.7 14.7 %collective-permute-start.7 = (bf16[128,2560]{1,0:T(8,128)(2,1)}, bf16[128,2560]{1,0:T(8,128)(2,1)S(1)}, u32[]{:S(2)}, u32[]{:S(2)}) collective-permute-start(bf16[128,2560]{1,0:T(8,128)(2,1)} %get-tuple-element.64.refs_0_), channel_id=1, source_target_pairs={{0,32},{16,48},{32,64},{48,80},{64,96},{80,112},{96,128},{112,144}... | collective-permute-start | bytes 1966088 | tf_op jit(solution)/shard_map/ppermute | solution.py:23
  36.6 14.8 %collective-permute-start.8 = (bf16[128,2560]{1,0:T(8,128)(2,1)}, bf16[128,2560]{1,0:T(8,128)(2,1)}, u32[]{:S(2)}, u32[]{:S(2)}) collective-permute-start(bf16[128,2560]{1,0:T(8,128)(2,1)} %get-tuple-element.65.refs_1_), channel_id=1, source_target_pairs={{0,224},{16,240},{32,0},{48,16},{64,32},{80,48},{96,64},{112,80},{... | collective-permute-start | bytes 1966088 | tf_op jit(solution)/shard_map/ppermute | solution.py:23
  51.4 14.8 %collective-permute-start.10 = (bf16[128,2560]{1,0:T(8,128)(2,1)}, bf16[128,2560]{1,0:T(8,128)(2,1)S(1)}, u32[]{:S(2)}, u32[]{:S(2)}) collective-permute-start(bf16[128,2560]{1,0:T(8,128)(2,1)} %collective-permute-done.8.refs_1_), channel_id=1, source_target_pairs={{0,224},{16,240},{32,0},{48,16},{64,32},{80,48},{96,64},{112,80},{... | collective-permute-start | bytes 1966088 | tf_op jit(solution)/shard_map/ppermute | solution.py:23
  52.8 13.5 %collective-permute-start.9 = (bf16[128,2560]{1,0:T(8,128)(2,1)S(1)}, bf16[128,2560]{1,0:T(8,128)(2,1)S(1)}, u32[]{:S(2)}, u32[]{:S(2)}) collective-permute-start(bf16[128,2560]{1,0:T(8,128)(2,1)S(1)} %collective-permute-done.7.refs_0_), channel_id=1, source_target_pairs={{0,32},{16,48},{32,64},{48,80},{64,96},{80,112},{96,128},{112,144}... | collective-permute-start | bytes 1966088 | tf_op jit(solution)/shard_map/ppermute | solution.py:23
  66.4 14.5 %collective-permute-start.11 = (bf16[128,2560]{1,0:T(8,128)(2,1)S(1)}, bf16[128,2560]{1,0:T(8,128)(2,1)S(1)}, u32[]{:S(2)}, u32[]{:S(2)}) collective-permute-start(bf16[128,2560]{1,0:T(8,128)(2,1)S(1)} %collective-permute-done.9.refs_0_), channel_id=1, source_target_pairs={{0,32},{16,48},{32,64},{48,80},{64,96},{80,112},{96,128},{112,144}... | collective-permute-start | bytes 1966088 | tf_op jit(solution)/shard_map/ppermute | solution.py:23
  66.5 14.4 %collective-permute-start.12 = (bf16[128,2560]{1,0:T(8,128)(2,1)S(1)}, bf16[128,2560]{1,0:T(8,128)(2,1)}, u32[]{:S(2)}, u32[]{:S(2)}) collective-permute-start(bf16[128,2560]{1,0:T(8,128)(2,1)S(1)} %collective-permute-done.10.refs_1_), channel_id=1, source_target_pairs={{0,224},{16,240},{32,0},{48,16},{64,32},{80,48},{96,64},{112,80},{... | collective-permute-start | bytes 1966088 | tf_op jit(solution)/shard_map/ppermute | solution.py:23
  80.9 10.2 %collective-permute-start.13 = (bf16[128,1792]{1,0:T(8,128)(2,1)S(1)}, bf16[128,1792]{1,0:T(8,128)(2,1)S(1)}, u32[]{:S(2)}, u32[]{:S(2)}) collective-permute-start(bf16[128,1792]{1,0:T(8,128)(2,1)S(1)} %slice.21), channel_id=1, source_target_pairs={{0,32},{16,48},{32,64},{48,80},{64,96},{80,112},{96,128},{112,144}... | collective-permute-start | bytes 1376264 | tf_op jit(solution)/shard_map/ppermute | solution.py:23
  96.1 13.8 %collective-permute-start.21 = (bf16[256,768]{1,0:T(8,128)(2,1)S(1)}, bf16[256,768]{1,0:T(8,128)(2,1)}, u32[]{:S(2)}, u32[]{:S(2)}) collective-permute-start(bf16[256,768]{1,0:T(8,128)(2,1)S(1)} %copy-done.16), channel_id=1, source_target_pairs={{0,32},{16,48},{32,64},{48,80},{64,96},{80,112},{96,128},{112,144}... | collective-permute-start | bytes 1179656 | tf_op jit(solution)/shard_map/ppermute | solution.py:23
  99.3 11.8 %collective-permute-start.22 = (bf16[256,768]{1,0:T(8,128)(2,1)}, bf16[256,768]{1,0:T(8,128)(2,1)}, u32[]{:S(2)}, u32[]{:S(2)}) collective-permute-start(bf16[256,768]{1,0:T(8,128)(2,1)} %add_convert_fusion.4), channel_id=1, source_target_pairs={{0,224},{16,240},{32,0},{48,16},{64,32},{80,48},{96,64},{112,80},{... | collective-permute-start | bytes 1179656 | tf_op jit(solution)/shard_map/ppermute | solution.py:23
  101.4 54.2 %collective-permute-start.28 = (bf16[1,1024,768]{2,1,0:T(8,128)(2,1)S(1)}, bf16[1,1024,768]{2,1,0:T(8,128)(2,1)}, u32[]{:S(2)}, u32[]{:S(2)}) collective-permute-start(bf16[1,1024,768]{2,1,0:T(8,128)(2,1)S(1)} %bitcast.17), channel_id=1, source_target_pairs={{0,16},{16,0},{32,48},{48,32},{64,80},{80,64},{96,112},{112,96},{1... | collective-permute-start | bytes 4718600 | tf_op jit(solution)/shard_map/ppermute | solution.py:27
  112.2 9.3 %collective-permute-start.17 = (bf16[128,1024]{1,0:T(8,128)(2,1)S(1)}, bf16[128,1024]{1,0:T(8,128)(2,1)S(1)}, u32[]{:S(2)}, u32[]{:S(2)}) collective-permute-start(bf16[128,1024]{1,0:T(8,128)(2,1)S(1)} %get-tuple-element.128), channel_id=1, source_target_pairs={{0,12},{1,13},{2,14},{3,15},{4,0},{5,1},{6,2},{7,3},{8,4},{9,5},{1... | collective-permute-start | bytes 786440 | tf_op jit(solution)/shard_map/ppermute | solution.py:32
  114.0 8.7 %collective-permute-start.16 = (bf16[128,1024]{1,0:T(8,128)(2,1)S(1)}, bf16[128,1024]{1,0:T(8,128)(2,1)S(1)}, u32[]{:S(2)}, u32[]{:S(2)}) collective-permute-start(bf16[128,1024]{1,0:T(8,128)(2,1)S(1)} %get-tuple-element.129), channel_id=1, source_target_pairs={{0,4},{1,5},{2,6},{3,7},{4,8},{5,9},{6,10},{7,11},{8,12},{9,13},{1... | collective-permute-start | bytes 786440 | tf_op jit(solution)/shard_map/ppermute | solution.py:32
  118.2 11.4 %collective-permute-start.23 = (bf16[256,768]{1,0:T(8,128)(2,1)S(1)}, bf16[256,768]{1,0:T(8,128)(2,1)S(1)}, u32[]{:S(2)}, u32[]{:S(2)}) collective-permute-start(bf16[256,768]{1,0:T(8,128)(2,1)S(1)} %get-tuple-element.125), channel_id=1, source_target_pairs={{0,32},{16,48},{32,64},{48,80},{64,96},{80,112},{96,128},{112,144}... | collective-permute-start | bytes 1179656 | tf_op jit(solution)/shard_map/ppermute | solution.py:23
  120.9 9.9 %collective-permute-start.24 = (bf16[256,768]{1,0:T(8,128)(2,1)S(1)}, bf16[256,768]{1,0:T(8,128)(2,1)S(1)}, u32[]{:S(2)}, u32[]{:S(2)}) collective-permute-start(bf16[256,768]{1,0:T(8,128)(2,1)S(1)} %get-tuple-element.124), channel_id=1, source_target_pairs={{0,224},{16,240},{32,0},{48,16},{64,32},{80,48},{96,64},{112,80},{... | collective-permute-start | bytes 1179656 | tf_op jit(solution)/shard_map/ppermute | solution.py:23
  133.0 16.7 %collective-permute-start.25 = (bf16[256,768]{1,0:T(8,128)(2,1)}, bf16[256,768]{1,0:T(8,128)(2,1)S(1)}, u32[]{:S(2)}, u32[]{:S(2)}) collective-permute-start(bf16[256,768]{1,0:T(8,128)(2,1)} %get-tuple-element.123), channel_id=1, source_target_pairs={{0,32},{16,48},{32,64},{48,80},{64,96},{80,112},{96,128},{112,144}... | collective-permute-start | bytes 1179656 | tf_op jit(solution)/shard_map/ppermute | solution.py:23
  134.4 15.3 %collective-permute-start.26 = (bf16[256,768]{1,0:T(8,128)(2,1)}, bf16[256,768]{1,0:T(8,128)(2,1)}, u32[]{:S(2)}, u32[]{:S(2)}) collective-permute-start(bf16[256,768]{1,0:T(8,128)(2,1)} %get-tuple-element.122), channel_id=1, source_target_pairs={{0,224},{16,240},{32,0},{48,16},{64,32},{80,48},{96,64},{112,80},{... | collective-permute-start | bytes 1179656 | tf_op jit(solution)/shard_map/ppermute | solution.py:23
  136.3 18.3 %collective-permute-start.18 = (bf16[256,1024]{1,0:T(8,128)(2,1)}, bf16[256,1024]{1,0:T(8,128)(2,1)S(1)}, u32[]{:S(2)}, u32[]{:S(2)}) collective-permute-start(bf16[256,1024]{1,0:T(8,128)(2,1)} %pad_maximum_fusion), channel_id=1, source_target_pairs={{0,4},{1,5},{2,6},{3,7},{4,8},{5,9},{6,10},{7,11},{8,12},{9,13},{1... | collective-permute-start | bytes 1572872 | tf_op jit(solution)/shard_map/ppermute | solution.py:32
  137.8 16.7 %collective-permute-start.19 = (bf16[256,1024]{1,0:T(8,128)(2,1)}, bf16[256,1024]{1,0:T(8,128)(2,1)S(1)}, u32[]{:S(2)}, u32[]{:S(2)}) collective-permute-start(bf16[256,1024]{1,0:T(8,128)(2,1)} %pad_maximum_fusion.1), channel_id=1, source_target_pairs={{0,12},{1,13},{2,14},{3,15},{4,0},{5,1},{6,2},{7,3},{8,4},{9,5},{1... | collective-permute-start | bytes 1572872 | tf_op jit(solution)/shard_map/ppermute | solution.py:32
  151.2 11.0 %collective-permute-start.27 = (bf16[128,768]{1,0:T(8,128)(2,1)S(1)}, bf16[128,768]{1,0:T(8,128)(2,1)S(1)}, u32[]{:S(2)}, u32[]{:S(2)}) collective-permute-start(bf16[128,768]{1,0:T(8,128)(2,1)S(1)} %dynamic-slice_convert_fusion.1), channel_id=1, source_target_pairs={{0,16},{16,0},{32,48},{48,32},{64,80},{80,64},{96,112},{112,96},{1... | collective-permute-start | bytes 589832 | tf_op jit(solution)/shard_map/ppermute | solution.py:27
  (28 other events, 214.2 us)
Sparse Core Ops, SparseCore 0:
  9.9 42.6 all-gather.2
  54.4 40.0 all-gather.4

commit v6 on v5

--- a/solution.py
+++ b/solution.py
@@ -219,7 +219,7 @@
             + [pl.BlockSpec((NZ, 2, TB, both_tile), moving[1])],
             out_specs=pl.BlockSpec((tile, n), lambda i, s: (i, 0)),
         ),
-        compiler_params=pltpu.CompilerParams(vmem_limit_bytes=40 * 2**20),
+        compiler_params=pltpu.CompilerParams(vmem_limit_bytes=(40 if turn else 60) * 2**20),
         cost_estimate=pl.CostEstimate(
             flops=4 * NZ * TB * m * n, bytes_accessed=4 * NZ * TB * (m + n) + 4 * m * n, transcendentals=0
         ),

time: 173 us -> 172 us (level)
  local copies, waits for them, and re-layouts: 11.2 us -> 6.93 us
  Pallas kernels: 49.7 us -> 51.9 us
    unnamed x42 -> x38, local copies, waits for them, and re-layouts: 6.6 us -> 2.38 us
    pallas_call x2, Pallas kernels: 13.8 us -> 16.1 us  [contract_rows(): pl.pallas_call(body, out_shape=jax.ShapeDtypeStruct((m, n), jnp.float32),...]
  transfers between devices with their start and end apart: 31 -> 31, of which waited for: 10 -> 10; matrix products, arithmetic and copies ran while one was open for 14% -> 14% of each run, Pallas kernels for 29% -> 31%
where the time goes in v6:
time: 172 us; the launch traced here: 170 us
  Pallas kernels  51.9 us (30%)
  starting transfers between devices  47.3 us (28%)
  waiting for transfers between devices  28.7 us (17%)
  other arithmetic  14.8 us (9%)
  between operations  14.3 us (8%)
  local copies, waits for them, and re-layouts  6.93 us (4%)
  matrix products  5.71 us (3%)
    ppermute x19, starting transfers between devices, over_z(): return lax.ppermute(value, 'dp', pairs)  32 us
    ppermute x19, waiting for transfers between devices, over_z(): return lax.ppermute(value, 'dp', pairs)  25.4 us
    pallas_call x5, Pallas kernels, absorb(): pl.pallas_call(body, out_shape=tuple(out_shape), grid_spec=pltpu.Prefetch...  25.4 us
    pallas_call x2, Pallas kernels, contract_rows(): pl.pallas_call(body, out_shape=jax.ShapeDtypeStruct((m, n), jnp.float32),...  16.1 us
    ppermute x4, starting transfers between devices, over_yh(): return lax.ppermute(value, 'dp', [(d, d ^ 1) for d in range(16)])  10.1 us
    convert_element_type x3, other arithmetic, add(): (part if got is None else part + got.astype(jnp.float32)).astype(jnp.bflo...  5.77 us
    dot_general x1, matrix products, contract_cols(): lax.dot_general(left, right, (((1,), (1,)), ((), ())), preferred_element_...  5.71 us
    pallas_call x1, Pallas kernels, chip_parts(): pl.pallas_call(body, out_shape=(jax.ShapeDtypeStruct((2 * TB, n), jnp.bfl...  5.36 us
  transfers between devices with their start and end apart: 31, of which 10 were waited for; matrix products, arithmetic and copies ran while one was open for 14% of the time, Pallas kernels for 31%

profile of v6, /device:TPU:2, one launch (start us, length us, event | category | flops | bytes accessed | tf_op | source)
XLA Modules:
  0.0 169.7 jit_solution(6380883279077023038)
XLA Ops:
  8.7 3.3 %collective-permute-start.1 = (s32[1,128]{1,0:T(1,128)}, s32[1,128]{1,0:T(1,128)S(1)}, u32[]{:S(2)}, u32[]{:S(2)}) collective-permute-start(s32[1,128]{1,0:T(1,128)} %bitcast.20), channel_id=1, source_target_pairs={{0,16},{16,0},{32,48},{48,32},{64,80},{80,64},{96,112},{112,96},{1... | collective-permute-start | bytes 1544 | tf_op jit(solution)/shard_map/ppermute | solution.py:27
  16.6 3.3 %collective-permute-start.3 = (s32[2,128]{1,0:T(2,128)S(1)}, s32[2,128]{1,0:T(2,128)S(1)}, u32[]{:S(2)}, u32[]{:S(2)}) collective-permute-start(s32[2,128]{1,0:T(2,128)S(1)} %add_select_fusion), channel_id=1, source_target_pairs={{0,64},{16,80},{32,96},{48,112},{64,128},{80,144},{96,160},{112,17... | collective-permute-start | bytes 3080 | tf_op jit(solution)/shard_map/ppermute | solution.py:23
  20.4 3.1 %collective-permute-start.5 = (bf16[128,768]{1,0:T(8,128)(2,1)}, bf16[128,768]{1,0:T(8,128)(2,1)S(1)}, u32[]{:S(2)}, u32[]{:S(2)}) collective-permute-start(bf16[128,768]{1,0:T(8,128)(2,1)} %block_ref.1), channel_id=1, source_target_pairs={{0,32},{16,48},{32,64},{48,80},{64,96},{80,112},{96,128},{112,144}... | collective-permute-start | bytes 589832 | tf_op jit(solution)/shard_map/ppermute | solution.py:23
  23.7 2.4 %collective-permute-start.4 = (s32[4,128]{1,0:T(4,128)S(1)}, s32[4,128]{1,0:T(4,128)S(1)}, u32[]{:S(2)}, u32[]{:S(2)}) collective-permute-start(s32[4,128]{1,0:T(4,128)S(1)} %pad_add_fusion), channel_id=1, source_target_pairs={{0,64},{16,80},{32,96},{48,112},{64,128},{80,144},{96,160},{112,17... | collective-permute-start | bytes 6152 | tf_op jit(solution)/shard_map/ppermute | solution.py:23
  26.9 2.6 %collective-permute-done.4 = s32[4,128]{1,0:T(4,128)S(1)} collective-permute-done((s32[4,128]{1,0:T(4,128)S(1)}, s32[4,128]{1,0:T(4,128)S(1)}, u32[]{:S(2)}, u32[]{:S(2)}) %collective-permute-start.4) | collective-permute-done | bytes 2080 | tf_op jit(solution)/shard_map/ppermute | solution.py:23
  31.9 2.8 %shard_map.102 = (bf16[128,2560]{1,0:T(8,128)(2,1)}, bf16[128,2560]{1,0:T(8,128)(2,1)}) custom-call(s32[5]{0:T(128)} %stack.23.where_ref.z_ref, bf16[128,896]{1,0:T(8,128)(2,1)} %own_ref.1, bf16[128,896]{1,0:T(8,128)(2,1)} %copy-done.16, f32[256,128]{1,0:T(8,128)} %get-tuple-element.131.cos_ref, f32[256,128]{1,0:T(8,128)} %get-tuple-element.130.sin_ref, ...), custom_call_target="tpu_custom_call" | custom-call | flops 2293760 | bytes 1835008 | tf_op jit(solution)/shard_map/pallas_call | solution.py:84
  37.9 11.5 %collective-permute-done.7.refs_0_ = bf16[128,2560]{1,0:T(8,128)(2,1)S(1)} collective-permute-done((bf16[128,2560]{1,0:T(8,128)(2,1)}, bf16[128,2560]{1,0:T(8,128)(2,1)S(1)}, u32[]{:S(2)}, u32[]{:S(2)}) %collective-permute-start.7) | collective-permute-done | bytes 655392 | tf_op jit(solution)/shard_map/ppermute | solution.py:23
  53.4 2.3 %shard_map.103.refs_3_ = bf16[8,128,768]{2,1,0:T(8,128)(2,1)} custom-call(s32[5]{0:T(128)} %stack.23.where_ref.z_ref, bf16[128,768]{1,0:T(8,128)(2,1)} %block_ref.1), custom_call_target="tpu_custom_call" | custom-call | tf_op jit(solution)/shard_map/pallas_call | solution.py:98
  55.6 5.2 %shard_map.104 = (bf16[2,8,128,896]{3,2,1,0:T(8,128)(2,1)}, bf16[8,128,1024]{2,1,0:T(8,128)(2,1)}, bf16[8,128,1024]{2,1,0:T(8,128)(2,1)}, bf16[8,128,768]{2,1,0:T(8,128)(2,1)}) custom-call(s32[5]{0:T(128)} %stack.23.where_ref.z_ref, bf16[128,2560]{1,0:T(8,128)(2,1)} %get-tuple-element.64.refs_0_, ...), custom_call_target="tpu_custom_call", output_to_operand_aliasing={{3}: (4, {})} | custom-call | flops 939524096 | bytes 5505024 | tf_op jit(solution)/shard_map/pallas_call | solution.py:149
  60.8 5.3 %shard_map.105 = (bf16[2,8,128,896]{3,2,1,0:T(8,128)(2,1)}, bf16[8,128,1024]{2,1,0:T(8,128)(2,1)}, bf16[8,128,1024]{2,1,0:T(8,128)(2,1)}, bf16[8,128,768]{2,1,0:T(8,128)(2,1)}) custom-call(s32[5]{0:T(128)} %stack.23.where_ref.z_ref, bf16[128,2560]{1,0:T(8,128)(2,1)} %copy-done.9, ...), custom_call_target="tpu_custom_call", output_to_operand_aliasing={{0}: (4, {}), {1}: (5, {}), {2}: (6, {}), {3}: (7, {})} | custom-call | flops 939524096 | bytes 5505024 | tf_op jit(solution)/shard_map/pallas_call | solution.py:149
  66.5 3.2 %collective-permute-start.12 = (bf16[128,2560]{1,0:T(8,128)(2,1)S(1)}, bf16[128,2560]{1,0:T(8,128)(2,1)}, u32[]{:S(2)}, u32[]{:S(2)}) collective-permute-start(bf16[128,2560]{1,0:T(8,128)(2,1)S(1)} %collective-permute-done.10.refs_1_), channel_id=1, source_target_pairs={{0,224},{16,240},{32,0},{48,16},{64,32},{80,48},{96,64},{112,80},{... | collective-permute-start | bytes 1966088 | tf_op jit(solution)/shard_map/ppermute | solution.py:23
  69.7 5.4 %shard_map.106 = (bf16[2,8,128,896]{3,2,1,0:T(8,128)(2,1)}, bf16[8,128,1024]{2,1,0:T(8,128)(2,1)}, bf16[8,128,1024]{2,1,0:T(8,128)(2,1)}, bf16[8,128,768]{2,1,0:T(8,128)(2,1)}) custom-call(s32[5]{0:T(128)} %stack.23.where_ref.z_ref, bf16[128,2560]{1,0:T(8,128)(2,1)} %copy-done.8, ...), custom_call_target="tpu_custom_call", output_to_operand_aliasing={{0}: (4, {}), {1}: (5, {}), {2}: (6, {}), {3}: (7, {})} | custom-call | flops 939524096 | bytes 5505024 | tf_op jit(solution)/shard_map/pallas_call | solution.py:149
  75.1 5.7 %convolution_convert_fusion = bf16[2048,768]{1,0:T(8,128)(2,1)S(1)} fusion(bf16[2048,1024]{1,0:T(8,128)(2,1)} %all-gather.3.cloned.1.call-done, bf16[768,1024]{1,0:T(8,128)(2,1)S(1)} %copy-done), kind=kOutput, calls=%fused_computation | convolution fusion | flops 3222798336 | bytes 8912896 | tf_op jit(solution)/shard_map/dot_general | solution.py:230
  85.0 5.3 %shard_map.107 = (bf16[2,8,128,896]{3,2,1,0:T(8,128)(2,1)}, bf16[8,128,1024]{2,1,0:T(8,128)(2,1)}, bf16[8,128,1024]{2,1,0:T(8,128)(2,1)}, bf16[8,128,768]{2,1,0:T(8,128)(2,1)}) custom-call(s32[5]{0:T(128)} %stack.23.where_ref.z_ref, bf16[128,2560]{1,0:T(8,128)(2,1)} %copy-done.5, ...), custom_call_target="tpu_custom_call", output_to_operand_aliasing={{0}: (4, {}), {1}: (5, {}), {2}: (6, {}), {3}: (7, {})} | custom-call | flops 939524096 | bytes 5505024 | tf_op jit(solution)/shard_map/pallas_call | solution.py:149
  92.0 4.2 %shard_map.108 = (bf16[2,8,128,896]{3,2,1,0:T(8,128)(2,1)}, bf16[8,128,1024]{2,1,0:T(8,128)(2,1)}, bf16[8,128,1024]{2,1,0:T(8,128)(2,1)}) custom-call(s32[5]{0:T(128)} %stack.23.where_ref.z_ref, bf16[128,1792]{1,0:T(8,128)(2,1)} %copy-done.13, bf16[1024,896]{1,0:T(8,128)(2,1)} %refs_1_.1, ...), custom_call_target="tpu_custom_call", output_to_operand_aliasing={{0}: (3, {}), {1}: (4, {}), {2}: (5, {})} | custom-call | flops 469762048 | bytes 3276800 | tf_op jit(solution)/shard_map/pallas_call | solution.py:149
  99.4 2.0 %collective-permute-start.22 = (bf16[256,768]{1,0:T(8,128)(2,1)}, bf16[256,768]{1,0:T(8,128)(2,1)}, u32[]{:S(2)}, u32[]{:S(2)}) collective-permute-start(bf16[256,768]{1,0:T(8,128)(2,1)} %add_convert_fusion.4), channel_id=1, source_target_pairs={{0,224},{16,240},{32,0},{48,16},{64,32},{80,48},{96,64},{112,80},{... | collective-permute-start | bytes 1179656 | tf_op jit(solution)/shard_map/ppermute | solution.py:23
  101.4 3.1 %collective-permute-start.28 = (bf16[1,1024,768]{2,1,0:T(8,128)(2,1)S(1)}, bf16[1,1024,768]{2,1,0:T(8,128)(2,1)}, u32[]{:S(2)}, u32[]{:S(2)}) collective-permute-start(bf16[1,1024,768]{2,1,0:T(8,128)(2,1)S(1)} %bitcast.16), channel_id=1, source_target_pairs={{0,16},{16,0},{32,48},{48,32},{64,80},{80,64},{96,112},{112,96},{1... | collective-permute-start | bytes 4718600 | tf_op jit(solution)/shard_map/ppermute | solution.py:27
  104.5 5.4 %shard_map.109 = (bf16[256,1024]{1,0:T(8,128)(2,1)}, bf16[256,1024]{1,0:T(8,128)(2,1)}, bf16[256,1024]{1,0:T(8,128)(2,1)}, bf16[256,1024]{1,0:T(8,128)(2,1)}) custom-call(s32[5]{0:T(128)} %stack.23.where_ref.z_ref, bf16[8,128,1024]{2,1,0:T(8,128)(2,1)} %get-tuple-element.101.kept_ref, bf16[8,128,1024]{2,1,0:T(8,128)(2,1)} %collective-permute-done.15.sent_ref), custom_call_target="tpu_custom_call" | custom-call | flops 1048576 | bytes 6291456 | tf_op jit(solution)/shard_map/pallas_call | solution.py:179
  118.2 2.8 %collective-permute-start.23 = (bf16[256,768]{1,0:T(8,128)(2,1)S(1)}, bf16[256,768]{1,0:T(8,128)(2,1)S(1)}, u32[]{:S(2)}, u32[]{:S(2)}) collective-permute-start(bf16[256,768]{1,0:T(8,128)(2,1)S(1)} %get-tuple-element.125), channel_id=1, source_target_pairs={{0,32},{16,48},{32,64},{48,80},{64,96},{80,112},{96,128},{112,144}... | collective-permute-start | bytes 1179656 | tf_op jit(solution)/shard_map/ppermute | solution.py:23
  123.6 5.9 %collective-permute-done.23 = bf16[256,768]{1,0:T(8,128)(2,1)S(1)} collective-permute-done((bf16[256,768]{1,0:T(8,128)(2,1)S(1)}, bf16[256,768]{1,0:T(8,128)(2,1)S(1)}, u32[]{:S(2)}, u32[]{:S(2)}) %collective-permute-start.23) | collective-permute-done | bytes 393248 | tf_op jit(solution)/shard_map/ppermute | solution.py:23
  130.8 2.2 %add_convert_fusion = (bf16[256,768]{1,0:T(8,128)(2,1)}, bf16[256,768]{1,0:T(8,128)(2,1)}) fusion(bf16[256,768]{1,0:T(8,128)(2,1)S(1)} %collective-permute-done.24, bf16[2048,768]{1,0:T(8,128)(2,1)} %copy-done.4, s32[]{:T(128)S(6)} %select_n.164, bf16[256,768]{1,0:T(8,128)(2,1)S(1)} %collective-permute-done.23, s32[]{:T(128)S(6)} %select_n.154), kind=kLoop, calls=%fused_computation.4 | loop fusion | flops 1572864 | bytes 2359304 | tf_op jit(solution)/shard_map/convert_element_type | solution.py:246
  138.3 9.5 %shard_map.110 = f32[1024,896]{1,0:T(8,128)} custom-call(s32[5]{0:T(128)} %stack.23.where_ref.z_ref, bf16[2,1024,896]{2,1,0:T(8,128)(2,1)} %bitcast.19, bf16[8,2,128,1024]{3,2,1,0:T(8,128)(2,1)} %bitcast.23), custom_call_target="tpu_custom_call" | custom-call | flops 3758096384 | bytes 11534336 | tf_op jit(solution)/shard_map/pallas_call | solution.py:212
  149.3 3.3 %collective-permute-start.27 = (bf16[128,768]{1,0:T(8,128)(2,1)S(1)}, bf16[128,768]{1,0:T(8,128)(2,1)S(1)}, u32[]{:S(2)}, u32[]{:S(2)}) collective-permute-start(bf16[128,768]{1,0:T(8,128)(2,1)S(1)} %dynamic-slice_convert_fusion.1), channel_id=1, source_target_pairs={{0,16},{16,0},{32,48},{48,32},{64,80},{80,64},{96,112},{112,96},{1... | collective-permute-start | bytes 589832 | tf_op jit(solution)/shard_map/ppermute | solution.py:27
  154.8 6.6 %shard_map.111 = f32[768,1024]{1,0:T(8,128)} custom-call(s32[5]{0:T(128)S(1)} %copy-done.2, bf16[1,1024,768]{2,1,0:T(8,128)(2,1)S(1)} %bitcast.17, bf16[1,1024,768]{2,1,0:T(8,128)(2,1)} %collective-permute-done.28.refs_1_, bf16[8,2,128,1024]{3,2,1,0:T(8,128)(2,1)S(1)} %bitcast.18), custom_call_target="tpu_custom_call" | custom-call | flops 3221225472 | bytes 10485760 | tf_op jit(solution)/shard_map/pallas_call | solution.py:212
  (116 shorter events, 49.1 us)
Async XLA Ops:
  7.2 67.9 %all-gather.3.cloned.1.call-start = ((), (), s32[]{:S(2)}) async-start(), calls=%async_computation | async-start | bytes 4456448 | tf_op jit(solution)/shard_map/all_gather | solution.py:266
  7.9 102.0 %all-gather.5.cloned.1.call-start = ((), (), s32[]{:S(2)}) async-start(), calls=%async_computation.1 | async-start | bytes 4456448 | tf_op jit(solution)/shard_map/all_gather | solution.py:267
  11.9 19.1 %collective-permute-start = (bf16[128,896]{1,0:T(8,128)(2,1)}, bf16[128,896]{1,0:T(8,128)(2,1)S(1)}, u32[]{:S(2)}, u32[]{:S(2)}) collective-permute-start(bf16[128,896]{1,0:T(8,128)(2,1)} %own_ref.1), channel_id=1, source_target_pairs={{0,16},{16,0},{32,48},{48,32},{64,80},{80,64},{96,112},{112,96},{1... | collective-permute-start | bytes 688136 | tf_op jit(solution)/shard_map/ppermute | solution.py:27
  14.7 9.0 %collective-permute-start.2 = (s32[2,128]{1,0:T(2,128)S(1)}, s32[2,128]{1,0:T(2,128)S(1)}, u32[]{:S(2)}, u32[]{:S(2)}) collective-permute-start(s32[2,128]{1,0:T(2,128)S(1)} %add_select_fusion), channel_id=1, source_target_pairs={{0,32},{16,48},{32,64},{48,80},{64,96},{80,112},{96,128},{112,144}... | collective-permute-start | bytes 3080 | tf_op jit(solution)/shard_map/ppermute | solution.py:23
  20.4 10.6 %collective-permute-start.5 = (bf16[128,768]{1,0:T(8,128)(2,1)}, bf16[128,768]{1,0:T(8,128)(2,1)S(1)}, u32[]{:S(2)}, u32[]{:S(2)}) collective-permute-start(bf16[128,768]{1,0:T(8,128)(2,1)} %block_ref.1), channel_id=1, source_target_pairs={{0,32},{16,48},{32,64},{48,80},{64,96},{80,112},{96,128},{112,144}... | collective-permute-start | bytes 589832 | tf_op jit(solution)/shard_map/ppermute | solution.py:23
  34.7 14.7 %collective-permute-start.7 = (bf16[128,2560]{1,0:T(8,128)(2,1)}, bf16[128,2560]{1,0:T(8,128)(2,1)S(1)}, u32[]{:S(2)}, u32[]{:S(2)}) collective-permute-start(bf16[128,2560]{1,0:T(8,128)(2,1)} %get-tuple-element.64.refs_0_), channel_id=1, source_target_pairs={{0,32},{16,48},{32,64},{48,80},{64,96},{80,112},{96,128},{112,144}... | collective-permute-start | bytes 1966088 | tf_op jit(solution)/shard_map/ppermute | solution.py:23
  36.6 14.8 %collective-permute-start.8 = (bf16[128,2560]{1,0:T(8,128)(2,1)}, bf16[128,2560]{1,0:T(8,128)(2,1)}, u32[]{:S(2)}, u32[]{:S(2)}) collective-permute-start(bf16[128,2560]{1,0:T(8,128)(2,1)} %get-tuple-element.65.refs_1_), channel_id=1, source_target_pairs={{0,224},{16,240},{32,0},{48,16},{64,32},{80,48},{96,64},{112,80},{... | collective-permute-start | bytes 1966088 | tf_op jit(solution)/shard_map/ppermute | solution.py:23
  51.3 14.8 %collective-permute-start.10 = (bf16[128,2560]{1,0:T(8,128)(2,1)}, bf16[128,2560]{1,0:T(8,128)(2,1)S(1)}, u32[]{:S(2)}, u32[]{:S(2)}) collective-permute-start(bf16[128,2560]{1,0:T(8,128)(2,1)} %collective-permute-done.8.refs_1_), channel_id=1, source_target_pairs={{0,224},{16,240},{32,0},{48,16},{64,32},{80,48},{96,64},{112,80},{... | collective-permute-start | bytes 1966088 | tf_op jit(solution)/shard_map/ppermute | solution.py:23
  52.8 13.5 %collective-permute-start.9 = (bf16[128,2560]{1,0:T(8,128)(2,1)S(1)}, bf16[128,2560]{1,0:T(8,128)(2,1)S(1)}, u32[]{:S(2)}, u32[]{:S(2)}) collective-permute-start(bf16[128,2560]{1,0:T(8,128)(2,1)S(1)} %collective-permute-done.7.refs_0_), channel_id=1, source_target_pairs={{0,32},{16,48},{32,64},{48,80},{64,96},{80,112},{96,128},{112,144}... | collective-permute-start | bytes 1966088 | tf_op jit(solution)/shard_map/ppermute | solution.py:23
  66.3 14.4 %collective-permute-start.11 = (bf16[128,2560]{1,0:T(8,128)(2,1)S(1)}, bf16[128,2560]{1,0:T(8,128)(2,1)S(1)}, u32[]{:S(2)}, u32[]{:S(2)}) collective-permute-start(bf16[128,2560]{1,0:T(8,128)(2,1)S(1)} %collective-permute-done.9.refs_0_), channel_id=1, source_target_pairs={{0,32},{16,48},{32,64},{48,80},{64,96},{80,112},{96,128},{112,144}... | collective-permute-start | bytes 1966088 | tf_op jit(solution)/shard_map/ppermute | solution.py:23
  66.5 14.4 %collective-permute-start.12 = (bf16[128,2560]{1,0:T(8,128)(2,1)S(1)}, bf16[128,2560]{1,0:T(8,128)(2,1)}, u32[]{:S(2)}, u32[]{:S(2)}) collective-permute-start(bf16[128,2560]{1,0:T(8,128)(2,1)S(1)} %collective-permute-done.10.refs_1_), channel_id=1, source_target_pairs={{0,224},{16,240},{32,0},{48,16},{64,32},{80,48},{96,64},{112,80},{... | collective-permute-start | bytes 1966088 | tf_op jit(solution)/shard_map/ppermute | solution.py:23
  80.9 10.2 %collective-permute-start.13 = (bf16[128,1792]{1,0:T(8,128)(2,1)S(1)}, bf16[128,1792]{1,0:T(8,128)(2,1)S(1)}, u32[]{:S(2)}, u32[]{:S(2)}) collective-permute-start(bf16[128,1792]{1,0:T(8,128)(2,1)S(1)} %slice.21), channel_id=1, source_target_pairs={{0,32},{16,48},{32,64},{48,80},{64,96},{80,112},{96,128},{112,144}... | collective-permute-start | bytes 1376264 | tf_op jit(solution)/shard_map/ppermute | solution.py:23
  96.2 13.7 %collective-permute-start.21 = (bf16[256,768]{1,0:T(8,128)(2,1)S(1)}, bf16[256,768]{1,0:T(8,128)(2,1)}, u32[]{:S(2)}, u32[]{:S(2)}) collective-permute-start(bf16[256,768]{1,0:T(8,128)(2,1)S(1)} %copy-done.14), channel_id=1, source_target_pairs={{0,32},{16,48},{32,64},{48,80},{64,96},{80,112},{96,128},{112,144}... | collective-permute-start | bytes 1179656 | tf_op jit(solution)/shard_map/ppermute | solution.py:23
  99.4 11.7 %collective-permute-start.22 = (bf16[256,768]{1,0:T(8,128)(2,1)}, bf16[256,768]{1,0:T(8,128)(2,1)}, u32[]{:S(2)}, u32[]{:S(2)}) collective-permute-start(bf16[256,768]{1,0:T(8,128)(2,1)} %add_convert_fusion.4), channel_id=1, source_target_pairs={{0,224},{16,240},{32,0},{48,16},{64,32},{80,48},{96,64},{112,80},{... | collective-permute-start | bytes 1179656 | tf_op jit(solution)/shard_map/ppermute | solution.py:23
  101.4 53.4 %collective-permute-start.28 = (bf16[1,1024,768]{2,1,0:T(8,128)(2,1)S(1)}, bf16[1,1024,768]{2,1,0:T(8,128)(2,1)}, u32[]{:S(2)}, u32[]{:S(2)}) collective-permute-start(bf16[1,1024,768]{2,1,0:T(8,128)(2,1)S(1)} %bitcast.16), channel_id=1, source_target_pairs={{0,16},{16,0},{32,48},{48,32},{64,80},{80,64},{96,112},{112,96},{1... | collective-permute-start | bytes 4718600 | tf_op jit(solution)/shard_map/ppermute | solution.py:27
  112.3 9.3 %collective-permute-start.17 = (bf16[128,1024]{1,0:T(8,128)(2,1)S(1)}, bf16[128,1024]{1,0:T(8,128)(2,1)S(1)}, u32[]{:S(2)}, u32[]{:S(2)}) collective-permute-start(bf16[128,1024]{1,0:T(8,128)(2,1)S(1)} %get-tuple-element.128), channel_id=1, source_target_pairs={{0,12},{1,13},{2,14},{3,15},{4,0},{5,1},{6,2},{7,3},{8,4},{9,5},{1... | collective-permute-start | bytes 786440 | tf_op jit(solution)/shard_map/ppermute | solution.py:32
  114.1 8.6 %collective-permute-start.16 = (bf16[128,1024]{1,0:T(8,128)(2,1)S(1)}, bf16[128,1024]{1,0:T(8,128)(2,1)S(1)}, u32[]{:S(2)}, u32[]{:S(2)}) collective-permute-start(bf16[128,1024]{1,0:T(8,128)(2,1)S(1)} %get-tuple-element.129), channel_id=1, source_target_pairs={{0,4},{1,5},{2,6},{3,7},{4,8},{5,9},{6,10},{7,11},{8,12},{9,13},{1... | collective-permute-start | bytes 786440 | tf_op jit(solution)/shard_map/ppermute | solution.py:32
  118.2 11.4 %collective-permute-start.23 = (bf16[256,768]{1,0:T(8,128)(2,1)S(1)}, bf16[256,768]{1,0:T(8,128)(2,1)S(1)}, u32[]{:S(2)}, u32[]{:S(2)}) collective-permute-start(bf16[256,768]{1,0:T(8,128)(2,1)S(1)} %get-tuple-element.125), channel_id=1, source_target_pairs={{0,32},{16,48},{32,64},{48,80},{64,96},{80,112},{96,128},{112,144}... | collective-permute-start | bytes 1179656 | tf_op jit(solution)/shard_map/ppermute | solution.py:23
  121.0 9.9 %collective-permute-start.24 = (bf16[256,768]{1,0:T(8,128)(2,1)S(1)}, bf16[256,768]{1,0:T(8,128)(2,1)S(1)}, u32[]{:S(2)}, u32[]{:S(2)}) collective-permute-start(bf16[256,768]{1,0:T(8,128)(2,1)S(1)} %get-tuple-element.124), channel_id=1, source_target_pairs={{0,224},{16,240},{32,0},{48,16},{64,32},{80,48},{96,64},{112,80},{... | collective-permute-start | bytes 1179656 | tf_op jit(solution)/shard_map/ppermute | solution.py:23
  133.0 14.8 %collective-permute-start.25 = (bf16[256,768]{1,0:T(8,128)(2,1)}, bf16[256,768]{1,0:T(8,128)(2,1)S(1)}, u32[]{:S(2)}, u32[]{:S(2)}) collective-permute-start(bf16[256,768]{1,0:T(8,128)(2,1)} %get-tuple-element.123), channel_id=1, source_target_pairs={{0,32},{16,48},{32,64},{48,80},{64,96},{80,112},{96,128},{112,144}... | collective-permute-start | bytes 1179656 | tf_op jit(solution)/shard_map/ppermute | solution.py:23
  134.5 13.4 %collective-permute-start.26 = (bf16[256,768]{1,0:T(8,128)(2,1)}, bf16[256,768]{1,0:T(8,128)(2,1)}, u32[]{:S(2)}, u32[]{:S(2)}) collective-permute-start(bf16[256,768]{1,0:T(8,128)(2,1)} %get-tuple-element.122), channel_id=1, source_target_pairs={{0,224},{16,240},{32,0},{48,16},{64,32},{80,48},{96,64},{112,80},{... | collective-permute-start | bytes 1179656 | tf_op jit(solution)/shard_map/ppermute | solution.py:23
  136.3 16.3 %collective-permute-start.18 = (bf16[256,1024]{1,0:T(8,128)(2,1)}, bf16[256,1024]{1,0:T(8,128)(2,1)S(1)}, u32[]{:S(2)}, u32[]{:S(2)}) collective-permute-start(bf16[256,1024]{1,0:T(8,128)(2,1)} %pad_maximum_fusion), channel_id=1, source_target_pairs={{0,4},{1,5},{2,6},{3,7},{4,8},{5,9},{6,10},{7,11},{8,12},{9,13},{1... | collective-permute-start | bytes 1572872 | tf_op jit(solution)/shard_map/ppermute | solution.py:32
  137.8 14.8 %collective-permute-start.19 = (bf16[256,1024]{1,0:T(8,128)(2,1)}, bf16[256,1024]{1,0:T(8,128)(2,1)}, u32[]{:S(2)}, u32[]{:S(2)}) collective-permute-start(bf16[256,1024]{1,0:T(8,128)(2,1)} %pad_maximum_fusion.1), channel_id=1, source_target_pairs={{0,12},{1,13},{2,14},{3,15},{4,0},{5,1},{6,2},{7,3},{8,4},{9,5},{1... | collective-permute-start | bytes 1572872 | tf_op jit(solution)/shard_map/ppermute | solution.py:32
  149.3 12.1 %collective-permute-start.27 = (bf16[128,768]{1,0:T(8,128)(2,1)S(1)}, bf16[128,768]{1,0:T(8,128)(2,1)S(1)}, u32[]{:S(2)}, u32[]{:S(2)}) collective-permute-start(bf16[128,768]{1,0:T(8,128)(2,1)S(1)} %dynamic-slice_convert_fusion.1), channel_id=1, source_target_pairs={{0,16},{16,0},{32,48},{48,32},{64,80},{80,64},{96,112},{112,96},{1... | collective-permute-start | bytes 589832 | tf_op jit(solution)/shard_map/ppermute | solution.py:27
  (26 other events, 200.5 us)
Sparse Core Ops, SparseCore 0:
  9.9 42.7 all-gather.2
  54.5 39.8 all-gather.4
